TPU v7x, 32 devices: a whole 2x2x4 slice. The times are simulated.
32 devices in a mesh: dp: 16 (over z, y, core), mp: 2 (over x).
Axes of the slice: x: 2, y: 2, z: 4, core: 2. Of those that a mesh axis runs over, the one named last changes fastest.
Arguments:
- tokens: bfloat16 [8192, 1536], P(('dp', 'mp')), may hold values from -6 to 6
- seq_lengths: int32 [16, 3], P('dp'), may hold values from 0 to 512, as said below
- norm_attn: bfloat16 [1536], replicated, may hold values from 0.5 to 1.5
- w_query: bfloat16 [1536, 1536], P('dp', 'mp'), may hold values from -0.15625 to 0.15625
- key_weight: bfloat16 [1536, 768], P('dp', 'mp'), may hold values from -0.15625 to 0.15625
- value_weight: bfloat16 [1536, 768], P('dp', 'mp'), may hold values from -0.15625 to 0.15625
- w_out: bfloat16 [1536, 1536], P('mp', 'dp'), may hold values from -2.5 to 2.5
- norm_mlp: bfloat16 [1536], replicated, may hold values from 0.5 to 1.5
- w_gate: bfloat16 [1536, 4096], P('dp', 'mp'), may hold values from -0.15625 to 0.15625
- w_up: bfloat16 [1536, 4096], P('dp', 'mp'), may hold values from -0.15625 to 0.15625
- w_down: bfloat16 [4096, 1536], P('mp', 'dp'), may hold values from -0.09375 to 0.09375
- cotangent: bfloat16 [8192, 1536], P(('dp', 'mp')), may hold values from -6 to 6
Outputs:
- block_out: bfloat16 [8192, 1536], P(('dp', 'mp'))
- grad_tokens: bfloat16 [8192, 1536], P(('dp', 'mp'))
- grad_norm_attn: float32 [1536], replicated
- grad_w_query: float32 [1536, 1536], P('dp', 'mp')
- grad_w_key: float32 [1536, 768], P('dp', 'mp')
- grad_w_value: float32 [1536, 768], P('dp', 'mp')
- grad_w_out: float32 [1536, 1536], P('mp', 'dp')
- grad_norm_mlp: float32 [1536], replicated
- grad_w_gate: float32 [1536, 4096], P('dp', 'mp')
- grad_w_up: float32 [1536, 4096], P('dp', 'mp')
- grad_w_down: float32 [4096, 1536], P('mp', 'dp')
Inputs may be any that keep to these rules, and one draw needn't show every extreme that they name: `seq_lengths`: row g lists three sequences packed in that order at the start of token group g; the rest of the group is padding. A zero length means that sequence is absent. The middle sequence starts in the first 256 rows of the group and ends in its last 256 rows; some group is one sequence of 512 tokens.
All inputs are finite; a program needn't handle non-finite values.
Results may differ from a plain program's by a relative error of at most 0.02.
Values may be sent and summed in bfloat16 or wider, within the bound.
A program may use at most 192 MiB of HBM per device.

v0:
```python
import jax
import jax.numpy as jnp
from jax import lax
from jax.sharding import PartitionSpec as P

MODEL_WIDTH = 1536
QUERY_HEADS = 16
KEY_VALUE_HEADS = 8
HEAD_SIZE = 96


EPSILON = 1e-05
ROPE_BASE = 100000.0
MASKED = -1e30


def layout(lengths, rows_total):
    places = jnp.arange(rows_total, dtype=jnp.int32)
    first_end = lengths[0]
    middle_end = lengths[0] + lengths[1]
    last_end = middle_end + lengths[2]
    segment = jnp.where(
        places < first_end,
        0,
        jnp.where(places < middle_end, 1, jnp.where(places < last_end, 2, -1)),
    ).astype(jnp.int32)
    offset = jnp.where(places < first_end, 0, jnp.where(places < middle_end, first_end, middle_end))
    position = jnp.where(segment >= 0, places - offset, 0)
    return (segment, position)


def rotation(position):
    half_dim = HEAD_SIZE // 2
    inverse = ROPE_BASE ** (-jnp.arange(half_dim, dtype=jnp.float32) * 2.0 / HEAD_SIZE)
    angles = position.astype(jnp.float32)[:, None] * inverse[None, :]
    return (jnp.cos(angles)[:, None, :], jnp.sin(angles)[:, None, :])


def apply_rotary(tensor, cosine_table, sine_lookup_table):
    half_dim = tensor.shape[-1] // 2
    lead_half = tensor[..., :half_dim]
    tail_half = tensor[..., half_dim:]
    return jnp.concatenate(
        [
            lead_half * cosine_table - tail_half * sine_lookup_table,
            tail_half * cosine_table + lead_half * sine_lookup_table,
        ],
        axis=-1,
    )


def invert_rotary(gradient, cosine_table, sine_lookup_table):
    half_dim = gradient.shape[-1] // 2
    lead_half = gradient[..., :half_dim]
    tail_half = gradient[..., half_dim:]
    return jnp.concatenate(
        [
            lead_half * cosine_table + tail_half * sine_lookup_table,
            tail_half * cosine_table - lead_half * sine_lookup_table,
        ],
        axis=-1,
    )


def rms_norm(inputs, gain_vec):
    factor = lax.rsqrt(jnp.mean(inputs * inputs, axis=-1, keepdims=True) + EPSILON)
    return inputs * factor * gain_vec


def rms_back(inputs, gain_vec, gradient):
    factor = lax.rsqrt(jnp.mean(inputs * inputs, axis=-1, keepdims=True) + EPSILON)
    normed = inputs * factor
    gain_grad = jnp.sum(gradient * normed, axis=0)
    scaled = gradient * gain_vec
    return (
        factor * (scaled - normed * jnp.mean(scaled * normed, axis=-1, keepdims=True)),
        gain_grad,
    )


def outer_sum(left_op, right_op):
    return lax.dot_general(
        left_op, right_op, (((0,), (0,)), ((), ())), preferred_element_type=jnp.float32
    )


def times_t(left_op, right_op):
    return lax.dot_general(
        left_op, right_op, (((1,), (1,)), ((), ())), preferred_element_type=jnp.float32
    )


def attention_parts(allowed, factor):

    def head_scores(query_h, key_h):
        raw_scores = (
            jnp.einsum("qgd,kd->gqk", query_h, key_h, preferred_element_type=jnp.float32) * factor
        )
        return jnp.where(allowed[None], raw_scores, MASKED)

    def head_forward(operands):
        query_h, key_h, value_h = operands
        scores = head_scores(query_h, key_h)
        row_max = jnp.max(scores, axis=-1, keepdims=True)
        exp_scores = jnp.exp(scores - row_max)
        row_sum = jnp.sum(exp_scores, axis=-1, keepdims=True)
        attn_probs = (exp_scores / row_sum).astype(jnp.bfloat16)
        mixed_out = jnp.einsum(
            "gqk,kd->qgd", attn_probs, value_h, preferred_element_type=jnp.float32
        )
        return (mixed_out, row_max, row_sum)

    def head_backward(operands):
        query_h, key_h, value_h, grad_h, row_max, row_sum = operands
        scores = head_scores(query_h, key_h)
        attn_probs = jnp.exp(scores - row_max) / row_sum
        dprob = jnp.einsum("qgd,kd->gqk", grad_h, value_h, preferred_element_type=jnp.float32)
        inner = jnp.sum(attn_probs * dprob, axis=-1, keepdims=True)
        dscore = (attn_probs * (dprob - inner)).astype(jnp.bfloat16)
        dquery = (
            jnp.einsum("gqk,kd->qgd", dscore, key_h, preferred_element_type=jnp.float32) * factor
        )
        dkey = (
            jnp.einsum("gqk,qgd->kd", dscore, query_h, preferred_element_type=jnp.float32) * factor
        )
        dvalue = jnp.einsum(
            "gqk,qgd->kd",
            attn_probs.astype(jnp.bfloat16),
            grad_h,
            preferred_element_type=jnp.float32,
        )
        return (dquery, dkey, dvalue)

    return (head_forward, head_backward)


def feed_forward(rows_in, gate_w, up_w, down_w):
    gate_act = jnp.dot(rows_in, gate_w, preferred_element_type=jnp.float32)
    up_act = jnp.dot(rows_in, up_w, preferred_element_type=jnp.float32)
    sigmoid_g = jax.nn.sigmoid(gate_act)
    swish = gate_act * sigmoid_g
    hidden = (swish * up_act).astype(jnp.bfloat16)
    branch_terms = jnp.dot(hidden, down_w, preferred_element_type=jnp.float32)
    return (hidden, branch_terms, (gate_act, up_act, sigmoid_g, swish))


def feed_back(rows_in, hidden, saved, gate_w, up_w, down_w, grad_rows):
    gate_act, up_act, sigmoid_g, swish = saved
    grad_down = outer_sum(hidden, grad_rows)
    grad_hidden = times_t(grad_rows, down_w)
    grad_gate = (grad_hidden * up_act * sigmoid_g * (1.0 + gate_act * (1.0 - sigmoid_g))).astype(
        jnp.bfloat16
    )
    grad_up = (grad_hidden * swish).astype(jnp.bfloat16)
    grad_gate_w = outer_sum(rows_in, grad_gate)
    grad_up_w = outer_sum(rows_in, grad_up)
    grad_rows_in = times_t(grad_gate, gate_w) + times_t(grad_up, up_w)
    return (grad_gate_w, grad_up_w, grad_down, grad_rows_in)


def shards(
    tokens,
    seq_lengths,
    norm_attn,
    w_query,
    key_weight,
    value_weight,
    w_out,
    norm_mlp,
    w_gate,
    w_up,
    w_down,
    cotangent,
):
    parts_mp = lax.axis_size("mp")
    local_row_slice = tokens.shape[0]
    grouped_rows = local_row_slice * parts_mp
    group_member_count = QUERY_HEADS // KEY_VALUE_HEADS
    factor = HEAD_SIZE ** (-0.5)
    query_part, key_part, value_part, out_part, gate_w, up_w, down_w = (
        lax.all_gather(w_query, "dp", axis=0, tiled=True),
        lax.all_gather(key_weight, "dp", axis=0, tiled=True),
        lax.all_gather(value_weight, "dp", axis=0, tiled=True),
        lax.all_gather(w_out, "dp", axis=1, tiled=True),
        lax.all_gather(w_gate, "dp", axis=0, tiled=True),
        lax.all_gather(w_up, "dp", axis=0, tiled=True),
        lax.all_gather(w_down, "dp", axis=1, tiled=True),
    )
    segment, position = layout(seq_lengths[0], grouped_rows)
    first_row = lax.axis_index("mp") * local_row_slice
    local_rows = first_row + jnp.arange(local_row_slice, dtype=jnp.int32)
    group_rows = jnp.arange(grouped_rows, dtype=jnp.int32)
    local_seg = lax.dynamic_slice_in_dim(segment, first_row, local_row_slice)
    local_pos = lax.dynamic_slice_in_dim(position, first_row, local_row_slice)
    cosine_local_rows, sine_local_rows = rotation(local_pos)
    inputs = tokens.astype(jnp.float32)
    gain_first = norm_attn.astype(jnp.float32)
    gain_second = norm_mlp.astype(jnp.float32)
    first_normed_rows = rms_norm(inputs, gain_first).astype(jnp.bfloat16)
    query_w, key_matrix, value_matrix, out_w = (
        lax.all_gather(query_part, "mp", axis=1, tiled=True),
        lax.all_gather(key_part, "mp", axis=1, tiled=True),
        lax.all_gather(value_part, "mp", axis=1, tiled=True),
        lax.all_gather(out_part, "mp", axis=0, tiled=True),
    )
    kv_width = key_matrix.shape[1]
    allowed = (
        (local_rows[:, None] >= group_rows[None, :])
        & (local_seg[:, None] == segment[None, :])
        & ((segment[None, :] >= 0) | (local_rows[:, None] == group_rows[None, :]))
    )
    head_forward, head_backward = attention_parts(allowed, factor)
    query_unrotated = jnp.dot(
        first_normed_rows, query_w, preferred_element_type=jnp.float32
    ).reshape(local_row_slice, QUERY_HEADS, HEAD_SIZE)
    key_unrotated = jnp.dot(
        first_normed_rows, key_matrix, preferred_element_type=jnp.float32
    ).reshape(local_row_slice, KEY_VALUE_HEADS, HEAD_SIZE)
    value_activation = jnp.dot(
        first_normed_rows, value_matrix, preferred_element_type=jnp.float32
    ).astype(jnp.bfloat16)
    query_rotated = apply_rotary(query_unrotated, cosine_local_rows, sine_local_rows).astype(
        jnp.bfloat16
    )
    key_rot = (
        apply_rotary(key_unrotated, cosine_local_rows, sine_local_rows)
        .astype(jnp.bfloat16)
        .reshape(local_row_slice, kv_width)
    )
    key_rows_full, value_rows_full, grad_rows = (
        lax.all_gather(key_rot, "mp", axis=0, tiled=True),
        lax.all_gather(value_activation, "mp", axis=0, tiled=True),
        lax.all_gather(cotangent, "mp", axis=0, tiled=True),
    )
    query_head_split = query_rotated.reshape(
        local_row_slice, KEY_VALUE_HEADS, group_member_count, HEAD_SIZE
    ).transpose(1, 0, 2, 3)
    key_head_split = key_rows_full.reshape(grouped_rows, KEY_VALUE_HEADS, HEAD_SIZE).transpose(
        1, 0, 2
    )
    value_head_split = value_rows_full.reshape(grouped_rows, KEY_VALUE_HEADS, HEAD_SIZE).transpose(
        1, 0, 2
    )
    mixed_heads, row_maxes, row_sums = lax.map(
        head_forward, (query_head_split, key_head_split, value_head_split)
    )
    attended = (
        mixed_heads.transpose(1, 0, 2, 3).reshape(local_row_slice, MODEL_WIDTH).astype(jnp.bfloat16)
    )
    residual = inputs + jnp.dot(attended, out_w, preferred_element_type=jnp.float32)
    normed_two = rms_norm(residual, gain_second).astype(jnp.bfloat16)
    rows_all = lax.all_gather(normed_two, "mp", axis=0, tiled=True)
    hidden, branch_terms, saved = feed_forward(rows_all, gate_w, up_w, down_w)
    branch = lax.psum_scatter(
        branch_terms.astype(jnp.bfloat16), "mp", scatter_dimension=0, tiled=True
    ).astype(jnp.float32)
    block_out = (residual + branch).astype(jnp.bfloat16)
    grad_gate_w, grad_up_w, grad_down, grad_terms = feed_back(
        rows_all, hidden, saved, gate_w, up_w, down_w, grad_rows
    )
    grad_normed_two = lax.psum_scatter(
        grad_terms.astype(jnp.bfloat16), "mp", scatter_dimension=0, tiled=True
    ).astype(jnp.float32)
    grad_from_norm, grad_gain_two = rms_back(residual, gain_second, grad_normed_two)
    grad_residual = cotangent.astype(jnp.float32) + grad_from_norm
    grad_branch = grad_residual.astype(jnp.bfloat16)
    grad_out_full = outer_sum(attended, grad_branch)
    attended_gradient = times_t(grad_branch, out_w).astype(jnp.bfloat16)
    heads_gradient = attended_gradient.reshape(
        local_row_slice, KEY_VALUE_HEADS, group_member_count, HEAD_SIZE
    ).transpose(1, 0, 2, 3)
    dquery_heads, dkey_heads, dvalue_heads = lax.map(
        head_backward,
        (query_head_split, key_head_split, value_head_split, heads_gradient, row_maxes, row_sums),
    )
    dkey_group = dkey_heads.transpose(1, 0, 2).reshape(grouped_rows, kv_width)
    dvalue_group = dvalue_heads.transpose(1, 0, 2).reshape(grouped_rows, kv_width)
    key_gradient_local, dvalue_local = (
        lax.psum_scatter(
            dkey_group.astype(jnp.bfloat16), "mp", scatter_dimension=0, tiled=True
        ).astype(jnp.float32),
        lax.psum_scatter(
            dvalue_group.astype(jnp.bfloat16), "mp", scatter_dimension=0, tiled=True
        ).astype(jnp.float32),
    )
    dquery_rows = dquery_heads.transpose(1, 0, 2, 3).reshape(
        local_row_slice, QUERY_HEADS, HEAD_SIZE
    )
    grad_queries = (
        invert_rotary(dquery_rows, cosine_local_rows, sine_local_rows)
        .reshape(local_row_slice, MODEL_WIDTH)
        .astype(jnp.bfloat16)
    )
    grad_keys = (
        invert_rotary(
            key_gradient_local.reshape(local_row_slice, KEY_VALUE_HEADS, HEAD_SIZE),
            cosine_local_rows,
            sine_local_rows,
        )
        .reshape(local_row_slice, kv_width)
        .astype(jnp.bfloat16)
    )
    grad_values = dvalue_local.astype(jnp.bfloat16)
    grad_query_full = outer_sum(first_normed_rows, grad_queries)
    grad_key_full = outer_sum(first_normed_rows, grad_keys)
    grad_value_full = outer_sum(first_normed_rows, grad_values)
    grad_normed_one = (
        times_t(grad_queries, query_w)
        + times_t(grad_keys, key_matrix)
        + times_t(grad_values, value_matrix)
    )
    grad_query_w, grad_key_w, grad_value_w, grad_out_w = (
        lax.psum_scatter(
            grad_query_full.astype(jnp.bfloat16), "mp", scatter_dimension=1, tiled=True
        ).astype(jnp.float32),
        lax.psum_scatter(
            grad_key_full.astype(jnp.bfloat16), "mp", scatter_dimension=1, tiled=True
        ).astype(jnp.float32),
        lax.psum_scatter(
            grad_value_full.astype(jnp.bfloat16), "mp", scatter_dimension=1, tiled=True
        ).astype(jnp.float32),
        lax.psum_scatter(
            grad_out_full.astype(jnp.bfloat16), "mp", scatter_dimension=0, tiled=True
        ).astype(jnp.float32),
    )
    grad_from_first, grad_gain_one = rms_back(inputs, gain_first, grad_normed_one)
    grad_input = (grad_residual + grad_from_first).astype(jnp.bfloat16)
    gain_one_sum, gain_two_sum = lax.psum((grad_gain_one, grad_gain_two), ("dp", "mp"))
    sums = (
        lax.psum_scatter(
            grad_query_w.astype(jnp.bfloat16), "dp", scatter_dimension=0, tiled=True
        ).astype(jnp.float32),
        lax.psum_scatter(
            grad_key_w.astype(jnp.bfloat16), "dp", scatter_dimension=0, tiled=True
        ).astype(jnp.float32),
        lax.psum_scatter(
            grad_value_w.astype(jnp.bfloat16), "dp", scatter_dimension=0, tiled=True
        ).astype(jnp.float32),
        lax.psum_scatter(
            grad_out_w.astype(jnp.bfloat16), "dp", scatter_dimension=1, tiled=True
        ).astype(jnp.float32),
        lax.psum_scatter(
            grad_gate_w.astype(jnp.bfloat16), "dp", scatter_dimension=0, tiled=True
        ).astype(jnp.float32),
        lax.psum_scatter(
            grad_up_w.astype(jnp.bfloat16), "dp", scatter_dimension=0, tiled=True
        ).astype(jnp.float32),
        lax.psum_scatter(
            grad_down.astype(jnp.bfloat16), "dp", scatter_dimension=1, tiled=True
        ).astype(jnp.float32),
    )
    return (
        block_out,
        grad_input,
        gain_one_sum,
        sums[0],
        sums[1],
        sums[2],
        sums[3],
        gain_two_sum,
        sums[4],
        sums[5],
        sums[6],
    )


def solution(mesh):
    in_specs = (
        P(("dp", "mp"), None),
        P("dp", None),
        P(),
        P("dp", "mp"),
        P("dp", "mp"),
        P("dp", "mp"),
        P("mp", "dp"),
        P(),
        P("dp", "mp"),
        P("dp", "mp"),
        P("mp", "dp"),
        P(("dp", "mp"), None),
    )
    out_specs = (
        P(("dp", "mp"), None),
        P(("dp", "mp"), None),
        P(),
        P("dp", "mp"),
        P("dp", "mp"),
        P("dp", "mp"),
        P("mp", "dp"),
        P(),
        P("dp", "mp"),
        P("dp", "mp"),
        P("mp", "dp"),
    )
    return jax.shard_map(shards, mesh=mesh, in_specs=in_specs, out_specs=out_specs, check_vma=False)
```

profile of v0, /device:TPU:10, one launch (start us, length us, event | category | flops | bytes accessed | tf_op | source)
XLA Modules:
  0.0 1541.5 jit_solution(9980105388218111087)
XLA Ops:
  10.0 39.0 %all-gather.18.cloned.1.call-done = bf16[1536,384]{1,0:T(8,128)(2,1)} async-done(((bf16[96,384]{1,0:T(8,128)(2,1)}), bf16[1536,384]{1,0:T(8,128)(2,1)}) %all-gather.18.cloned.1.call-update) | async-done | bytes 1179664 | tf_op jit(solution)/shard_map/all_gather | solution.py:182
  49.0 39.5 %all-gather.14.cloned.1.call-done = bf16[1536,384]{1,0:T(8,128)(2,1)} async-done(((bf16[96,384]{1,0:T(8,128)(2,1)}), bf16[1536,384]{1,0:T(8,128)(2,1)}) %all-gather.14.cloned.1.call-update) | async-done | bytes 1179664 | tf_op jit(solution)/shard_map/all_gather | solution.py:183
  88.6 43.7 %all-gather.22.cloned.1.call-done = bf16[1536,768]{1,0:T(8,128)(2,1)} async-done(((bf16[96,768]{1,0:T(8,128)(2,1)}), bf16[1536,768]{1,0:T(8,128)(2,1)}) %all-gather.22.cloned.1.call-update) | async-done | bytes 2359312 | tf_op jit(solution)/shard_map/all_gather | solution.py:181
  137.8 37.7 %all-gather.26.cloned.1.call-done = bf16[768,1536]{0,1:T(8,128)(2,1)} async-done(((bf16[768,96]{0,1:T(8,128)(2,1)}), bf16[768,1536]{0,1:T(8,128)(2,1)}) %all-gather.26.cloned.1.call-update) | async-done | bytes 2359312 | tf_op jit(solution)/shard_map/all_gather | solution.py:184
  175.6 35.8 %all-gather.20.cloned.1.call-done = bf16[1536,768]{1,0:T(8,128)(2,1)} async-done(((bf16[1536,384]{1,0:T(8,128)(2,1)}), bf16[1536,768]{1,0:T(8,128)(2,1)}) %all-gather.20.cloned.1.call-update) | async-done | bytes 2359312 | tf_op jit(solution)/shard_map/all_gather | solution.py:202
  214.4 15.0 all_gather.50
  229.4 22.0 %all-gather.16.cloned.1.call-done = bf16[1536,768]{1,0:T(8,128)(2,1)} async-done(((bf16[1536,384]{1,0:T(8,128)(2,1)}), bf16[1536,768]{1,0:T(8,128)(2,1)}) %all-gather.16.cloned.1.call-update) | async-done | bytes 2359312 | tf_op jit(solution)/shard_map/all_gather | solution.py:203
  253.9 13.3 all_gather.47
  268.3 48.1 %all-gather.24.cloned.1.call-done = bf16[1536,1536]{1,0:T(8,128)(2,1)} async-done(((bf16[1536,768]{1,0:T(8,128)(2,1)}), bf16[1536,1536]{1,0:T(8,128)(2,1)}) %all-gather.24.cloned.1.call-update) | async-done | bytes 4718608 | tf_op jit(solution)/shard_map/all_gather | solution.py:201
  316.5 4.3 fusion.82
  321.1 16.3 %while.32 = (s32[]{:T(128)}, bf16[8,256,2,96]{1,3,2,0:T(8,128)(2,1)S(1)}, f32[8,2,256,1]{2,1,3,0:T(2,128)S(1)}, f32[8,2,256,1]{2,1,3,0:T(2,128)S(1)}, bf16[8,512...) while((s32[]{:T(128)}, ...), condition=%wide.region_4.5_spmd.clone.clone, body=%wide.region_1.4_spmd.clone.sunk.clone | while | flops 103545856 | bytes 3924593 | solution.py:244
  337.5 43.3 %all-gather.28.cloned.1.call-done = bf16[1536,1536]{0,1:T(8,128)(2,1)} async-done(((bf16[768,1536]{0,1:T(8,128)(2,1)}), bf16[1536,1536]{0,1:T(8,128)(2,1)}) %all-gather.28.cloned.1.call-update) | async-done | bytes 4718608 | tf_op jit(solution)/shard_map/all_gather | solution.py:204
  380.7 3.9 multiply_reduce_fusion.1
  388.9 24.2 %all-gather.30.cloned.1.call-done = bf16[512,1536]{1,0:T(8,128)(2,1)} async-done(((bf16[256,1536]{1,0:T(8,128)(2,1)}), bf16[512,1536]{1,0:T(8,128)(2,1)}) %all-gather.30.cloned.1.call-update) | async-done | bytes 1572880 | tf_op jit(solution)/shard_map/all_gather | solution.py:252
  413.1 64.9 %all-gather.32.cloned.1.call-done = bf16[1536,2048]{1,0:T(8,128)(2,1)} async-done(((bf16[96,2048]{1,0:T(8,128)(2,1)}), bf16[1536,2048]{1,0:T(8,128)(2,1)}) %all-gather.32.cloned.1.call-update) | async-done | bytes 6291472 | tf_op jit(solution)/shard_map/all_gather | solution.py:185
  478.0 8.6 fusion.89
  486.6 54.1 %all-gather.34.cloned.1.call-done = bf16[1536,2048]{1,0:T(8,128)(2,1)} async-done(((bf16[96,2048]{1,0:T(8,128)(2,1)}), bf16[1536,2048]{1,0:T(8,128)(2,1)}) %all-gather.34.cloned.1.call-update) | async-done | bytes 6291472 | tf_op jit(solution)/shard_map/all_gather | solution.py:186
  540.8 8.6 fusion.90
  549.4 17.7 %all-gather.38.cloned.1.call-done = bf16[512,1536]{1,0:T(8,128)(2,1)} async-done(((bf16[256,1536]{1,0:T(8,128)(2,1)}), bf16[512,1536]{1,0:T(8,128)(2,1)}) %all-gather.38.cloned.1.call-update) | async-done | bytes 1572880 | tf_op jit(solution)/shard_map/all_gather | solution.py:233
  567.1 65.1 %all-gather.36.cloned.1.call-done = bf16[2048,1536]{0,1:T(8,128)(2,1)} async-done(((bf16[2048,96]{0,1:T(8,128)(2,1)}), bf16[2048,1536]{0,1:T(8,128)(2,1)}) %all-gather.36.cloned.1.call-update) | async-done | bytes 6291472 | tf_op jit(solution)/shard_map/all_gather | solution.py:187
  632.2 11.7 multiply_convert_fusion.1
  643.9 7.2 fusion.91
  651.1 4.6 fusion.58
  656.0 8.0 convolution_convert_fusion.7
  664.1 15.6 %reduce-scatter.24.cloned.1.call-done = bf16[256,1536]{1,0:T(8,128)(2,1)} async-done(((bf16[512,1536]{1,0:T(8,128)(2,1)}), bf16[256,1536]{1,0:T(8,128)(2,1)}) %reduce-scatter.24.cloned.1.call-update) | async-done | bytes 786448 | tf_op jit(solution)/shard_map/reduce_scatter | solution.py:261
  682.0 26.0 %reduce-scatter.22.cloned.1.call-done = bf16[256,1536]{1,0:T(8,128)(2,1)} async-done(((bf16[512,1536]{1,0:T(8,128)(2,1)}), bf16[256,1536]{1,0:T(8,128)(2,1)}) %reduce-scatter.22.cloned.1.call-update) | async-done | bytes 786448 | tf_op jit(solution)/shard_map/reduce_scatter | solution.py:254
  712.0 4.6 convolution_convert_fusion.8
  718.3 55.9 %while.33 = (s32[]{:T(128)}, f32[8,256,2,96]{1,3,2,0:T(8,128)S(1)}, bf16[8,512,96]{1,2,0:T(8,128)(2,1)}, bf16[8,512,96]{1,2,0:T(8,128)(2,1)}, bf16[8,512,96]{1,2...) while((s32[]{:T(128)}, f32[8,256,2,96]{1,3,2,0:T(8,128)S(1)}, ...), condition=%wide.region_11.12_spmd.clone.clone, body=%wide.region_9.11_spmd.clone.sunk.clone | while | flops 255163904 | bytes 9430665 | solution.py:272
  774.8 16.9 %reduce-scatter.26.cloned.1.call-done = bf16[256,768]{0,1:T(8,128)(2,1)} async-done(((bf16[512,768]{0,1:T(8,128)(2,1)}), bf16[256,768]{0,1:T(8,128)(2,1)}) %reduce-scatter.26.cloned.1.call-update) | async-done | bytes 393232 | tf_op jit(solution)/shard_map/reduce_scatter | solution.py:279
  796.5 15.5 %reduce-scatter.28.cloned.1.call-done = bf16[256,768]{0,1:T(8,128)(2,1)} async-done(((bf16[512,768]{0,1:T(8,128)(2,1)}), bf16[256,768]{0,1:T(8,128)(2,1)}) %reduce-scatter.28.cloned.1.call-update) | async-done | bytes 393232 | tf_op jit(solution)/shard_map/reduce_scatter | solution.py:282
  817.9 3.6 convolution_convert_fusion.3
  824.0 3.7 convolution_convert_fusion.4
  827.8 8.2 convolution_convert_fusion.2
  836.0 8.2 convolution_convert_fusion.1
  844.3 8.1 convolution_convert_fusion
  855.2 30.7 %reduce-scatter.48.cloned.1.call-done = bf16[384,1536]{1,0:T(8,128)(2,1)} async-done(((bf16[768,1536]{1,0:T(8,128)(2,1)}), bf16[384,1536]{1,0:T(8,128)(2,1)}) %reduce-scatter.48.cloned.1.call-update) | async-done | bytes 1179664
  888.4 59.7 %reduce-scatter.38.cloned.1.call-done = bf16[768,1536]{1,0:T(8,128)(2,1)} async-done(((bf16[1536,1536]{1,0:T(8,128)(2,1)}), bf16[768,1536]{1,0:T(8,128)(2,1)}) %reduce-scatter.38.cloned.1.call-update) | async-done | bytes 2359312 | tf_op jit(solution)/shard_map/reduce_scatter | solution.py:322
  948.1 4.3 copy.64
  952.4 58.1 %reduce-scatter.30.cloned.1.call-done = bf16[1536,768]{1,0:T(8,128)(2,1)} async-done(((bf16[1536,1536]{1,0:T(8,128)(2,1)}), bf16[1536,768]{1,0:T(8,128)(2,1)}) %reduce-scatter.30.cloned.1.call-update) | async-done | bytes 2359312 | tf_op jit(solution)/shard_map/reduce_scatter | solution.py:313
  1010.6 3.9 fusion.92
  1018.5 41.5 %all-reduce = (f32[1536]{0:T(1024)}, f32[1536]{0:T(1024)}) all-reduce(f32[1536]{0:T(1024)S(1)} %get-tuple-element.217, f32[1536]{0:T(1024)S(1)} %copy-done.17), channel_id=1, replica_groups=mesh['dp'=16,'mp'=2] {'dp','mp'}, use_global_device_ids=true, to_apply=%region_16.17 | all-reduce | flops 3072 | bytes 24576 | tf_op jit(solution)/shard_map/psum | solution.py:328
  1062.8 38.1 %reduce-scatter.40.cloned.1.call-done = bf16[96,2048]{1,0:T(8,128)(2,1)} async-done(((bf16[1536,2048]{1,0:T(8,128)(2,1)}), bf16[96,2048]{1,0:T(8,128)(2,1)}) %reduce-scatter.40.cloned.1.call-update) | async-done | bytes 393232 | tf_op jit(solution)/shard_map/reduce_scatter | solution.py:342
  1102.8 87.0 %reduce-scatter.42.cloned.1.call-done = bf16[96,2048]{1,0:T(8,128)(2,1)} async-done(((bf16[1536,2048]{1,0:T(8,128)(2,1)}), bf16[96,2048]{1,0:T(8,128)(2,1)}) %reduce-scatter.42.cloned.1.call-update) | async-done | bytes 393232 | tf_op jit(solution)/shard_map/reduce_scatter | solution.py:345
  1191.8 86.2 %reduce-scatter.44.cloned.1.call-done = bf16[2048,96]{0,1:T(8,128)(2,1)} async-done(((bf16[2048,1536]{0,1:T(8,128)(2,1)}), bf16[2048,96]{0,1:T(8,128)(2,1)}) %reduce-scatter.44.cloned.1.call-update) | async-done | bytes 393232 | tf_op jit(solution)/shard_map/reduce_scatter | solution.py:348
  1279.9 59.8 %reduce-scatter.34.cloned.1.call-done = bf16[96,384]{1,0:T(8,128)(2,1)} async-done(((bf16[1536,384]{1,0:T(8,128)(2,1)}), bf16[96,384]{1,0:T(8,128)(2,1)}) %reduce-scatter.34.cloned.1.call-update) | async-done | bytes 73744 | tf_op jit(solution)/shard_map/reduce_scatter | solution.py:333
  1341.3 59.4 %reduce-scatter.36.cloned.1.call-done = bf16[96,384]{1,0:T(8,128)(2,1)} async-done(((bf16[1536,384]{1,0:T(8,128)(2,1)}), bf16[96,384]{1,0:T(8,128)(2,1)}) %reduce-scatter.36.cloned.1.call-update) | async-done | bytes 73744 | tf_op jit(solution)/shard_map/reduce_scatter | solution.py:336
  1402.3 64.5 %reduce-scatter.50.cloned.1.call-done = bf16[96,768]{1,0:T(8,128)(2,1)} async-done(((bf16[1536,768]{1,0:T(8,128)(2,1)}), bf16[96,768]{1,0:T(8,128)(2,1)}) %reduce-scatter.50.cloned.1.call-update) | async-done | bytes 147472
  1468.7 63.8 %reduce-scatter.32.cloned.1.call-done = bf16[96,768]{1,0:T(8,128)(2,1)} async-done(((bf16[1536,768]{1,0:T(8,128)(2,1)}), bf16[96,768]{1,0:T(8,128)(2,1)}) %reduce-scatter.32.cloned.1.call-update) | async-done | bytes 147472 | tf_op jit(solution)/shard_map/reduce_scatter | solution.py:330
  (264 shorter events, 135.6 us)
Async XLA Ops:
  7.2 41.8 %all-gather.18.cloned.1.call-start = ((), (), s32[]{:S(2)}) async-start(), calls=%async_computation.17 | async-start | bytes 1253376 | tf_op jit(solution)/shard_map/all_gather | solution.py:182
  7.9 80.7 %all-gather.14.cloned.1.call-start = ((), (), s32[]{:S(2)}) async-start(), calls=%async_computation.15 | async-start | bytes 1253376 | tf_op jit(solution)/shard_map/all_gather | solution.py:183
  8.7 123.7 %all-gather.22.cloned.1.call-start = ((), (), s32[]{:S(2)}) async-start(), calls=%async_computation.19 | async-start | bytes 2506752 | tf_op jit(solution)/shard_map/all_gather | solution.py:181
  9.4 166.1 %all-gather.26.cloned.1.call-start = ((), (), s32[]{:S(2)}) async-start(), calls=%async_computation.21 | async-start | bytes 2506752 | tf_op jit(solution)/shard_map/all_gather | solution.py:184
  10.0 201.4 %all-gather.20.cloned.1.call-start = ((), (), s32[]{:S(2)}) async-start(), calls=%async_computation.18 | async-start | bytes 3538944 | tf_op jit(solution)/shard_map/all_gather | solution.py:202
  49.0 202.4 %all-gather.16.cloned.1.call-start = ((), (), s32[]{:S(2)}) async-start(), calls=%async_computation.16 | async-start | bytes 3538944 | tf_op jit(solution)/shard_map/all_gather | solution.py:203
  88.6 43.9 %copy-start.19 = (bf16[1536]{0:T(1024)(128)(2,1)S(1)}, bf16[1536]{0:T(1024)(128)(2,1)}, u32[]{:S(2)}) copy-start(bf16[1536]{0:T(1024)(128)(2,1)} %param.18) | copy-start | bytes 9220
  88.6 43.9 %copy-start.20 = (bf16[1536]{0:T(1024)(128)(2,1)S(1)}, bf16[1536]{0:T(1024)(128)(2,1)}, u32[]{:S(2)}) copy-start(bf16[1536]{0:T(1024)(128)(2,1)} %param.23) | copy-start | bytes 9220
  88.6 43.9 %copy-start.18 = (s32[1,3]{1,0:T(1,128)S(1)}, s32[1,3]{1,0:T(1,128)}, u32[]{:S(2)}) copy-start(s32[1,3]{1,0:T(1,128)} %param.17) | copy-start | bytes 40
  88.6 227.9 %all-gather.24.cloned.1.call-start = ((), (), s32[]{:S(2)}) async-start(), calls=%async_computation.20 | async-start | bytes 7077888 | tf_op jit(solution)/shard_map/all_gather | solution.py:201
  132.3 4.9 copy-start
  132.4 248.4 %all-gather.28.cloned.1.call-start = ((), (), s32[]{:S(2)}) async-start(), calls=%async_computation.22 | async-start | bytes 7077888 | tf_op jit(solution)/shard_map/all_gather | solution.py:204
  137.8 655.0 %copy-start.13 = (f32[256,48]{0,1:T(8,128)}, f32[256,48]{0,1:T(8,128)S(1)}, u32[]{:S(2)}) copy-start(f32[256,48]{0,1:T(8,128)S(1)} %get-tuple-element.292) | copy-start | bytes 147460
  137.8 655.0 %copy-start.15 = (f32[256,48]{0,1:T(8,128)}, f32[256,48]{0,1:T(8,128)S(1)}, u32[]{:S(2)}) copy-start(f32[256,48]{0,1:T(8,128)S(1)} %get-tuple-element.293) | copy-start | bytes 147460
  175.5 237.6 %all-gather.30.cloned.1.call-start = ((), (), s32[]{:S(2)}) async-start(), calls=%async_computation.23 | async-start | bytes 2359296 | tf_op jit(solution)/shard_map/all_gather | solution.py:252
  337.4 43.3 %copy-start.8 = (bf16[8,512,96]{1,2,0:T(8,128)(2,1)}, bf16[8,512,96]{1,2,0:T(8,128)(2,1)S(1)}, u32[]{:S(2)}) copy-start(bf16[8,512,96]{1,2,0:T(8,128)(2,1)S(1)} %get-tuple-element.670) | copy-start | bytes 2359300
  337.4 43.3 %copy-start.9 = (bf16[8,256,2,96]{1,3,2,0:T(8,128)(2,1)}, bf16[8,256,2,96]{1,3,2,0:T(8,128)(2,1)S(1)}, u32[]{:S(2)}) copy-start(bf16[8,256,2,96]{1,3,2,0:T(8,128)(2,1)S(1)} %get-tuple-element.672) | copy-start | bytes 2359300
  337.4 47.1 %copy-start.3 = (bf16[8,256,2,96]{1,3,2,0:T(8,128)(2,1)}, bf16[8,256,2,96]{1,3,2,0:T(8,128)(2,1)S(1)}, u32[]{:S(2)}) copy-start(bf16[8,256,2,96]{1,3,2,0:T(8,128)(2,1)S(1)} %get-tuple-element.114) | copy-start | bytes 2359300
  385.7 92.3 %all-gather.32.cloned.1.call-start = ((), (), s32[]{:S(2)}) async-start(), calls=%async_computation.24 | async-start | bytes 6684672 | tf_op jit(solution)/shard_map/all_gather | solution.py:185
  386.3 154.5 %all-gather.34.cloned.1.call-start = ((), (), s32[]{:S(2)}) async-start(), calls=%async_computation.25 | async-start | bytes 6684672 | tf_op jit(solution)/shard_map/all_gather | solution.py:186
  387.0 180.1 %all-gather.38.cloned.1.call-start = ((), (), s32[]{:S(2)}) async-start(), calls=%async_computation.28 | async-start | bytes 2359296 | tf_op jit(solution)/shard_map/all_gather | solution.py:233
  387.6 244.6 %all-gather.36.cloned.1.call-start = ((), (), s32[]{:S(2)}) async-start(), calls=%async_computation.26 | async-start | bytes 6684672 | tf_op jit(solution)/shard_map/all_gather | solution.py:187
  388.4 291.3 %reduce-scatter.24.cloned.1.call-start = ((), (), s32[]{:S(2)}) async-start(), calls=%async_computation.29 | async-start | bytes 2359296 | tf_op jit(solution)/shard_map/reduce_scatter | solution.py:261
  643.9 7.2 copy-start.23
  643.9 7.2 copy-start.22
  643.9 7.2 copy-start.21
  655.8 52.2 %reduce-scatter.22.cloned.1.call-start = ((), (), s32[]{:S(2)}) async-start(), calls=%async_computation.27 | async-start | bytes 2359296 | tf_op jit(solution)/shard_map/reduce_scatter | solution.py:254
  664.0 44.0 %copy-start.5 = (bf16[256,1536]{1,0:T(8,128)(2,1)S(1)}, bf16[256,1536]{1,0:T(8,128)(2,1)}, u32[]{:S(2)}) copy-start(bf16[256,1536]{1,0:T(8,128)(2,1)} %param.27) | copy-start | bytes 2359300
  664.0 127.7 %reduce-scatter.26.cloned.1.call-start = ((), (), s32[]{:S(2)}) async-start(), calls=%async_computation.30 | async-start | bytes 1179648 | tf_op jit(solution)/shard_map/reduce_scatter | solution.py:279
  716.6 1.6 copy-start.10
  774.1 18.8 %copy-start.11 = (f32[8,256,2,96]{1,3,2,0:T(8,128)}, f32[8,256,2,96]{1,3,2,0:T(8,128)S(1)}, u32[]{:S(2)}) copy-start(f32[8,256,2,96]{1,3,2,0:T(8,128)S(1)} %get-tuple-element.117) | copy-start | bytes 4718596
  774.2 37.8 %reduce-scatter.28.cloned.1.call-start = ((), (), s32[]{:S(2)}) async-start(), calls=%async_computation.31 | async-start | bytes 1179648 | tf_op jit(solution)/shard_map/reduce_scatter | solution.py:282
  774.8 77.7 %reduce-scatter.46.cloned.1.call-start = ((), (), s32[]{:S(2)}) async-start(), calls=%async_computation.40 | async-start | bytes 3538944
  796.4 89.5 %reduce-scatter.48.cloned.1.call-start = ((), (), s32[]{:S(2)}) async-start(), calls=%async_computation.41 | async-start | bytes 3538944
  816.3 1.6 copy-start.4
  816.3 131.7 %reduce-scatter.38.cloned.1.call-start = ((), (), s32[]{:S(2)}) async-start(), calls=%async_computation.36 | async-start | bytes 7077888 | tf_op jit(solution)/shard_map/reduce_scatter | solution.py:322
  821.5 189.0 %reduce-scatter.30.cloned.1.call-start = ((), (), s32[]{:S(2)}) async-start(), calls=%async_computation.32 | async-start | bytes 7077888 | tf_op jit(solution)/shard_map/reduce_scatter | solution.py:313
  827.7 273.1 %reduce-scatter.40.cloned.1.call-start = ((), (), s32[]{:S(2)}) async-start(), calls=%async_computation.37 | async-start | bytes 6684672 | tf_op jit(solution)/shard_map/reduce_scatter | solution.py:342
  836.0 353.8 %reduce-scatter.42.cloned.1.call-start = ((), (), s32[]{:S(2)}) async-start(), calls=%async_computation.38 | async-start | bytes 6684672 | tf_op jit(solution)/shard_map/reduce_scatter | solution.py:345
  844.3 433.7 %reduce-scatter.44.cloned.1.call-start = ((), (), s32[]{:S(2)}) async-start(), calls=%async_computation.39 | async-start | bytes 6684672 | tf_op jit(solution)/shard_map/reduce_scatter | solution.py:348
  852.4 487.3 %reduce-scatter.34.cloned.1.call-start = ((), (), s32[]{:S(2)}) async-start(), calls=%async_computation.34 | async-start | bytes 1253376 | tf_op jit(solution)/shard_map/reduce_scatter | solution.py:333
  854.9 545.8 %reduce-scatter.36.cloned.1.call-start = ((), (), s32[]{:S(2)}) async-start(), calls=%async_computation.35 | async-start | bytes 1253376 | tf_op jit(solution)/shard_map/reduce_scatter | solution.py:336
  888.3 578.5 %reduce-scatter.50.cloned.1.call-start = ((), (), s32[]{:S(2)}) async-start(), calls=%async_computation.42 | async-start | bytes 2506752
  952.4 580.2 %reduce-scatter.32.cloned.1.call-start = ((), (), s32[]{:S(2)}) async-start(), calls=%async_computation.33 | async-start | bytes 2506752 | tf_op jit(solution)/shard_map/reduce_scatter | solution.py:330
  1010.6 3.9 copy-start.7
  1014.5 1.7 copy-start.6
  1014.5 1.7 copy-start.12
  1016.2 2.3 copy-start.17
  (4 other events, 4.3 us)
Sparse Core Ops, SparseCore 0:
  10.3 38.6 all-gather.17
  51.3 37.2 all-gather.13
  90.9 41.4 all-gather.21
  134.5 40.9 all-gather.25
  176.9 34.4 all-gather.19
  212.8 38.5 all-gather.15
  253.0 63.4 all-gather.23
  318.0 62.6 all-gather.27
  385.8 27.1 all-gather.29
  415.2 62.7 all-gather.31
  480.3 60.4 all-gather.33
  542.2 24.8 all-gather.37
  569.4 62.7 all-gather.35
  655.9 23.7 reduce-scatter.23
  681.9 26.0 reduce-scatter.21
  774.3 17.4 reduce-scatter.25
  794.5 17.4 reduce-scatter.27
  814.1 34.7 reduce-scatter.45
  851.2 34.6 reduce-scatter.47
  888.1 59.9 reduce-scatter.37
  950.5 60.0 reduce-scatter.29
  1014.5 86.3 reduce-scatter.39
  1105.3 84.4 reduce-scatter.41
  1193.6 84.3 reduce-scatter.43
  1282.0 57.6 reduce-scatter.33
  1343.7 57.0 reduce-scatter.35
  1404.8 61.9 reduce-scatter.49
  1470.6 61.9 reduce-scatter.31
where the time goes:
time: 1550 us; the launch traced here: 1540 us
  waiting for transfers between devices  1220 us (79%)
  matrix products  173 us (11%)
  blocking collectives  69.8 us (5%)
  other arithmetic  31.9 us (2%)
  local copies, waits for them, and re-layouts  23.7 us (2%)
  between operations  17.3 us (1%)
    unnamed x31, waiting for transfers between devices  101 us
    reduce_scatter x1, waiting for transfers between devices, shards(): lax.psum_scatter(grad_up_w.astype(jnp.bfloat16), 'dp', scatter_dimension=...  87 us
    reduce_scatter x1, waiting for transfers between devices, shards(): lax.psum_scatter(grad_down.astype(jnp.bfloat16), 'dp', scatter_dimension=...  86.2 us
    all_gather x1, waiting for transfers between devices, shards(): lax.all_gather(w_down, 'dp', axis=1, tiled=True)  65.1 us
    all_gather x1, waiting for transfers between devices, shards(): lax.all_gather(w_gate, 'dp', axis=0, tiled=True)  64.9 us
    reduce_scatter x1, waiting for transfers between devices, shards(): lax.psum_scatter(grad_query_w.astype(jnp.bfloat16), 'dp', scatter_dimensi...  63.8 us
    reduce_scatter x1, waiting for transfers between devices, shards(): lax.psum_scatter(grad_key_w.astype(jnp.bfloat16), 'dp', scatter_dimension...  59.8 us
    reduce_scatter x1, waiting for transfers between devices, shards(): lax.psum_scatter(grad_out_full.astype(jnp.bfloat16), 'mp', scatter_dimens...  59.7 us
  transfers between devices with their start and end apart: 28, of which 27 were waited for; matrix products, arithmetic and copies ran while one was open for 8% of the time, Pallas kernels for 0%

commit v1 on v0

v1 whole, which is shorter than its diff:
```python
import jax
import jax.numpy as jnp
from jax import lax
from jax.sharding import PartitionSpec as P

HEAD_SIZE = 96
EPSILON = 1e-05
ROPE_BASE = 100000.0
MASKED = -1e30
F32 = jnp.float32
BF16 = jnp.bfloat16


def layout(lengths, rows_total):
    places = jnp.arange(rows_total, dtype=jnp.int32)
    first_end = lengths[0]
    middle_end = lengths[0] + lengths[1]
    last_end = middle_end + lengths[2]
    segment = jnp.where(
        places < first_end,
        0,
        jnp.where(places < middle_end, 1, jnp.where(places < last_end, 2, -1)),
    ).astype(jnp.int32)
    offset = jnp.where(places < first_end, 0, jnp.where(places < middle_end, first_end, middle_end))
    position = jnp.where(segment >= 0, places - offset, 0)
    return segment, position


def rotation(position):
    half_dim = HEAD_SIZE // 2
    inverse = ROPE_BASE ** (-jnp.arange(half_dim, dtype=F32) * 2.0 / HEAD_SIZE)
    angles = position.astype(F32)[:, None] * inverse[None, :]
    return jnp.cos(angles)[:, None, :], jnp.sin(angles)[:, None, :]


def rotate(tensor, cosine, sine):
    half_dim = tensor.shape[-1] // 2
    lead, tail = tensor[..., :half_dim], tensor[..., half_dim:]
    return jnp.concatenate([lead * cosine - tail * sine, tail * cosine + lead * sine], axis=-1)


def rms_parts(inputs):
    factor = lax.rsqrt(jnp.mean(inputs * inputs, axis=-1, keepdims=True) + EPSILON)
    return factor, inputs * factor


def rms_back(inputs, gain, gradient):
    factor, normed = rms_parts(inputs)
    gain_grad = jnp.sum(gradient * normed, axis=0)
    scaled = gradient * gain
    return (
        factor * (scaled - normed * jnp.mean(scaled * normed, axis=-1, keepdims=True)),
        gain_grad,
    )


def mul(left, right):
    return jnp.dot(left, right, preferred_element_type=F32)


def mul_t(left, right):
    return lax.dot_general(left, right, (((1,), (1,)), ((), ())), preferred_element_type=F32)


def outer_sum(left, right):
    return lax.dot_general(left, right, (((0,), (0,)), ((), ())), preferred_element_type=F32)


def mp_shift(block, step, parts):
    return lax.ppermute(block, "mp", [(i, (i + step) % parts) for i in range(parts)])


def mp_gather(block, parts):
    me = lax.axis_index("mp")
    rows = block.shape[0]
    whole = jnp.zeros((parts * rows,) + block.shape[1:], block.dtype)
    for step in range(parts):
        piece = block if step == 0 else mp_shift(block, step, parts)
        owner = lax.rem(me - step + parts, parts)
        whole = lax.dynamic_update_slice_in_dim(whole, piece, owner * rows, 0)
    return whole


def mp_sum_rows(whole, parts):
    me = lax.axis_index("mp")
    rows = whole.shape[0] // parts
    total = lax.dynamic_slice_in_dim(whole, me * rows, rows, 0)
    for step in range(1, parts):
        owner = lax.rem(me + step, parts)
        piece = lax.dynamic_slice_in_dim(whole, owner * rows, rows, 0).astype(BF16)
        total = total + mp_shift(piece, step, parts).astype(F32)
    return total


def shards(
    tokens,
    seq_lengths,
    norm_attn,
    w_query,
    key_weight,
    value_weight,
    w_out,
    norm_mlp,
    w_gate,
    w_up,
    w_down,
    cotangent,
):
    parts = lax.axis_size("mp")
    rows = tokens.shape[0]
    group = rows * parts
    q_width, kv_width, hidden_width = w_query.shape[1], key_weight.shape[1], w_gate.shape[1]
    heads, kv_heads = q_width // HEAD_SIZE, kv_width // HEAD_SIZE
    members = heads // kv_heads
    factor = HEAD_SIZE ** (-0.5)

    attn_w = lax.all_gather(
        jnp.concatenate([w_query, key_weight, value_weight, w_out.T], axis=1),
        "dp", axis=0, tiled=True,
    )
    mlp_w = lax.all_gather(
        jnp.concatenate([w_gate, w_up, w_down.T], axis=1), "dp", axis=0, tiled=True
    )
    cuts = (q_width, q_width + kv_width, q_width + 2 * kv_width)
    query_w, key_w, value_w, out_wt = jnp.split(attn_w, cuts, axis=1)
    gate_w, up_w, down_wt = jnp.split(mlp_w, 3, axis=1)

    inputs = tokens.astype(F32)
    gain_one, gain_two = norm_attn.astype(F32), norm_mlp.astype(F32)
    normed_one = mp_gather((rms_parts(inputs)[1] * gain_one).astype(BF16), parts)
    grad_rows = mp_gather(cotangent, parts)

    segment, position = layout(seq_lengths[0], group)
    cosine, sine = rotation(position)
    places = jnp.arange(group, dtype=jnp.int32)
    allowed = (
        (places[:, None] >= places[None, :])
        & (segment[:, None] == segment[None, :])
        & ((segment[None, :] >= 0) | (places[:, None] == places[None, :]))
    )

    query = rotate(mul(normed_one, query_w).reshape(group, heads, HEAD_SIZE), cosine, sine)
    key = rotate(mul(normed_one, key_w).reshape(group, kv_heads, HEAD_SIZE), cosine, sine)
    value = mul(normed_one, value_w).astype(BF16).reshape(group, kv_heads, HEAD_SIZE)
    query = query.astype(BF16).reshape(group, kv_heads, members, HEAD_SIZE)
    key = key.astype(BF16)
    scores = jnp.einsum("qhgd,khd->hgqk", query, key, preferred_element_type=F32) * factor
    scores = jnp.where(allowed[None, None], scores, MASKED)
    peak = jnp.max(scores, axis=-1, keepdims=True)
    grown = jnp.exp(scores - peak)
    probs = grown / jnp.sum(grown, axis=-1, keepdims=True)
    probs_low = probs.astype(BF16)
    attended = (
        jnp.einsum("hgqk,khd->qhgd", probs_low, value, preferred_element_type=F32)
        .astype(BF16)
        .reshape(group, q_width)
    )
    residual = inputs + mp_sum_rows(mul_t(attended, out_wt), parts)
    normed_two = mp_gather((rms_parts(residual)[1] * gain_two).astype(BF16), parts)

    gate_act, up_act = mul(normed_two, gate_w), mul(normed_two, up_w)
    sigmoid_g = jax.nn.sigmoid(gate_act)
    swish = gate_act * sigmoid_g
    hidden = (swish * up_act).astype(BF16)
    branch = mul_t(hidden, down_wt)
    grad_hidden = mul(grad_rows, down_wt)
    grad_gate = (grad_hidden * up_act * sigmoid_g * (1.0 + gate_act * (1.0 - sigmoid_g))).astype(
        BF16
    )
    grad_up = (grad_hidden * swish).astype(BF16)
    grad_mlp = jnp.concatenate(
        [
            outer_sum(normed_two, grad_gate).astype(BF16),
            outer_sum(normed_two, grad_up).astype(BF16),
            outer_sum(grad_rows, hidden).astype(BF16),
        ],
        axis=1,
    )
    grad_mlp = lax.psum_scatter(grad_mlp, "dp", scatter_dimension=0, tiled=True)
    grad_two = mp_sum_rows(mul_t(grad_gate, gate_w) + mul_t(grad_up, up_w), parts)
    block_out = (residual + mp_sum_rows(branch, parts)).astype(BF16)

    from_two, gain_two_grad = rms_back(residual, gain_two, grad_two)
    grad_residual = cotangent.astype(F32) + from_two
    grad_branch = mp_gather(grad_residual.astype(BF16), parts)
    grad_attended = (
        mul(grad_branch, out_wt).astype(BF16).reshape(group, kv_heads, members, HEAD_SIZE)
    )
    dprob = jnp.einsum("qhgd,khd->hgqk", grad_attended, value, preferred_element_type=F32)
    inner = jnp.sum(probs * dprob, axis=-1, keepdims=True)
    dscore = (probs * (dprob - inner)).astype(BF16)
    grad_query = jnp.einsum("hgqk,khd->qhgd", dscore, key, preferred_element_type=F32) * factor
    grad_key = jnp.einsum("hgqk,qhgd->khd", dscore, query, preferred_element_type=F32) * factor
    grad_value = jnp.einsum(
        "hgqk,qhgd->khd", probs_low, grad_attended, preferred_element_type=F32
    )
    grad_query = rotate(grad_query.reshape(group, heads, HEAD_SIZE), cosine, -sine)
    grad_query = grad_query.astype(BF16).reshape(group, q_width)
    grad_key = rotate(grad_key, cosine, -sine).astype(BF16).reshape(group, kv_width)
    grad_value = grad_value.astype(BF16).reshape(group, kv_width)
    grad_attn = jnp.concatenate(
        [
            outer_sum(normed_one, grad_query).astype(BF16),
            outer_sum(normed_one, grad_key).astype(BF16),
            outer_sum(normed_one, grad_value).astype(BF16),
            outer_sum(grad_branch, attended).astype(BF16),
        ],
        axis=1,
    )
    grad_attn = lax.psum_scatter(grad_attn, "dp", scatter_dimension=0, tiled=True)
    grad_one = mp_sum_rows(
        mul_t(grad_query, query_w) + mul_t(grad_key, key_w) + mul_t(grad_value, value_w), parts
    )
    from_one, gain_one_grad = rms_back(inputs, gain_one, grad_one)
    grad_tokens = (grad_residual + from_one).astype(BF16)
    gains = lax.psum(jnp.stack([gain_one_grad, gain_two_grad]), ("dp", "mp"))

    attn_parts = jnp.split(grad_attn.astype(F32), cuts, axis=1)
    mlp_parts = jnp.split(grad_mlp.astype(F32), 3, axis=1)
    return (
        block_out,
        grad_tokens,
        gains[0],
        attn_parts[0],
        attn_parts[1],
        attn_parts[2],
        attn_parts[3].T,
        gains[1],
        mlp_parts[0],
        mlp_parts[1],
        mlp_parts[2].T,
    )


def solution(mesh):
    rows, whole = P(("dp", "mp"), None), P()
    split, turned = P("dp", "mp"), P("mp", "dp")
    return jax.shard_map(
        shards,
        mesh=mesh,
        in_specs=(
            rows, P("dp", None), whole, split, split, split, turned, whole, split, split, turned, rows,
        ),
        out_specs=(
            rows, rows, whole, split, split, split, turned, whole, split, split, turned,
        ),
        check_vma=False,
    )
```

time: 1550 us -> 614 us (0.40)
  waiting for transfers between devices: 1220 us -> 362 us
  matrix products: 173 us -> 97.3 us
  blocking collectives: 69.8 us -> 42.6 us
    all_gather x13 -> x2, waiting for transfers between devices: 535 us -> 63.5 us  [the longest x1 45.6 us: shards(): lax.all_gather(jnp.concatenate([w_query, key_weight, value_weight, w_out....]
    reduce_scatter x12 -> x1, waiting for transfers between devices: 586 us -> 178 us  [shards(): grad_mlp = lax.psum_scatter(grad_mlp, 'dp', scatter_dimension=0, tiled=True)]
    ppermute x0 -> x8, waiting for transfers between devices: none -> 121 us  [mp_shift(): lax.ppermute(block, 'mp', [(i, (i + step) % parts) for i in range(parts)])]
    unnamed x31 -> x5, waiting for transfers between devices: 101 us -> 0.07 us
    dot_general x77 -> x26, matrix products: 173 us -> 91.3 us  [the longest x7 32.9 us: mul(): return jnp.dot(left, right, preferred_element_type=F32)]
    all_gather x2 -> x0, blocking collectives: 28.3 us -> none  [the longest x1 15 us: shards(): lax.all_gather(key_rot, 'mp', axis=0, tiled=True)]
    concatenate x3 -> x6, other arithmetic: 0.13 us -> 24.3 us  [the longest x1 16.4 us: shards(): jnp.concatenate([outer_sum(normed_two, grad_gate).astype(BF16), outer_sum...]
  transfers between devices with their start and end apart: 28 -> 12, of which waited for: 27 -> 11; matrix products, arithmetic and copies ran while one was open for 8% -> 16% of each run, Pallas kernels for 0% -> 0%
where the time goes in v1:
time: 614 us; the launch traced here: 606 us
  waiting for transfers between devices  362 us (59%)
  matrix products  97.3 us (16%)
  other arithmetic  44.3 us (7%)
  blocking collectives  42.6 us (7%)
  local copies, waits for them, and re-layouts  35.9 us (6%)
  between operations  16.9 us (3%)
  starting transfers between devices  6.68 us (1%)
    reduce_scatter x1, waiting for transfers between devices, shards(): grad_mlp = lax.psum_scatter(grad_mlp, 'dp', scatter_dimension=0, tiled=True)  178 us
    ppermute x8, waiting for transfers between devices, mp_shift(): lax.ppermute(block, 'mp', [(i, (i + step) % parts) for i in range(parts)])  121 us
    all_gather x1, waiting for transfers between devices, shards(): lax.all_gather(jnp.concatenate([w_query, key_weight, value_weight, w_out....  45.6 us
    psum x1, blocking collectives, shards(): gains = lax.psum(jnp.stack([gain_one_grad, gain_two_grad]), ('dp', 'mp'))  42.6 us
    dot_general x7, matrix products, mul(): return jnp.dot(left, right, preferred_element_type=F32)  32.9 us
    unnamed x84, local copies, waits for them, and re-layouts  24.8 us
    dot_general x7, matrix products, mul_t(): lax.dot_general(left, right, (((1,), (1,)), ((), ())), preferred_element_...  24.6 us
    dot_general x7, matrix products, outer_sum(): lax.dot_general(left, right, (((0,), (0,)), ((), ())), preferred_element_...  20.8 us
  transfers between devices with their start and end apart: 12, of which 11 were waited for; matrix products, arithmetic and copies ran while one was open for 16% of the time, Pallas kernels for 0%

profile of v1, /device:TPU:10, one launch (start us, length us, event | category | flops | bytes accessed | tf_op | source)
XLA Modules:
  0.0 605.8 jit_solution(16463034688795348160)
XLA Ops:
  7.2 1.8 pad_maximum_fusion.5
  9.2 2.5 pad_maximum_fusion.2
  19.0 13.7 %collective-permute-done = bf16[256,1536]{1,0:T(8,128)(2,1)S(1)} collective-permute-done((bf16[256,1536]{1,0:T(8,128)(2,1)}, bf16[256,1536]{1,0:T(8,128)(2,1)S(1)}, u32[]{:S(2)}, u32[]{:S(2)}) %collective-permute-start) | collective-permute-done | bytes 786464 | tf_op jit(solution)/shard_map/ppermute | solution.py:70
  32.8 45.6 %all-gather.3.cloned.1.call-done = bf16[1536,2304]{1,0:T(8,128)(2,1)} async-done(((bf16[96,2304]{1,0:T(8,128)(2,1)}), bf16[1536,2304]{1,0:T(8,128)(2,1)}) %all-gather.3.cloned.1.call-update) | async-done | bytes 7077904 | tf_op jit(solution)/shard_map/all_gather | solution.py:117
  78.5 2.1 fusion.66
  81.4 3.6 fusion.38
  85.3 1.6 copy-done.14
  86.9 2.4 convolution_convert_fusion.7
  89.3 6.0 fusion.86
  95.4 4.3 fusion.51
  100.6 3.3 fusion.34
  104.0 1.6 copy-done.6
  107.7 18.5 %collective-permute-done.1 = bf16[256,1536]{1,0:T(8,128)(2,1)} collective-permute-done((bf16[256,1536]{1,0:T(8,128)(2,1)S(1)}, bf16[256,1536]{1,0:T(8,128)(2,1)}, u32[]{:S(2)}, u32[]{:S(2)}) %collective-permute-start.1) | collective-permute-done | bytes 786464 | tf_op jit(solution)/shard_map/ppermute | solution.py:70
  126.1 2.1 multiply_reduce_fusion.2
  133.5 9.5 %collective-permute-done.4 = bf16[256,1536]{1,0:T(8,128)(2,1)} collective-permute-done((bf16[256,1536]{1,0:T(8,128)(2,1)S(1)}, bf16[256,1536]{1,0:T(8,128)(2,1)}, u32[]{:S(2)}, u32[]{:S(2)}) %collective-permute-start.4) | collective-permute-done | bytes 786464 | tf_op jit(solution)/shard_map/ppermute | solution.py:70
  143.0 2.1 constant_dynamic-update-slice_fusion.2
  145.1 13.8 %collective-permute-done.2 = bf16[256,1536]{1,0:T(8,128)(2,1)S(1)} collective-permute-done((bf16[256,1536]{1,0:T(8,128)(2,1)S(1)}, bf16[256,1536]{1,0:T(8,128)(2,1)S(1)}, u32[]{:S(2)}, u32[]{:S(2)}) %collective-permute-start.2) | collective-permute-done | bytes 786464 | tf_op jit(solution)/shard_map/ppermute | solution.py:70
  159.9 17.8 %all-gather.5.cloned.1.call-done = bf16[1536,6144]{1,0:T(8,128)(2,1)} async-done(((bf16[96,6144]{1,0:T(8,128)(2,1)}), bf16[1536,6144]{1,0:T(8,128)(2,1)}) %all-gather.5.cloned.1.call-update) | async-done | bytes 18874384 | tf_op jit(solution)/shard_map/all_gather | solution.py:121
  177.7 6.1 %fusion.5 = f32[512,2048]{1,0:T(8,128)S(1)} fusion(bf16[512,1536]{1,0:T(8,128)(2,1)} %constant_dynamic-update-slice_fusion.2, bf16[1536,6144]{1,0:T(8,128)(2,1)} %all-gather.5.cloned.1.call-done), kind=kOutput, calls=%fused_computation.14 | convolution fusion | flops 3221225472 | bytes 12058624 | tf_op jit(solution)/shard_map/dot_general | solution.py:58
  183.9 2.6 copy-done.29
  186.4 6.5 %fusion.11 = f32[512,2048]{1,0:T(8,128)} fusion(bf16[512,1536]{1,0:T(8,128)(2,1)} %constant_dynamic-update-slice_fusion.4, bf16[1536,6144]{1,0:T(8,128)(2,1)S(1)} %copy-done.29), kind=kOutput, calls=%fused_computation.20 | convolution fusion | flops 3221225472 | bytes 12058624 | tf_op jit(solution)/shard_map/dot_general | solution.py:58
  193.0 9.1 %multiply_convert_fusion.1 = (bf16[512,2048]{1,0:T(8,128)(2,1)}, bf16[512,2048]{1,0:T(8,128)(2,1)S(1)}, bf16[512,2048]{1,0:T(8,128)(2,1)}) fusion(f32[512,2048]{1,0:T(8,128)S(1)} %fusion.5, f32[512,2048]{1,0:T(8,128)} %fusion.11, bf16[512,1536]{1,0:T(8,128)(2,1)} %constant_dynamic-update-slice_fusion.4, bf16[1536,6144]{1,0:T(8,128)(2,1)S(1)} %copy-done.29), kind=kOutput, calls=%fused_computation.27 | convolution fusion | flops 3236954112 | bytes 22544384 | tf_op jit(solution)/shard_map/dot_general | solution.py:58
  202.1 3.5 fusion.9
  205.5 5.1 fusion.21
  211.3 5.0 fusion.7
  216.5 1.5 collective-permute-start.3
  218.0 13.1 %collective-permute-done.5 = bf16[256,1536]{1,0:T(8,128)(2,1)S(1)} collective-permute-done((bf16[256,1536]{1,0:T(8,128)(2,1)S(1)}, bf16[256,1536]{1,0:T(8,128)(2,1)S(1)}, u32[]{:S(2)}, u32[]{:S(2)}) %collective-permute-start.5) | collective-permute-done | bytes 786464 | tf_op jit(solution)/shard_map/ppermute | solution.py:70
  231.2 16.2 %collective-permute-done.3 = bf16[256,1536]{1,0:T(8,128)(2,1)S(1)} collective-permute-done((bf16[256,1536]{1,0:T(8,128)(2,1)S(1)}, bf16[256,1536]{1,0:T(8,128)(2,1)S(1)}, u32[]{:S(2)}, u32[]{:S(2)}) %collective-permute-start.3) | collective-permute-done | bytes 786464 | tf_op jit(solution)/shard_map/ppermute | solution.py:70
  247.3 1.7 multiply_reduce_fusion
  249.1 1.7 constant_dynamic-update-slice_fusion.1
  251.4 18.3 %collective-permute-done.6 = bf16[256,1536]{1,0:T(8,128)(2,1)S(1)} collective-permute-done((bf16[256,1536]{1,0:T(8,128)(2,1)S(1)}, bf16[256,1536]{1,0:T(8,128)(2,1)S(1)}, u32[]{:S(2)}, u32[]{:S(2)}) %collective-permute-start.6) | collective-permute-done | bytes 786464 | tf_op jit(solution)/shard_map/ppermute | solution.py:70
  271.0 3.1 fusion.48
  274.4 5.1 fusion.1
  280.3 2.3 fusion.3
  292.6 3.5 pad_maximum_fusion.1
  296.1 9.9 %copy.69 = bf16[1536,2304]{1,0:T(8,128)(2,1)} copy(bf16[1536,2304]{0,1:T(8,128)(2,1)} %pad_maximum_fusion.1) | data formatting | bytes 14155776
  306.1 5.7 convolution_convert_fusion
  311.8 5.5 convolution_convert_fusion.1
  317.4 5.2 convolution_convert_fusion.2
  322.7 16.4 %pad_maximum_fusion = bf16[1536,6144]{1,0:T(8,128)(2,1)} fusion(bf16[1536,2048]{1,0:T(8,128)(2,1)S(1)} %convolution_convert_fusion, bf16[1536,2048]{1,0:T(8,128)(2,1)S(1)} %convolution_convert_fusion.1, bf16[1536,2048]{1,0:T(8,128)(2,1)S(1)} %convolution_convert_fusion.2), kind=kLoop, calls=%fused_computation.1 | loop fusion | flops 56623104 | bytes 37748736 | tf_op jit(solution)/shard_map/concatenate | solution.py:171
  339.0 3.1 fusion.36
  342.1 2.3 convolution_add_fusion.1
  344.5 2.3 convolution_add_fusion
  347.6 17.6 %collective-permute-done.7 = bf16[256,1536]{1,0:T(8,128)(2,1)S(1)} collective-permute-done((bf16[256,1536]{1,0:T(8,128)(2,1)S(1)}, bf16[256,1536]{1,0:T(8,128)(2,1)S(1)}, u32[]{:S(2)}, u32[]{:S(2)}) %collective-permute-start.7) | collective-permute-done | bytes 786464 | tf_op jit(solution)/shard_map/ppermute | solution.py:70
  365.9 42.6 %psum.7 = f32[2,1536]{1,0:T(2,128)S(1)} all-reduce(f32[2,1536]{1,0:T(2,128)S(1)} %pad_maximum_fusion.14), channel_id=1, replica_groups=mesh['dp'=16,'mp'=2] {'dp','mp'}, use_global_device_ids=true, to_apply=%region_9.10 | all-reduce | flops 3072 | bytes 24576 | tf_op jit(solution)/shard_map/psum | solution.py:216
  409.2 3.2 fusion.45
  417.3 177.7 %reduce-scatter.5.cloned.1.call-done = bf16[96,6144]{1,0:T(8,128)(2,1)} async-done(((bf16[1536,6144]{1,0:T(8,128)(2,1)}), bf16[96,6144]{1,0:T(8,128)(2,1)}) %reduce-scatter.5.cloned.1.call-update) | async-done | bytes 1179664 | tf_op jit(solution)/shard_map/reduce_scatter | solution.py:179
  595.0 1.6 convert_element_type.170
  (149 shorter events, 38.8 us)
Async XLA Ops:
  7.2 71.3 %all-gather.3.cloned.1.call-start = ((), (), s32[]{:S(2)}) async-start(), calls=%async_computation.2 | async-start | bytes 7520256 | tf_op jit(solution)/shard_map/all_gather | solution.py:117
  9.1 2.6 copy-start.27
  9.1 2.7 copy-start
  9.1 168.6 %all-gather.5.cloned.1.call-start = ((), (), s32[]{:S(2)}) async-start(), calls=%async_computation.3 | async-start | bytes 20054016 | tf_op jit(solution)/shard_map/all_gather | solution.py:121
  11.6 400.7 %reduce-scatter.7.cloned.1.call-start = ((), (), s32[]{:S(2)}) async-start(), calls=%async_computation.5 | async-start | bytes 7520256
  11.7 1.5 copy-start.20
  12.0 1.8 copy-start.26
  12.0 1.3 copy-start.24
  13.3 19.5 %collective-permute-start = (bf16[256,1536]{1,0:T(8,128)(2,1)}, bf16[256,1536]{1,0:T(8,128)(2,1)S(1)}, u32[]{:S(2)}, u32[]{:S(2)}) collective-permute-start(bf16[256,1536]{1,0:T(8,128)(2,1)} %get-tuple-element.58), channel_id=1, source_target_pairs={{0,1},{1,0},{2,3},{3,2},{4,5},{5,4},{6,7},{7,6},{8,9},{9,8},{10,11... | collective-permute-start | bytes 2359304 | tf_op jit(solution)/shard_map/ppermute | solution.py:70
  32.8 47.7 %copy-start.13 = (bf16[512,1536]{1,0:T(8,128)(2,1)}, bf16[512,1536]{1,0:T(8,128)(2,1)S(1)}, u32[]{:S(2)}) copy-start(bf16[512,1536]{1,0:T(8,128)(2,1)S(1)} %constant_dynamic-update-slice_fusion.6) | copy-start | bytes 4718596
  85.0 1.8 copy-start.14
  86.9 8.5 %copy-start.7 = (bf16[512,8,48]{0,2,1:T(8,128)(2,1)}, bf16[512,8,48]{0,2,1:T(8,128)(2,1)S(1)}, u32[]{:S(2)}) copy-start(bf16[512,8,48]{0,2,1:T(8,128)(2,1)S(1)} %get-tuple-element.64) | copy-start | bytes 1179652
  86.9 8.5 %copy-start.9 = (bf16[512,8,48]{0,2,1:T(8,128)(2,1)}, bf16[512,8,48]{0,2,1:T(8,128)(2,1)S(1)}, u32[]{:S(2)}) copy-start(bf16[512,8,48]{0,2,1:T(8,128)(2,1)S(1)} %get-tuple-element.65) | copy-start | bytes 1179652
  86.9 2.5 copy-start.16
  86.9 2.5 copy-start.17
  86.9 2.5 copy-start.19
  89.3 6.1 %copy-start.32 = (bf16[512,384]{0,1:T(8,128)(2,1)}, bf16[512,384]{0,1:T(8,128)(2,1)S(1)}, u32[]{:S(2)}) copy-start(bf16[512,384]{0,1:T(8,128)(2,1)S(1)} %convolution_convert_fusion.7) | copy-start | bytes 1179652
  95.4 4.4 copy-start.22
  100.6 5.6 copy-start.5
  100.6 7.1 %copy-start.28 = (bf16[1536]{0:T(1024)(128)(2,1)S(1)}, bf16[1536]{0:T(1024)(128)(2,1)}, u32[]{:S(2)}) copy-start(bf16[1536]{0:T(1024)(128)(2,1)} %param.19) | copy-start | bytes 9220
  103.9 1.7 copy-start.6
  105.6 20.5 %collective-permute-start.1 = (bf16[256,1536]{1,0:T(8,128)(2,1)S(1)}, bf16[256,1536]{1,0:T(8,128)(2,1)}, u32[]{:S(2)}, u32[]{:S(2)}) collective-permute-start(bf16[256,1536]{1,0:T(8,128)(2,1)S(1)} %dynamic-slice_convert_fusion.3), channel_id=1, source_target_pairs={{0,1},{1,0},{2,3},{3,2},{4,5},{5,4},{6,7},{7,6},{8,9},{9,8},{10,11... | collective-permute-start | bytes 2359304 | tf_op jit(solution)/shard_map/ppermute | solution.py:70
  106.2 36.8 %collective-permute-start.4 = (bf16[256,1536]{1,0:T(8,128)(2,1)S(1)}, bf16[256,1536]{1,0:T(8,128)(2,1)}, u32[]{:S(2)}, u32[]{:S(2)}) collective-permute-start(bf16[256,1536]{1,0:T(8,128)(2,1)S(1)} %copy-done.5), channel_id=1, source_target_pairs={{0,1},{1,0},{2,3},{3,2},{4,5},{5,4},{6,7},{7,6},{8,9},{9,8},{10,11... | collective-permute-start | bytes 2359304 | tf_op jit(solution)/shard_map/ppermute | solution.py:70
  130.7 28.2 %collective-permute-start.2 = (bf16[256,1536]{1,0:T(8,128)(2,1)S(1)}, bf16[256,1536]{1,0:T(8,128)(2,1)S(1)}, u32[]{:S(2)}, u32[]{:S(2)}) collective-permute-start(bf16[256,1536]{1,0:T(8,128)(2,1)S(1)} %get-tuple-element.54), channel_id=1, source_target_pairs={{0,1},{1,0},{2,3},{3,2},{4,5},{5,4},{6,7},{7,6},{8,9},{9,8},{10,11... | collective-permute-start | bytes 2359304 | tf_op jit(solution)/shard_map/ppermute | solution.py:70
  177.7 8.7 %copy-start.29 = (bf16[1536,6144]{1,0:T(8,128)(2,1)S(1)}, bf16[1536,6144]{1,0:T(8,128)(2,1)}, u32[]{:S(2)}) copy-start(bf16[1536,6144]{1,0:T(8,128)(2,1)} %all-gather.5.cloned.1.call-done) | copy-start | bytes 56623108
  202.1 3.5 copy-start.35
  210.7 20.4 %collective-permute-start.5 = (bf16[256,1536]{1,0:T(8,128)(2,1)S(1)}, bf16[256,1536]{1,0:T(8,128)(2,1)S(1)}, u32[]{:S(2)}, u32[]{:S(2)}) collective-permute-start(bf16[256,1536]{1,0:T(8,128)(2,1)S(1)} %dynamic-slice_convert_fusion.1), channel_id=1, source_target_pairs={{0,1},{1,0},{2,3},{3,2},{4,5},{5,4},{6,7},{7,6},{8,9},{9,8},{10,11... | collective-permute-start | bytes 2359304 | tf_op jit(solution)/shard_map/ppermute | solution.py:70
  216.5 30.8 %collective-permute-start.3 = (bf16[256,1536]{1,0:T(8,128)(2,1)S(1)}, bf16[256,1536]{1,0:T(8,128)(2,1)S(1)}, u32[]{:S(2)}, u32[]{:S(2)}) collective-permute-start(bf16[256,1536]{1,0:T(8,128)(2,1)S(1)} %dynamic-slice_convert_fusion.2), channel_id=1, source_target_pairs={{0,1},{1,0},{2,3},{3,2},{4,5},{5,4},{6,7},{7,6},{8,9},{9,8},{10,11... | collective-permute-start | bytes 2359304 | tf_op jit(solution)/shard_map/ppermute | solution.py:70
  250.9 18.9 %collective-permute-start.6 = (bf16[256,1536]{1,0:T(8,128)(2,1)S(1)}, bf16[256,1536]{1,0:T(8,128)(2,1)S(1)}, u32[]{:S(2)}, u32[]{:S(2)}) collective-permute-start(bf16[256,1536]{1,0:T(8,128)(2,1)S(1)} %get-tuple-element.51), channel_id=1, source_target_pairs={{0,1},{1,0},{2,3},{3,2},{4,5},{5,4},{6,7},{7,6},{8,9},{9,8},{10,11... | collective-permute-start | bytes 2359304 | tf_op jit(solution)/shard_map/ppermute | solution.py:70
  269.8 1.2 copy-start.11
  271.0 3.4 copy-start.23
  271.0 3.4 copy-start.33
  274.4 5.1 slice-start
  274.4 5.8 slice-start.1
  280.3 2.4 copy-start.18
  285.1 1.5 copy-start.12
  285.2 1.6 copy-start.31
  288.1 1.4 copy-start.15
  306.1 288.9 %reduce-scatter.5.cloned.1.call-start = ((), (), s32[]{:S(2)}) async-start(), calls=%async_computation.4 | async-start | bytes 20054016 | tf_op jit(solution)/shard_map/reduce_scatter | solution.py:179
  306.1 5.7 copy-start.36
  311.8 5.6 copy-start.34
  344.5 20.8 %copy-start.21 = (f32[1536]{0:T(1024)S(1)}, f32[1536]{0:T(1024)}, u32[]{:S(2)}) copy-start(f32[1536]{0:T(1024)} %copy-done.20) | copy-start | bytes 18436
  344.5 20.8 %copy-start.25 = (f32[256]{0:T(256)S(1)}, f32[256]{0:T(256)}, u32[]{:S(2)}) copy-start(f32[256]{0:T(256)} %copy-done.24) | copy-start | bytes 3076
  346.8 19.1 %copy-start.2 = (f32[512,1536]{1,0:T(8,128)}, f32[512,1536]{1,0:T(8,128)S(1)}, u32[]{:S(2)}) copy-start(f32[512,1536]{1,0:T(8,128)S(1)} %convolution_add_fusion) | copy-start | bytes 9437188
  346.8 18.4 %copy-start.1 = (bf16[256,1536]{1,0:T(8,128)(2,1)S(1)}, bf16[256,1536]{1,0:T(8,128)(2,1)}, u32[]{:S(2)}) copy-start(bf16[256,1536]{1,0:T(8,128)(2,1)} %param.12) | copy-start | bytes 2359300
  346.8 62.4 %copy-start.4 = (f32[256,1536]{1,0:T(8,128)S(1)}, f32[256,1536]{1,0:T(8,128)}, u32[]{:S(2)}) copy-start(f32[256,1536]{1,0:T(8,128)} %get-tuple-element.52) | copy-start | bytes 4718596
  346.9 18.3 %collective-permute-start.7 = (bf16[256,1536]{1,0:T(8,128)(2,1)S(1)}, bf16[256,1536]{1,0:T(8,128)(2,1)S(1)}, u32[]{:S(2)}, u32[]{:S(2)}) collective-permute-start(bf16[256,1536]{1,0:T(8,128)(2,1)S(1)} %dynamic-slice_convert_fusion), channel_id=1, source_target_pairs={{0,1},{1,0},{2,3},{3,2},{4,5},{5,4},{6,7},{7,6},{8,9},{9,8},{10,11... | collective-permute-start | bytes 2359304 | tf_op jit(solution)/shard_map/ppermute | solution.py:70
  595.0 2.5 copy-start.3
  (3 other events, 3.0 us)
Sparse Core Ops, SparseCore 0:
  10.9 67.5 all-gather.2
  80.0 97.6 all-gather.4
  306.2 91.1 reduce-scatter.6
  401.9 193.0 reduce-scatter.4

commit v2 on v1

--- a/solution.py
+++ b/solution.py
@@ -1,6 +1,10 @@
+import functools
+
 import jax
 import jax.numpy as jnp
 from jax import lax
+from jax.experimental import pallas as pl
+from jax.experimental.pallas import tpu as pltpu
 from jax.sharding import PartitionSpec as P
 
 HEAD_SIZE = 96
@@ -44,16 +48,6 @@
     return factor, inputs * factor
 
 
-def rms_back(inputs, gain, gradient):
-    factor, normed = rms_parts(inputs)
-    gain_grad = jnp.sum(gradient * normed, axis=0)
-    scaled = gradient * gain
-    return (
-        factor * (scaled - normed * jnp.mean(scaled * normed, axis=-1, keepdims=True)),
-        gain_grad,
-    )
-
-
 def mul(left, right):
     return jnp.dot(left, right, preferred_element_type=F32)
 
@@ -90,6 +84,498 @@
         piece = lax.dynamic_slice_in_dim(whole, owner * rows, rows, 0).astype(BF16)
         total = total + mp_shift(piece, step, parts).astype(F32)
     return total
+
+
+MESH = pl.DeviceIdType.MESH
+VMEM_SPEC = pl.BlockSpec(memory_space=pltpu.VMEM)
+ANY_SPEC = pl.BlockSpec(memory_space=pl.ANY)
+DMA = pltpu.SemaphoreType.DMA
+
+
+def place(depth, parts):
+    me, part = lax.axis_index("dp"), lax.axis_index("mp")
+    z, y, core = me // 4, lax.rem(me // 2, 2), lax.rem(me, 2)
+
+    def dp_of(step, at_y, at_core):
+        return lax.rem(z + step, depth) * 4 + at_y * 2 + at_core
+
+    def mp_of(step):
+        return lax.rem(part + step, parts)
+
+    return me, part, z, y, core, dp_of, mp_of
+
+
+def greet(depth, parts):
+    me, part, z, y, core, dp_of, mp_of = place(depth, parts)
+    near = [(dp_of(0, y, 1 - core), part), (dp_of(0, 1 - y, core), part)]
+    near += [(dp_of(step, y, core), part) for step in range(1, depth)]
+    near += [(me, mp_of(step)) for step in range(1, parts)]
+    barrier = pltpu.get_barrier_semaphore()
+    for device in near:
+        pl.semaphore_signal(barrier, inc=1, device_id=device, device_id_type=MESH)
+    pl.semaphore_wait(barrier, len(near))
+
+
+def send(source, target, sems, at, device):
+    sent, landed = sems
+    copy = pltpu.make_async_remote_copy(
+        src_ref=source,
+        dst_ref=target,
+        send_sem=sent.at[at],
+        recv_sem=landed.at[at],
+        device_id=device,
+        device_id_type=MESH,
+    )
+    return copy
+
+
+def gather_kernel(depth, parts, shard, normed, cot, weights, normed_all, cot_all,
+                  z_sent, z_got, y_sent, y_got, c_sent, c_got, x_sent, x_got, kept):
+    me, part, z, y, core, dp_of, mp_of = place(depth, parts)
+    own = [
+        pltpu.make_async_copy(shard, weights.at[me], kept.at[0]),
+        pltpu.make_async_copy(normed, normed_all.at[part], kept.at[1]),
+        pltpu.make_async_copy(cot, cot_all.at[part], kept.at[2]),
+    ]
+    for copy in own:
+        copy.start()
+    greet(depth, parts)
+    other_y, other_core = (dp_of(0, 1 - y, core), part), (dp_of(0, y, 1 - core), part)
+
+    along_z = [
+        send(shard, weights.at[me], (z_sent, z_got), step - 1, (dp_of(step, y, core), part))
+        for step in range(1, depth)
+    ]
+    along_x = [
+        send(source, target.at[part], (x_sent, x_got), 2 * (step - 1) + i, (me, mp_of(step)))
+        for i, (source, target) in enumerate(((normed, normed_all), (cot, cot_all)))
+        for step in range(1, parts)
+    ]
+
+    def block_from(step, at_y):
+        return weights.at[dp_of(depth - step, at_y, core)]
+
+    def to_y(step):
+        block = shard if step == 0 else block_from(step, y)
+        return send(block, block_from(step, y), (y_sent, y_got), step, other_y)
+
+    def to_core(step, at_y, slot):
+        block = block_from(step, at_y)
+        source = shard if step == 0 and slot == 0 else block
+        return send(source, block, (c_sent, c_got), 2 * step + slot, other_core)
+
+    along_y = [to_y(step) for step in range(depth)]
+    across = [[to_core(step, y, 0), to_core(step, 1 - y, 1)] for step in range(depth)]
+    for copy in along_z:
+        copy.start()
+    along_y[0].start()
+    across[0][0].start()
+    for copy in along_x:
+        copy.start()
+    for step in range(1, depth):
+        along_z[step - 1].wait_recv()
+        along_y[step].start()
+        across[step][0].start()
+    for step in range(depth):
+        along_y[step].wait_recv()
+        across[step][1].start()
+    for copy in along_x:
+        copy.wait()
+    for copy in along_z + along_y:
+        copy.wait_send()
+    for pair in across:
+        for copy in pair:
+            copy.wait()
+    for copy in own:
+        copy.wait()
+
+
+def gather_attn(shard, normed, cot):
+    depth, parts = lax.axis_size("dp") // 4, lax.axis_size("mp")
+    size = depth * 4
+    return pl.pallas_call(
+        functools.partial(gather_kernel, depth, parts),
+        out_shape=(
+            jax.ShapeDtypeStruct((size,) + shard.shape, shard.dtype),
+            jax.ShapeDtypeStruct((parts,) + normed.shape, normed.dtype),
+            jax.ShapeDtypeStruct((parts,) + cot.shape, cot.dtype),
+        ),
+        in_specs=[ANY_SPEC] * 3,
+        out_specs=(ANY_SPEC,) * 3,
+        scratch_shapes=[DMA((depth - 1,))] * 2 + [DMA((depth,))] * 2 + [DMA((2 * depth,))] * 2
+        + [DMA((2 * (parts - 1),))] * 2 + [DMA((3,))],
+        compiler_params=pltpu.CompilerParams(collective_id=0, has_side_effects=True),
+        name="gather_attn",
+    )(shard, normed, cot)
+
+
+def add_rows(target, sources):
+    def body(i, carry):
+        here = pl.ds(pl.multiple_of(i * 16, 16), 16)
+        total = sources[0][here, :].astype(F32)
+        for source in sources[1:]:
+            total = total + source[here, :].astype(F32)
+        target[here, :] = total.astype(target.dtype)
+        return carry
+
+    lax.fori_loop(0, target.shape[0] // 16, body, 0)
+
+
+class Sums:
+    CORE_AHEAD = 3
+    Y_AHEAD = 3
+
+    def __init__(self, depth, parts, pieces, wholes, outs, scratch):
+        self.depth, self.parts, self.wholes, self.outs = depth, parts, wholes, outs
+        count = len(wholes)
+        self.mine, self.core_in, self.y_in, self.z_in = (
+            scratch[i * count : (i + 1) * count] for i in range(4)
+        )
+        self.sems = scratch[4 * count :]
+        self.order = [
+            (step, k, piece)
+            for step in range(1, depth + 1)
+            for k in range(count)
+            for piece in range(pieces)
+        ]
+        self.pieces = pieces
+        self.where = place(depth, parts)
+        self.items = [self.parts_of(n) for n in range(len(self.order))]
+
+    @staticmethod
+    def scratch(depth, pieces, wholes):
+        kinds = ((depth, 2), (depth, 2), (depth,), (depth - 1,))
+        buffers = [
+            pltpu.VMEM(lead + whole.shape[3:], BF16) for lead in kinds for whole in wholes
+        ]
+        count = depth * len(wholes) * pieces
+        return buffers + [DMA((count,))] * 7
+
+    def parts_of(self, n):
+        step, k, piece = self.order[n]
+        me, part, z, y, core, dp_of, mp_of = self.where
+        at = lax.rem(z + step, self.depth)
+        kept, c_sent, c_got, y_sent, y_got, z_sent, z_got = self.sems
+        whole, mine = self.wholes[k], self.mine[k]
+        width = mine.shape[3] // self.pieces
+        cols = pl.ds(piece * width, width)
+        own = pltpu.make_async_copy(
+            whole.at[at, :, core, :, cols], mine.at[at, :, :, cols], kept.at[n]
+        )
+        across = send(
+            whole.at[at, :, 1 - core, :, cols], self.core_in[k].at[at, :, :, cols],
+            (c_sent, c_got), n, (dp_of(0, y, 1 - core), part),
+        )
+        along_y = send(
+            mine.at[at, 1 - y, :, cols], self.y_in[k].at[at, :, cols], (y_sent, y_got), n,
+            (dp_of(0, 1 - y, core), part),
+        )
+        along_z = None
+        if step < self.depth:
+            along_z = send(
+                mine.at[at, y, :, cols], self.z_in[k].at[step - 1, :, cols], (z_sent, z_got), n,
+                (dp_of(step, y, core), part),
+            )
+        return at, k, cols, own, across, along_y, along_z
+
+    def begin(self):
+        for n in range(min(self.CORE_AHEAD, len(self.items))):
+            self.load(n)
+
+    def load(self, n):
+        self.items[n][3].start()
+        self.items[n][4].start()
+
+    def cross(self, n):
+        at, k, cols, own, across, along_y, along_z = self.items[n]
+        own.wait()
+        across.wait_recv()
+        if n + self.CORE_AHEAD < len(self.items):
+            self.load(n + self.CORE_AHEAD)
+        for at_y in range(2):
+            mine = self.mine[k].at[at, at_y, :, cols]
+            add_rows(mine, (mine, self.core_in[k].at[at, at_y, :, cols]))
+        along_y.start()
+
+    def onward(self, n):
+        y = self.where[3]
+        at, k, cols, own, across, along_y, along_z = self.items[n]
+        along_y.wait_recv()
+        mine = self.mine[k].at[at, y, :, cols]
+        add_rows(mine, (mine, self.y_in[k].at[at, :, cols]))
+        if along_z is not None:
+            along_z.start()
+
+    def advance(self, n):
+        if n < len(self.items):
+            self.cross(n)
+        if n >= self.Y_AHEAD:
+            self.onward(n - self.Y_AHEAD)
+
+    def steps(self):
+        return len(self.items) + self.Y_AHEAD
+
+    def end(self):
+        z, y = self.where[2:4]
+        for at, k, cols, own, across, along_y, along_z in self.items:
+            if along_z is not None:
+                along_z.wait_recv()
+        for k, out in enumerate(self.outs):
+            add_rows(
+                out, [self.mine[k].at[z, y]] + [self.z_in[k].at[i] for i in range(self.depth - 1)]
+            )
+        for at, k, cols, own, across, along_y, along_z in self.items:
+            across.wait_send()
+            along_y.wait_send()
+            if along_z is not None:
+                along_z.wait_send()
+
+
+def pieces_of(width, wanted):
+    return wanted if width % (128 * wanted) == 0 else 1
+
+
+def norm_back(rows_in, gain, gradient):
+    factor = lax.rsqrt(jnp.mean(rows_in * rows_in, axis=-1, keepdims=True) + EPSILON)
+    normed = rows_in * factor
+    scaled = gradient * gain
+    back = factor * (scaled - normed * jnp.mean(scaled * normed, axis=-1, keepdims=True))
+    return back, gradient * normed
+
+
+TILE = 16
+
+
+def fold(terms):
+    total = terms[0:8]
+    for at in range(8, terms.shape[0], 8):
+        total = total + terms[at : at + 8]
+    return total
+
+
+def sum_mlp_kernel(depth, parts, *refs):
+    (gate, up, down, own_two, give_two, own_out, give_out, residual, cot, gain,
+     gate_out, up_out, down_out, block_out, grad_residual, branch_all, gain_grad,
+     in_two, in_out, branch, two_sent, two_got, out_sent, out_got, b_sent, b_got, kept) = refs[:27]
+    me, part, z, y, core, dp_of, mp_of = place(depth, parts)
+    rows = own_two.shape[0]
+    sums = Sums(depth, parts, 1, (gate, up, down), (gate_out, up_out, down_out), refs[27:])
+    greet(depth, parts)
+
+    def along_x(source, target, sems):
+        return [
+            send(source(step), target(step), sems, step - 1, (me, mp_of(step)))
+            for step in range(1, parts)
+        ]
+
+    to_two = along_x(
+        lambda s: give_two.at[s - 1], lambda s: in_two.at[s - 1], (two_sent, two_got)
+    )
+    to_out = along_x(
+        lambda s: give_out.at[s - 1], lambda s: in_out.at[s - 1], (out_sent, out_got)
+    )
+    to_branch = along_x(lambda s: branch, lambda s: branch_all.at[part], (b_sent, b_got))
+    for copy in to_two:
+        copy.start()
+    sums.begin()
+    at = 0
+    while at < sums.Y_AHEAD:
+        sums.advance(at)
+        at += 1
+    for copy in to_two:
+        copy.wait_recv()
+    gain_grad[...] = jnp.zeros_like(gain_grad)
+
+    def body(i, carry):
+        here = pl.ds(pl.multiple_of(i * TILE, TILE), TILE)
+        total = own_two[here, :]
+        for step in range(parts - 1):
+            total = total + in_two[step, here, :].astype(F32)
+        back, terms = norm_back(residual[here, :], gain[...], total)
+        gain_grad[...] += fold(terms)
+        result = cot[here, :].astype(F32) + back
+        grad_residual[here, :] = result
+        branch[here, :] = result.astype(BF16)
+        return carry
+
+    lax.fori_loop(0, rows // TILE, body, 0)
+    mine = pltpu.make_async_copy(branch, branch_all.at[part], kept.at[0])
+    mine.start()
+    for copy in to_branch + to_out:
+        copy.start()
+    while at < sums.steps():
+        sums.advance(at)
+        at += 1
+    for copy in to_out:
+        copy.wait_recv()
+
+    def finish(i, carry):
+        here = pl.ds(pl.multiple_of(i * TILE, TILE), TILE)
+        total = own_out[here, :]
+        for step in range(parts - 1):
+            total = total + in_out[step, here, :].astype(F32)
+        block_out[here, :] = (residual[here, :] + total).astype(BF16)
+        return carry
+
+    lax.fori_loop(0, rows // TILE, finish, 0)
+    sums.end()
+    mine.wait()
+    for copy in to_branch:
+        copy.wait()
+    for copy in to_two + to_out:
+        copy.wait_send()
+
+
+def sum_mlp(grads, own_two, give_two, own_out, give_out, residual, cot, gain):
+    depth, parts = lax.axis_size("dp") // 4, lax.axis_size("mp")
+    rows, width = residual.shape
+    wholes = [grad.reshape(depth, 2, 2, grad.shape[0] // (4 * depth), -1) for grad in grads]
+    return pl.pallas_call(
+        functools.partial(sum_mlp_kernel, depth, parts),
+        out_shape=[jax.ShapeDtypeStruct(whole.shape[3:], F32) for whole in wholes]
+        + [
+            jax.ShapeDtypeStruct((rows, width), BF16),
+            jax.ShapeDtypeStruct((rows, width), F32),
+            jax.ShapeDtypeStruct((parts, rows, width), BF16),
+            jax.ShapeDtypeStruct((8, width), F32),
+        ],
+        in_specs=[ANY_SPEC] * 3 + [VMEM_SPEC, ANY_SPEC, VMEM_SPEC, ANY_SPEC] + [VMEM_SPEC] * 3,
+        out_specs=[VMEM_SPEC] * 5 + [ANY_SPEC, VMEM_SPEC],
+        scratch_shapes=[pltpu.VMEM((parts - 1, rows, width), BF16)] * 2
+        + [pltpu.VMEM((rows, width), BF16)]
+        + [DMA((parts - 1,))] * 6 + [DMA((1,))]
+        + Sums.scratch(depth, 1, wholes),
+        compiler_params=pltpu.CompilerParams(
+            collective_id=1, has_side_effects=True, vmem_limit_bytes=56 * 2**20
+        ),
+        name="sum_mlp",
+    )(*wholes, own_two, give_two, own_out, give_out, residual, cot, gain)
+
+
+def sum_attn_kernel(depth, parts, *refs):
+    (grad, own_one, give_one, tokens, grad_residual, gain, gain_two_grad,
+     grad_out, grad_tokens, gains,
+     in_one, held, around, one_sent, one_got, g_sent, g_got) = refs[:17]
+    me, part, z, y, core, dp_of, mp_of = place(depth, parts)
+    rows = own_one.shape[0]
+    pieces = pieces_of(grad.shape[4], 3)
+    sums = Sums(depth, parts, pieces, (grad,), (grad_out,), refs[17:])
+    greet(depth, parts)
+    to_one = [
+        send(give_one.at[step - 1], in_one.at[step - 1], (one_sent, one_got), step - 1,
+             (me, mp_of(step)))
+        for step in range(1, parts)
+    ]
+    for copy in to_one:
+        copy.start()
+    sums.begin()
+    at = 0
+    while at < sums.Y_AHEAD:
+        sums.advance(at)
+        at += 1
+    for copy in to_one:
+        copy.wait_recv()
+    held[0:8] = jnp.zeros((8, held.shape[1]), F32)
+    held[8:16] = gain_two_grad[...]
+
+    def body(i, carry):
+        here = pl.ds(pl.multiple_of(i * TILE, TILE), TILE)
+        total = own_one[here, :]
+        for step in range(parts - 1):
+            total = total + in_one[step, here, :].astype(F32)
+        back, terms = norm_back(tokens[here, :].astype(F32), gain[...], total)
+        held[0:8] += fold(terms)
+        grad_tokens[here, :] = (grad_residual[here, :] + back).astype(BF16)
+        return carry
+
+    lax.fori_loop(0, rows // TILE, body, 0)
+    stages = [
+        [(dp_of(0, y, 1 - core), part)],
+        [(me, mp_of(step)) for step in range(1, parts)],
+        [(dp_of(step, y, core), part) for step in range(1, depth)],
+        [(dp_of(0, 1 - y, core), part)],
+    ]
+    levels, slot = [], 0
+    for number, stage in enumerate(stages):
+        copies = []
+        for device in stage:
+            landing = around.at[pl.ds(16 * slot, 16)]
+            copies.append(
+                (send(held.at[pl.ds(16 * number, 16)], landing, (g_sent, g_got), slot, device),
+                 landing)
+            )
+            slot += 1
+        levels.append(copies)
+
+    def begin_level(number):
+        for copy, landing in levels[number]:
+            copy.start()
+
+    def end_level(number):
+        total = held[16 * number : 16 * number + 16]
+        for copy, landing in levels[number]:
+            copy.wait_recv()
+            total = total + landing[...]
+        held[16 * (number + 1) : 16 * (number + 2)] = total
+
+    number = 0
+    begin_level(0)
+    while at < sums.steps():
+        sums.advance(at)
+        at += 1
+        if number < len(levels):
+            end_level(number)
+            number += 1
+            if number < len(levels):
+                begin_level(number)
+    while number < len(levels):
+        end_level(number)
+        number += 1
+        if number < len(levels):
+            begin_level(number)
+    gains[...] = held[64:80]
+    sums.end()
+    for copy in to_one + [copy for copies in levels for copy, landing in copies]:
+        copy.wait_send()
+
+
+def sum_attn(grad, own_one, give_one, tokens, grad_residual, gain, gain_two_grad):
+    depth, parts = lax.axis_size("dp") // 4, lax.axis_size("mp")
+    rows, width = tokens.shape
+    whole = grad.reshape(depth, 2, 2, grad.shape[0] // (4 * depth), -1)
+    stops = depth + parts
+    return pl.pallas_call(
+        functools.partial(sum_attn_kernel, depth, parts),
+        out_shape=[
+            jax.ShapeDtypeStruct(whole.shape[3:], F32),
+            jax.ShapeDtypeStruct((rows, width), BF16),
+            jax.ShapeDtypeStruct((16, width), F32),
+        ],
+        in_specs=[ANY_SPEC, VMEM_SPEC, ANY_SPEC] + [VMEM_SPEC] * 4,
+        out_specs=[VMEM_SPEC] * 3,
+        scratch_shapes=[
+            pltpu.VMEM((parts - 1, rows, width), BF16),
+            pltpu.VMEM((80, width), F32),
+            pltpu.VMEM((16 * stops, width), F32),
+        ]
+        + [DMA((parts - 1,))] * 2 + [DMA((stops,))] * 2
+        + Sums.scratch(depth, pieces_of(whole.shape[4], 3), [whole]),
+        compiler_params=pltpu.CompilerParams(
+            collective_id=2, has_side_effects=True, vmem_limit_bytes=56 * 2**20
+        ),
+        name="sum_attn",
+    )(whole, own_one, give_one, tokens, grad_residual, gain, gain_two_grad)
+
+
+def own_and_give(whole, parts):
+    me = lax.axis_index("mp")
+    rows = whole.shape[0] // parts
+    own = lax.dynamic_slice_in_dim(whole, me * rows, rows, 0)
+    give = [
+        lax.dynamic_slice_in_dim(whole, lax.rem(me + step, parts) * rows, rows, 0).astype(BF16)
+        for step in range(1, parts)
+    ]
+    return own, jnp.stack(give)
 
 
 def shards(
@@ -114,21 +600,22 @@
     members = heads // kv_heads
     factor = HEAD_SIZE ** (-0.5)
 
-    attn_w = lax.all_gather(
-        jnp.concatenate([w_query, key_weight, value_weight, w_out.T], axis=1),
-        "dp", axis=0, tiled=True,
-    )
     mlp_w = lax.all_gather(
         jnp.concatenate([w_gate, w_up, w_down.T], axis=1), "dp", axis=0, tiled=True
     )
+    inputs = tokens.astype(F32)
+    gain_one, gain_two = norm_attn.astype(F32), norm_mlp.astype(F32)
+    attn_w, normed_one, grad_rows = gather_attn(
+        jnp.concatenate([w_query, key_weight, value_weight, w_out.T], axis=1),
+        (rms_parts(inputs)[1] * gain_one).astype(BF16),
+        cotangent,
+    )
+    width = tokens.shape[1]
+    attn_w = attn_w.reshape(width, -1)
+    normed_one, grad_rows = normed_one.reshape(group, width), grad_rows.reshape(group, width)
     cuts = (q_width, q_width + kv_width, q_width + 2 * kv_width)
     query_w, key_w, value_w, out_wt = jnp.split(attn_w, cuts, axis=1)
     gate_w, up_w, down_wt = jnp.split(mlp_w, 3, axis=1)
-
-    inputs = tokens.astype(F32)
-    gain_one, gain_two = norm_attn.astype(F32), norm_mlp.astype(F32)
-    normed_one = mp_gather((rms_parts(inputs)[1] * gain_one).astype(BF16), parts)
-    grad_rows = mp_gather(cotangent, parts)
 
     segment, position = layout(seq_lengths[0], group)
     cosine, sine = rotation(position)
@@ -168,21 +655,22 @@
         BF16
     )
     grad_up = (grad_hidden * swish).astype(BF16)
-    grad_mlp = jnp.concatenate(
-        [
-            outer_sum(normed_two, grad_gate).astype(BF16),
-            outer_sum(normed_two, grad_up).astype(BF16),
-            outer_sum(grad_rows, hidden).astype(BF16),
-        ],
-        axis=1,
-    )
-    grad_mlp = lax.psum_scatter(grad_mlp, "dp", scatter_dimension=0, tiled=True)
-    grad_two = mp_sum_rows(mul_t(grad_gate, gate_w) + mul_t(grad_up, up_w), parts)
-    block_out = (residual + mp_sum_rows(branch, parts)).astype(BF16)
-
-    from_two, gain_two_grad = rms_back(residual, gain_two, grad_two)
-    grad_residual = cotangent.astype(F32) + from_two
-    grad_branch = mp_gather(grad_residual.astype(BF16), parts)
+    grads_mlp = (
+        outer_sum(normed_two, grad_gate).astype(BF16),
+        outer_sum(normed_two, grad_up).astype(BF16),
+        outer_sum(grad_rows, hidden).astype(BF16),
+    )
+    (grad_gate_w, grad_up_w, grad_down_w, block_out, grad_residual, grad_branch, gain_two_grad) = (
+        sum_mlp(
+            grads_mlp,
+            *own_and_give(mul_t(grad_gate, gate_w) + mul_t(grad_up, up_w), parts),
+            *own_and_give(branch, parts),
+            residual,
+            cotangent,
+            gain_two[None, :],
+        )
+    )
+    grad_branch = grad_branch.reshape(group, width)
     grad_attended = (
         mul(grad_branch, out_wt).astype(BF16).reshape(group, kv_heads, members, HEAD_SIZE)
     )
@@ -207,16 +695,18 @@
         ],
         axis=1,
     )
-    grad_attn = lax.psum_scatter(grad_attn, "dp", scatter_dimension=0, tiled=True)
-    grad_one = mp_sum_rows(
-        mul_t(grad_query, query_w) + mul_t(grad_key, key_w) + mul_t(grad_value, value_w), parts
-    )
-    from_one, gain_one_grad = rms_back(inputs, gain_one, grad_one)
-    grad_tokens = (grad_residual + from_one).astype(BF16)
-    gains = lax.psum(jnp.stack([gain_one_grad, gain_two_grad]), ("dp", "mp"))
-
-    attn_parts = jnp.split(grad_attn.astype(F32), cuts, axis=1)
-    mlp_parts = jnp.split(grad_mlp.astype(F32), 3, axis=1)
+    grad_attn, grad_tokens, gains = sum_attn(
+        grad_attn,
+        *own_and_give(
+            mul_t(grad_query, query_w) + mul_t(grad_key, key_w) + mul_t(grad_value, value_w), parts
+        ),
+        tokens,
+        grad_residual,
+        gain_one[None, :],
+        gain_two_grad,
+    )
+    attn_parts = jnp.split(grad_attn, cuts, axis=1)
+    gains = jnp.sum(gains.reshape(2, 8, width), axis=1)
     return (
         block_out,
         grad_tokens,
@@ -226,9 +716,9 @@
         attn_parts[2],
         attn_parts[3].T,
         gains[1],
-        mlp_parts[0],
-        mlp_parts[1],
-        mlp_parts[2].T,
+        grad_gate_w,
+        grad_up_w,
+        grad_down_w.T,
     )
 
 

time: 614 us -> 530 us (0.86)
  waiting for transfers between devices: 362 us -> 37.2 us
  Pallas kernels: 0 us -> 310 us
  blocking collectives: 42.6 us -> 0 us
  other arithmetic: 44.3 us -> 16.6 us
  local copies, waits for them, and re-layouts: 35.9 us -> 43.1 us
  starting transfers between devices: 6.68 us -> 0.4 us
    pallas_call x0 -> x3, Pallas kernels: none -> 310 us  [the longest x1 158 us: sum_mlp(): pl.pallas_call(functools.partial(sum_mlp_kernel, depth, parts), out_shape...]
    reduce_scatter x1 -> x0, waiting for transfers between devices: 178 us -> none  [shards(): grad_mlp = lax.psum_scatter(grad_mlp, 'dp', scatter_dimension=0, tiled=True)]
    ppermute x8 -> x2, waiting for transfers between devices: 121 us -> 37.1 us  [mp_shift(): lax.ppermute(block, 'mp', [(i, (i + step) % parts) for i in range(parts)])]
    all_gather x1 -> x0, waiting for transfers between devices: 45.6 us -> none  [shards(): lax.all_gather(jnp.concatenate([w_query, key_weight, value_weight, w_out....]
    psum x1 -> x0, blocking collectives: 42.6 us -> none  [shards(): gains = lax.psum(jnp.stack([gain_one_grad, gain_two_grad]), ('dp', 'mp'))]
    all_gather x1, waiting for transfers between devices: 17.8 us -> 0.02 us  [shards(): lax.all_gather(jnp.concatenate([w_gate, w_up, w_down.T], axis=1), 'dp', a...]
    concatenate x3 -> x0, other arithmetic: 16.4 us -> none  [the longest x1 16.4 us: shards(): jnp.concatenate([outer_sum(normed_two, grad_gate).astype(BF16), outer_sum...]
    unnamed x84 -> x85, local copies, waits for them, and re-layouts: 24.8 us -> 10.7 us
  transfers between devices with their start and end apart: 12 -> 3, of which waited for: 11 -> 2; matrix products, arithmetic and copies ran while one was open for 16% -> 7% of each run, Pallas kernels for 0% -> 14%
where the time goes in v2:
time: 530 us; the launch traced here: 519 us
  Pallas kernels  310 us (58%)
  matrix products  95.1 us (18%)
  local copies, waits for them, and re-layouts  43.1 us (8%)
  waiting for transfers between devices  37.2 us (7%)
  between operations  17 us (3%)
  other arithmetic  16.6 us (3%)
    pallas_call x1, Pallas kernels, sum_mlp(): pl.pallas_call(functools.partial(sum_mlp_kernel, depth, parts), out_shape...  158 us
    pallas_call x1, Pallas kernels, sum_attn(): pl.pallas_call(functools.partial(sum_attn_kernel, depth, parts), out_shap...  78.4 us
    pallas_call x1, Pallas kernels, gather_attn(): pl.pallas_call(functools.partial(gather_kernel, depth, parts), out_shape=...  73.8 us
    ppermute x2, waiting for transfers between devices, mp_shift(): lax.ppermute(block, 'mp', [(i, (i + step) % parts) for i in range(parts)])  37.1 us
    dot_general x7, matrix products, mul(): return jnp.dot(left, right, preferred_element_type=F32)  33.9 us
    dot_general x7, matrix products, outer_sum(): lax.dot_general(left, right, (((0,), (0,)), ((), ())), preferred_element_...  20.8 us
    dot_general x7, matrix products, mul_t(): lax.dot_general(left, right, (((1,), (1,)), ((), ())), preferred_element_...  18.6 us
    unnamed x85, local copies, waits for them, and re-layouts  10.7 us
  transfers between devices with their start and end apart: 3, of which 2 were waited for; matrix products, arithmetic and copies ran while one was open for 7% of the time, Pallas kernels for 14%

profile of v2, /device:TPU:10, one launch (start us, length us, event | category | flops | bytes accessed | tf_op | source)
XLA Modules:
  0.0 519.4 jit_solution(15459892592390012148)
XLA Ops:
  7.3 2.4 pad_maximum_fusion.1
  10.8 1.1 fusion.36.normed
  12.0 73.8 %gather_attn.1 = (bf16[16,96,2304]{2,1,0:T(8,128)(2,1)}, bf16[2,256,1536]{2,1,0:T(8,128)(2,1)}, bf16[2,256,1536]{2,1,0:T(8,128)(2,1)}) custom-call(bf16[96,2304]{1,0:T(8,128)(2,1)} %pad_maximum_fusion.3.shard, bf16[256,1536]{1,0:T(8,128)(2,1)} %fusion.36.normed, bf16[256,1536]{1,0:T(8,128)(2,1)} %refs_8_.1), custom_call_target="tpu_custom_call" | custom-call | tf_op jit(solution)/shard_map/gather_attn/pallas_call | solution.py:196
  85.8 1.5 slice_bitcast_fusion.1
  87.3 1.5 copy.32
  88.8 2.0 slice_bitcast_fusion
  90.7 2.4 copy.33
  97.8 2.8 fusion.75
  100.9 1.4 fusion.76
  102.6 2.4 convolution_convert_fusion.7
  105.0 5.4 %fusion.74 = (f32[4,2,512]{2,1,0:T(2,128)S(1)}, f32[4,2,512,512]{2,3,1,0:T(8,128)}) fusion(pred[512,512]{0,1:T(8,128)(4,1)S(1)} %fusion.52, bf16[512,4,2,48]{0,3,2,1:T(8,128)(2,1)S(1)} %bitcast.154, bf16[512,4,2,48]{0,3,2,1:T(8,128)(2,1)S(1)} %bitcast.152, bf16[512,4,48]{0,2,1:T(8,128)(2,1)S(1)} %get-tuple-element.53, ...), kind=kOutput, calls=%fused_computation.130 | convolution fusion | flops 413401600 | bytes 9846784 | tf_op jit(solution)/shard_map/sub | solution.py:637
  110.5 4.4 fusion.40
  115.7 3.1 fusion.30
  118.9 1.7 copy-done.3
  120.7 19.6 %collective-permute-done = bf16[256,1536]{1,0:T(8,128)(2,1)S(1)} collective-permute-done((bf16[256,1536]{1,0:T(8,128)(2,1)S(1)}, bf16[256,1536]{1,0:T(8,128)(2,1)S(1)}, u32[]{:S(2)}, u32[]{:S(2)}) %collective-permute-start) | collective-permute-done | bytes 786464 | tf_op jit(solution)/shard_map/ppermute | solution.py:64
  140.4 1.8 multiply_reduce_fusion
  144.9 17.5 %collective-permute-done.1 = bf16[256,1536]{1,0:T(8,128)(2,1)S(1)} collective-permute-done((bf16[256,1536]{1,0:T(8,128)(2,1)S(1)}, bf16[256,1536]{1,0:T(8,128)(2,1)S(1)}, u32[]{:S(2)}, u32[]{:S(2)}) %collective-permute-start.1) | collective-permute-done | bytes 786464 | tf_op jit(solution)/shard_map/ppermute | solution.py:64
  162.5 9.0 %fusion.15 = f32[512,2048]{1,0:T(8,128)} fusion(bf16[512,1536]{1,0:T(8,128)(2,1)} %bitcast.174, bf16[1536,6144]{1,0:T(8,128)(2,1)} %all-gather.2.cloned.1.call-done), kind=kOutput, calls=%fused_computation.23 | convolution fusion | flops 3221225472 | bytes 12058624 | tf_op jit(solution)/shard_map/dot_general | solution.py:52
  171.4 1.2 copy-done.24
  172.6 5.2 fusion.7
  177.8 8.6 %multiply_convert_fusion = (bf16[512,2048]{1,0:T(8,128)(2,1)S(1)}, bf16[512,2048]{1,0:T(8,128)(2,1)S(1)}, bf16[512,2048]{1,0:T(8,128)(2,1)}) fusion(f32[512,2048]{1,0:T(8,128)} %fusion.7, f32[512,2048]{1,0:T(8,128)} %fusion.15, bf16[512,1536]{1,0:T(8,128)(2,1)S(1)} %constant_dynamic-update-slice_fusion, bf16[1536,6144]{1,0:T(8,128)(2,1)S(1)} %copy-done.24), kind=kOutput, calls=%fused_computation.25 | convolution fusion | flops 3236954112 | bytes 22544384 | tf_op jit(solution)/shard_map/dot_general | solution.py:52
  186.4 3.5 fusion.13
  190.8 1.3 constant_dynamic-slice_fusion.1.refs_5_
  192.2 5.8 %convolution_convert_fusion = bf16[1536,2048]{1,0:T(8,128)(2,1)} fusion(bf16[512,1536]{1,0:T(8,128)(2,1)S(1)} %bitcast.175, bf16[512,2048]{1,0:T(8,128)(2,1)S(1)} %get-tuple-element.43), kind=kOutput, calls=%fused_computation.8 | convolution fusion | flops 3224371200 | bytes 9961472 | tf_op jit(solution)/shard_map/dot_general | solution.py:60
  198.0 3.5 fusion.5
  201.4 5.1 fusion.21
  207.5 1.2 constant_dynamic-slice_fusion.2.refs_3_
  208.7 5.4 %convolution_convert_fusion.1 = bf16[1536,2048]{1,0:T(8,128)(2,1)} fusion(bf16[512,1536]{1,0:T(8,128)(2,1)S(1)} %constant_dynamic-update-slice_fusion, bf16[512,2048]{1,0:T(8,128)(2,1)S(1)} %copy-done.35), kind=kOutput, calls=%fused_computation.9 | convolution fusion | flops 3224371200 | bytes 9961472 | tf_op jit(solution)/shard_map/dot_general | solution.py:60
  214.1 5.4 %convolution_convert_fusion.2 = bf16[1536,2048]{1,0:T(8,128)(2,1)} fusion(bf16[512,1536]{1,0:T(8,128)(2,1)S(1)} %constant_dynamic-update-slice_fusion, bf16[512,2048]{1,0:T(8,128)(2,1)S(1)} %copy-done.34), kind=kOutput, calls=%fused_computation.10 | convolution fusion | flops 3224371200 | bytes 9961472 | tf_op jit(solution)/shard_map/dot_general | solution.py:60
  219.5 157.8 %sum_mlp.1 = (f32[96,2048]{1,0:T(8,128)}, f32[96,2048]{1,0:T(8,128)}, f32[96,2048]{1,0:T(8,128)}, bf16[256,1536]{1,0:T(8,128)(2,1)}, f32[256,1536]{1,0:T(8,128)}...) custom-call(bf16[4,2,2,96,2048]{4,3,2,1,0:T(8,128)(2,1)} %bitcast.140, bf16[4,2,2,96,2048]{4,3,2,1,0:T(8,128)(2,1)} %bitcast.139, ...), custom_call_target="tpu_custom_call" | custom-call | tf_op jit(solution)/shard_map/sum_mlp/pallas_call | solution.py:433
  377.3 4.6 fusion.37
  381.8 1.4 convolution_convert_fusion.3
  383.2 1.4 copy.35
  384.7 5.0 fusion.48
  389.7 4.9 fusion.1
  394.6 2.6 fusion.3
  397.2 1.4 fusion.47
  399.8 1.4 copy-done.26
  401.2 1.4 convolution_convert_fusion.4
  402.6 1.4 fusion.32
  405.8 1.0 convolution_add_fusion.1
  406.9 1.0 convolution_add_fusion
  408.9 1.3 constant_dynamic-slice_fusion.refs_1_
  410.2 3.6 pad_maximum_fusion
  413.8 10.3 %copy.39 = bf16[1536,2304]{1,0:T(8,128)(2,1)} copy(bf16[1536,2304]{0,1:T(8,128)(2,1)} %pad_maximum_fusion) | data formatting | bytes 14155776 | tf_op jit(solution)/shard_map/concatenate | solution.py:689
  424.1 78.4 %sum_attn.1 = (f32[96,2304]{1,0:T(8,128)}, bf16[256,1536]{1,0:T(8,128)(2,1)}, f32[16,1536]{1,0:T(8,128)}) custom-call(bf16[4,2,2,96,2304]{4,3,2,1,0:T(8,128)(2,1)} %bitcast.134, f32[256,1536]{1,0:T(8,128)} %constant_dynamic-slice_fusion.refs_1_, bf16[1,256,1536]{2,1,0:T(8,128)(2,1)} %fusion.61.refs_2_, bf16[256,1536]{1,0:T(8,128)(2,1)} %refs_3_.1, ...), custom_call_target="tpu_custom_call" | custom-call | tf_op jit(solution)/shard_map/sum_attn/pallas_call | solution.py:547
  502.5 1.8 fusion.72
  504.3 2.0 slice_bitcast_fusion.2
  (121 shorter events, 19.8 us)
Async XLA Ops:
  7.2 2.6 copy-start.19
  7.2 2.6 copy-start.1
  7.2 2.8 copy-start.15
  7.2 2.8 copy-start.17
  7.2 2.8 copy-start.18
  7.2 2.8 copy-start.16
  7.2 155.2 %all-gather.2.cloned.1.call-start = ((), (), s32[]{:S(2)}) async-start(), calls=%async_computation | async-start | bytes 20054016 | tf_op jit(solution)/shard_map/all_gather | solution.py:603
  90.7 2.5 copy-start.23
  97.8 3.0 copy-start.2
  97.8 3.1 copy-start.25
  100.7 4.3 copy-start.8
  102.6 7.9 %copy-start.4 = (bf16[512,8,48]{0,2,1:T(8,128)(2,1)}, bf16[512,8,48]{0,2,1:T(8,128)(2,1)S(1)}, u32[]{:S(2)}) copy-start(bf16[512,8,48]{0,2,1:T(8,128)(2,1)S(1)} %get-tuple-element.48) | copy-start | bytes 1179652
  102.6 7.9 %copy-start.6 = (bf16[512,8,48]{0,2,1:T(8,128)(2,1)}, bf16[512,8,48]{0,2,1:T(8,128)(2,1)S(1)}, u32[]{:S(2)}) copy-start(bf16[512,8,48]{0,2,1:T(8,128)(2,1)S(1)} %get-tuple-element.49) | copy-start | bytes 1179652
  105.0 5.4 %copy-start.31 = (bf16[512,384]{0,1:T(8,128)(2,1)}, bf16[512,384]{0,1:T(8,128)(2,1)S(1)}, u32[]{:S(2)}) copy-start(bf16[512,384]{0,1:T(8,128)(2,1)S(1)} %convolution_convert_fusion.7) | copy-start | bytes 1179652
  114.9 0.9 copy-start.29
  115.7 5.0 copy-start.21
  118.9 1.7 copy-start.3
  120.6 19.8 %collective-permute-start = (bf16[256,1536]{1,0:T(8,128)(2,1)S(1)}, bf16[256,1536]{1,0:T(8,128)(2,1)S(1)}, u32[]{:S(2)}, u32[]{:S(2)}) collective-permute-start(bf16[256,1536]{1,0:T(8,128)(2,1)S(1)} %dynamic-slice_convert_fusion.3), channel_id=1, source_target_pairs={{0,1},{1,0},{2,3},{3,2},{4,5},{5,4},{6,7},{7,6},{8,9},{9,8},{10,11... | collective-permute-start | bytes 2359304 | tf_op jit(solution)/shard_map/ppermute | solution.py:64
  142.2 1.2 copy-start
  142.2 1.5 copy-start.20
  142.2 2.1 copy-start.22
  143.4 19.0 %collective-permute-start.1 = (bf16[256,1536]{1,0:T(8,128)(2,1)S(1)}, bf16[256,1536]{1,0:T(8,128)(2,1)S(1)}, u32[]{:S(2)}, u32[]{:S(2)}) collective-permute-start(bf16[256,1536]{1,0:T(8,128)(2,1)S(1)} %get-tuple-element.40), channel_id=1, source_target_pairs={{0,1},{1,0},{2,3},{3,2},{4,5},{5,4},{6,7},{7,6},{8,9},{9,8},{10,11... | collective-permute-start | bytes 2359304 | tf_op jit(solution)/shard_map/ppermute | solution.py:64
  162.5 10.2 %copy-start.24 = (bf16[1536,6144]{1,0:T(8,128)(2,1)S(1)}, bf16[1536,6144]{1,0:T(8,128)(2,1)}, u32[]{:S(2)}) copy-start(bf16[1536,6144]{1,0:T(8,128)(2,1)} %all-gather.2.cloned.1.call-done) | copy-start | bytes 56623108
  186.4 11.6 %copy-start.33 = (bf16[512,2048]{1,0:T(8,128)(2,1)}, bf16[512,2048]{1,0:T(8,128)(2,1)S(1)}, u32[]{:S(2)}) copy-start(bf16[512,2048]{1,0:T(8,128)(2,1)S(1)} %get-tuple-element.44) | copy-start | bytes 6291460
  189.8 2.3 copy-start.27
  206.5 2.2 copy-start.35
  208.7 5.4 %copy-start.34 = (bf16[512,2048]{1,0:T(8,128)(2,1)S(1)}, bf16[512,2048]{1,0:T(8,128)(2,1)}, u32[]{:S(2)}) copy-start(bf16[512,2048]{1,0:T(8,128)(2,1)} %copy-done.33) | copy-start | bytes 6291460
  377.3 4.6 copy-start.28
  377.3 4.6 copy-start.30
  384.6 5.0 copy-start.32
  384.7 9.9 %slice-start = ((s8[8388608]{0:T(1024)(128)(4,1)}), s8[4194304]{0:T(1024)(128)(4,1)S(1)}, s32[]{:S(2)}) async-start(s8[8388608]{0:T(1024)(128)(4,1)} %bitcast.135), calls=%async_computation.1 | async-start | bytes 8388608
  389.6 4.9 slice-start.1
  394.6 2.6 copy-start.5
  394.6 2.6 copy-start.7
  397.2 1.4 copy-start.9
  398.6 4.0 slice-start.2
  399.4 1.8 copy-start.26
  399.7 2.9 slice-start.3
  502.5 5.4 %copy-start.13 = (bf16[256,1536]{1,0:T(8,128)(2,1)S(1)}, bf16[256,1536]{1,0:T(8,128)(2,1)}, u32[]{:S(2)}) copy-start(bf16[256,1536]{1,0:T(8,128)(2,1)} %get-tuple-element.81) | copy-start | bytes 2359300
  502.5 6.3 %copy-start.14 = (bf16[256,1536]{1,0:T(8,128)(2,1)S(1)}, bf16[256,1536]{1,0:T(8,128)(2,1)}, u32[]{:S(2)}) copy-start(bf16[256,1536]{1,0:T(8,128)(2,1)} %get-tuple-element.82) | copy-start | bytes 2359300
  504.3 5.3 %copy-start.12 = (f32[96,2048]{1,0:T(8,128)S(1)}, f32[96,2048]{1,0:T(8,128)}, u32[]{:S(2)}) copy-start(f32[96,2048]{1,0:T(8,128)} %get-tuple-element.89) | copy-start | bytes 2359300
  507.9 2.7 copy-start.11
  508.8 2.6 copy-start.10
Sparse Core Ops, SparseCore 0:
  9.8 134.2 all-gather.1

commit v3 on v1

--- a/solution.py
+++ b/solution.py
@@ -1,6 +1,10 @@
+import functools
+
 import jax
 import jax.numpy as jnp
 from jax import lax
+from jax.experimental import pallas as pl
+from jax.experimental.pallas import tpu as pltpu
 from jax.sharding import PartitionSpec as P
 
 HEAD_SIZE = 96
@@ -44,16 +48,6 @@
     return factor, inputs * factor
 
 
-def rms_back(inputs, gain, gradient):
-    factor, normed = rms_parts(inputs)
-    gain_grad = jnp.sum(gradient * normed, axis=0)
-    scaled = gradient * gain
-    return (
-        factor * (scaled - normed * jnp.mean(scaled * normed, axis=-1, keepdims=True)),
-        gain_grad,
-    )
-
-
 def mul(left, right):
     return jnp.dot(left, right, preferred_element_type=F32)
 
@@ -90,6 +84,650 @@
         piece = lax.dynamic_slice_in_dim(whole, owner * rows, rows, 0).astype(BF16)
         total = total + mp_shift(piece, step, parts).astype(F32)
     return total
+
+
+MESH = pl.DeviceIdType.MESH
+VMEM_SPEC = pl.BlockSpec(memory_space=pltpu.VMEM)
+ANY_SPEC = pl.BlockSpec(memory_space=pl.ANY)
+DMA = pltpu.SemaphoreType.DMA
+
+
+def place(depth, parts):
+    me, part = lax.axis_index("dp"), lax.axis_index("mp")
+    z, y, core = me // 4, lax.rem(me // 2, 2), lax.rem(me, 2)
+
+    def dp_of(step, at_y, at_core):
+        return lax.rem(z + step, depth) * 4 + at_y * 2 + at_core
+
+    def mp_of(step):
+        return lax.rem(part + step, parts)
+
+    return me, part, z, y, core, dp_of, mp_of
+
+
+def greet(depth, parts):
+    me, part, z, y, core, dp_of, mp_of = place(depth, parts)
+    near = [(dp_of(0, y, 1 - core), part), (dp_of(0, 1 - y, core), part)]
+    near += [(dp_of(step, y, core), part) for step in range(1, depth)]
+    near += [(me, mp_of(step)) for step in range(1, parts)]
+    barrier = pltpu.get_barrier_semaphore()
+    for device in near:
+        pl.semaphore_signal(barrier, inc=1, device_id=device, device_id_type=MESH)
+    pl.semaphore_wait(barrier, len(near))
+
+
+def send(source, target, sems, at, device):
+    sent, landed = sems
+    return pltpu.make_async_remote_copy(
+        src_ref=source,
+        dst_ref=target,
+        send_sem=sent.at[at],
+        recv_sem=landed.at[at],
+        device_id=device,
+        device_id_type=MESH,
+    )
+
+
+def gather_kernel(depth, parts, count, *refs):
+    shards, normed, cot = refs[:count], refs[count], refs[count + 1]
+    weights, normed_all, cot_all = refs[count + 2 : 2 * count + 2], refs[-11], refs[-10]
+    z_sent, z_got, y_sent, y_got, c_sent, c_got, x_sent, x_got, kept = refs[-9:]
+    me, part, z, y, core, dp_of, mp_of = place(depth, parts)
+    own = [
+        pltpu.make_async_copy(shard, whole.at[me], kept.at[i])
+        for i, (shard, whole) in enumerate(zip(shards, weights))
+    ]
+    own.append(pltpu.make_async_copy(normed, normed_all.at[part], kept.at[count]))
+    own.append(pltpu.make_async_copy(cot, cot_all.at[part], kept.at[count + 1]))
+    for copy in own:
+        copy.start()
+    greet(depth, parts)
+    other_y, other_core = (dp_of(0, 1 - y, core), part), (dp_of(0, y, 1 - core), part)
+    steps = [(step, i) for step in range(depth) for i in range(count)]
+
+    along_z = [
+        send(shards[i], weights[i].at[me], (z_sent, z_got), n, (dp_of(step, y, core), part))
+        for n, (step, i) in enumerate(steps[count:])
+    ]
+    along_x = [
+        send(source, target.at[part], (x_sent, x_got), i * (parts - 1) + step - 1,
+             (me, mp_of(step)))
+        for i, (source, target) in enumerate(((normed, normed_all), (cot, cot_all)))
+        for step in range(1, parts)
+    ]
+
+    def block(step, i, at_y):
+        return weights[i].at[dp_of(depth - step, at_y, core)]
+
+    along_y, here_across, there_across = [], [], []
+    for n, (step, i) in enumerate(steps):
+        source = shards[i] if step == 0 else block(step, i, y)
+        along_y.append(send(source, block(step, i, y), (y_sent, y_got), n, other_y))
+        here_across.append(
+            send(source, block(step, i, y), (c_sent, c_got), 2 * n, other_core)
+        )
+        there_across.append(
+            send(block(step, i, 1 - y), block(step, i, 1 - y), (c_sent, c_got), 2 * n + 1,
+                 other_core)
+        )
+    for copy in along_z:
+        copy.start()
+    for copy in along_y[:count] + here_across[:count]:
+        copy.start()
+    for copy in along_x:
+        copy.start()
+    for n in range(count, len(steps)):
+        along_z[n - count].wait_recv()
+        along_y[n].start()
+        here_across[n].start()
+    for n in range(len(steps)):
+        along_y[n].wait_recv()
+        there_across[n].start()
+    for copy in along_x:
+        copy.wait()
+    for copy in along_z + along_y:
+        copy.wait_send()
+    for copy in here_across + there_across:
+        copy.wait()
+    for copy in own:
+        copy.wait()
+
+
+def gather_attn(shards, normed, cot):
+    depth, parts, count = lax.axis_size("dp") // 4, lax.axis_size("mp"), len(shards)
+    size = depth * 4
+    return pl.pallas_call(
+        functools.partial(gather_kernel, depth, parts, count),
+        out_shape=[jax.ShapeDtypeStruct((size,) + shard.shape, shard.dtype) for shard in shards]
+        + [jax.ShapeDtypeStruct((parts,) + rows.shape, rows.dtype) for rows in (normed, cot)],
+        in_specs=[ANY_SPEC] * (count + 2),
+        out_specs=[ANY_SPEC] * (count + 2),
+        scratch_shapes=[DMA((count * (depth - 1),))] * 2 + [DMA((count * depth,))] * 2
+        + [DMA((2 * count * depth,))] * 2 + [DMA((2 * (parts - 1),))] * 2 + [DMA((count + 2,))],
+        compiler_params=pltpu.CompilerParams(collective_id=0, has_side_effects=True),
+        name="gather_attn",
+    )(*shards, normed, cot)
+
+
+def add_rows(target, sources):
+    def body(i, carry):
+        here = pl.ds(pl.multiple_of(i * 16, 16), 16)
+        total = sources[0][here, :].astype(F32)
+        for source in sources[1:]:
+            total = total + source[here, :].astype(F32)
+        target[here, :] = total.astype(target.dtype)
+        return carry
+
+    lax.fori_loop(0, target.shape[0] // 16, body, 0)
+
+
+SLOTS = 2
+
+
+class Sums:
+    def __init__(self, depth, parts, wholes, outs, scratch):
+        self.depth, self.wholes, self.outs = depth, wholes, outs
+        count = len(outs)
+        self.held, self.ring, self.y_in, self.z_in = (
+            scratch[i * count : (i + 1) * count] for i in range(4)
+        )
+        self.sems = scratch[4 * count :]
+        self.order = [(step, k) for step in range(1, depth + 1) for k in range(count)]
+        self.where = place(depth, parts)
+        self.items = [self.item(n) for n in range(len(self.order))]
+
+    @staticmethod
+    def scratch(depth, blocks, computed):
+        count = len(blocks)
+        lead = (SLOTS, 2, 2) if computed else (SLOTS, 2)
+        buffers = [pltpu.VMEM((depth, 2) + block, BF16) for block in blocks]
+        buffers += [pltpu.VMEM(lead + block, BF16) for block in blocks]
+        buffers += [pltpu.VMEM((depth,) + block, BF16) for block in blocks]
+        buffers += [pltpu.VMEM((depth - 1,) + block, BF16) for block in blocks]
+        return buffers + [DMA((depth * count,))] * 7
+
+    def item(self, n):
+        step, k = self.order[n]
+        me, part, z, y, core, dp_of, mp_of = self.where
+        at = lax.rem(z + step, self.depth)
+        kept, c_sent, c_got, y_sent, y_got, z_sent, z_got = self.sems
+        held, slot = self.held[k], (n // len(self.outs)) % SLOTS
+        own = None
+        if self.wholes is None:
+            mine = self.ring[k].at[slot, :, core]
+            give = self.ring[k].at[slot, :, 1 - core]
+        else:
+            mine = self.ring[k].at[slot]
+            give = self.wholes[k].at[at, :, 1 - core]
+            own = pltpu.make_async_copy(self.wholes[k].at[at, :, core], mine, kept.at[n])
+        across = send(give, held.at[at], (c_sent, c_got), n, (dp_of(0, y, 1 - core), part))
+        along_y = send(
+            held.at[at, 1 - y], self.y_in[k].at[at], (y_sent, y_got), n,
+            (dp_of(0, 1 - y, core), part),
+        )
+        along_z = None
+        if step < self.depth:
+            along_z = send(
+                held.at[at, y], self.z_in[k].at[step - 1], (z_sent, z_got), n,
+                (dp_of(step, y, core), part),
+            )
+        return at, k, slot, own, across, along_y, along_z
+
+    def load(self, n):
+        self.items[n][3].start()
+        self.items[n][4].start()
+
+    def begin(self):
+        self.ahead = SLOTS * len(self.outs)
+        for n in range(min(self.ahead, len(self.items))):
+            self.load(n)
+
+    def cross(self, n):
+        core = self.where[4]
+        at, k, slot, own, across, along_y, along_z = self.items[n]
+        if own is not None:
+            own.wait()
+        across.wait_recv()
+        for at_y in range(2):
+            if own is not None:
+                mine = self.ring[k].at[slot, at_y]
+            else:
+                mine = self.ring[k].at[slot, at_y, core]
+            add_rows(self.held[k].at[at, at_y], (mine, self.held[k].at[at, at_y]))
+        along_y.start()
+        if own is not None and n + self.ahead < len(self.items):
+            self.load(n + self.ahead)
+
+    def onward(self, n):
+        y = self.where[3]
+        at, k, slot, own, across, along_y, along_z = self.items[n]
+        along_y.wait_recv()
+        held = self.held[k].at[at, y]
+        add_rows(held, (held, self.y_in[k].at[at]))
+        if along_z is not None:
+            along_z.start()
+
+    def end(self):
+        z, y = self.where[2:4]
+        for k, out in enumerate(self.outs):
+            for item in self.items:
+                if item[1] == k and item[6] is not None:
+                    item[6].wait_recv()
+            add_rows(
+                out, [self.held[k].at[z, y]] + [self.z_in[k].at[i] for i in range(self.depth - 1)]
+            )
+
+    def drain(self, crossed=0):
+        for n, (at, k, slot, own, across, along_y, along_z) in enumerate(self.items):
+            if n >= crossed:
+                across.wait_send()
+            along_y.wait_send()
+            if along_z is not None:
+                along_z.wait_send()
+
+
+class Gains:
+    def __init__(self, depth, parts, held, around, sems):
+        me, part, z, y, core, dp_of, mp_of = place(depth, parts)
+        self.held = held
+        stages = [
+            [(dp_of(0, y, 1 - core), part)],
+            [(me, mp_of(step)) for step in range(1, parts)],
+            [(dp_of(step, y, core), part) for step in range(1, depth)],
+            [(dp_of(0, 1 - y, core), part)],
+        ]
+        self.levels, slot = [], 0
+        for number, stage in enumerate(stages):
+            copies = []
+            for device in stage:
+                landing = around.at[pl.ds(16 * slot, 16)]
+                source = held.at[pl.ds(16 * number, 16)]
+                copies.append((send(source, landing, sems, slot, device), landing))
+                slot += 1
+            self.levels.append(copies)
+        self.number = 0
+
+    def begin(self):
+        for copy, landing in self.levels[self.number]:
+            copy.start()
+
+    def advance(self):
+        number = self.number
+        if number == len(self.levels):
+            return
+        total = self.held[16 * number : 16 * number + 16]
+        for copy, landing in self.levels[number]:
+            copy.wait_recv()
+            total = total + landing[...]
+        self.held[16 * (number + 1) : 16 * (number + 2)] = total
+        self.number += 1
+        if self.number < len(self.levels):
+            self.begin()
+
+    def drain(self):
+        for level in self.levels:
+            for copy, landing in level:
+                copy.wait_send()
+
+
+def norm_back(rows_in, gain, gradient):
+    factor = lax.rsqrt(jnp.mean(rows_in * rows_in, axis=-1, keepdims=True) + EPSILON)
+    normed = rows_in * factor
+    scaled = gradient * gain
+    back = factor * (scaled - normed * jnp.mean(scaled * normed, axis=-1, keepdims=True))
+    return back, gradient * normed
+
+
+TILE = 16
+
+
+def fold(terms):
+    total = terms[0:8]
+    for at in range(8, terms.shape[0], 8):
+        total = total + terms[at : at + 8]
+    return total
+
+
+def tiles(rows, tile, body):
+    def run(i, carry):
+        body(pl.ds(pl.multiple_of(i * tile, tile), tile))
+        return carry
+
+    lax.fori_loop(0, rows // tile, run, 0)
+
+
+def backward_kernel(depth, parts, heads, kv_heads, *refs):
+    (gate, up, down, own_two_in, give_two, own_out_in, give_out, residual_in, cot_in, tokens_in,
+     gain_one, gain_two, weights_in, out_w_in, normed_t_in, query_t_in, key_t_in, value_t_in,
+     attended_in, id_col, id_row, cosine, sine) = refs[:23]
+    (gate_out, up_out, down_out, attn_out, block_out, grad_tokens, gains, in_out) = refs[23:31]
+    (work, work_out, residual, cot, tokens, weights, out_w, normed_t, query_t, key_t, value_t,
+     attended, in_x, out_tile, branch, branch_t, grad_t, give_one, key_acc, value_acc, low,
+     held, around, loaded, stored, two_sent, two_got, out_sent, out_got, b_sent, b_got,
+     one_sent, one_got, g_sent, g_got) = refs[31:66]
+    rest = refs[66:]
+    me, part, z, y, core, dp_of, mp_of = place(depth, parts)
+    rows, width = residual.shape
+    group = rows * parts
+    members = heads // kv_heads
+    q_width, kv_width = heads * HEAD_SIZE, kv_heads * HEAD_SIZE
+    all_width = q_width + 2 * kv_width
+    half = HEAD_SIZE // 2
+    scale = HEAD_SIZE ** (-0.5)
+    mlp_refs = 4 * 3 + 7
+    mlp = Sums(depth, parts, (gate, up, down), (gate_out, up_out, down_out), rest[:mlp_refs])
+    attn = Sums(depth, parts, None, (attn_out,), rest[mlp_refs:])
+    total_gains = Gains(depth, parts, held, around, (g_sent, g_got))
+
+    pairs = [
+        (own_two_in, work), (residual_in, residual), (cot_in, cot), (out_w_in, out_w),
+        (query_t_in, query_t), (key_t_in, key_t), (value_t_in, value_t), (own_out_in, work_out),
+        (weights_in, weights), (normed_t_in, normed_t), (attended_in, attended),
+        (tokens_in, tokens),
+    ]
+    loads = [pltpu.make_async_copy(a, b, loaded.at[i]) for i, (a, b) in enumerate(pairs)]
+
+    def along_x(source, target, sems):
+        return [
+            send(source(step), target(step), sems, step - 1, (me, mp_of(step)))
+            for step in range(1, parts)
+        ]
+
+    to_two = along_x(lambda s: give_two.at[s - 1], lambda s: in_x.at[s - 1], (two_sent, two_got))
+    to_out = along_x(lambda s: give_out.at[s - 1], lambda s: in_out.at[s - 1], (out_sent, out_got))
+    to_branch = along_x(lambda s: branch.at[part], lambda s: branch.at[part], (b_sent, b_got))
+    to_one = along_x(lambda s: give_one.at[s - 1], lambda s: in_x.at[s - 1], (one_sent, one_got))
+
+    greet(depth, parts)
+    for copy in to_two:
+        copy.start()
+    mlp.begin()
+    for copy in loads:
+        copy.start()
+    items = len(mlp.items)
+    early = min(8, items)
+    for n in range(early):
+        mlp.cross(n)
+    for copy in loads[:3]:
+        copy.wait()
+    for copy in to_two:
+        copy.wait_recv()
+
+    held[0:16] = jnp.zeros((16, width), F32)
+
+    def second(here):
+        total = work[here, :]
+        for step in range(parts - 1):
+            total = total + in_x[step, here, :].astype(F32)
+        back, terms = norm_back(residual[here, :], gain_two[...], total)
+        held[8:16] += fold(terms)
+        result = cot[here, :].astype(F32) + back
+        work[here, :] = result
+        branch[part, here, :] = result.astype(BF16)
+
+    tiles(rows, TILE, second)
+    for copy in to_branch + to_out:
+        copy.start()
+    for n in range(early, items):
+        mlp.cross(n)
+    mlp.onward(0)
+    mlp.onward(1)
+    for copy in to_branch:
+        copy.wait()
+    for copy in loads[3:7]:
+        copy.wait()
+
+    block = 256 if q_width % 256 == 0 else q_width
+    for p in range(parts):
+        across = slice(p * rows, (p + 1) * rows)
+        for first in range(0, q_width, block):
+            piece = jnp.dot(
+                branch[p], out_w[:, first : first + block], preferred_element_type=F32
+            )
+            grad_t[first : first + block, across] = piece.T.astype(BF16)
+
+        def turn(i, carry):
+            here = pl.ds(pl.multiple_of(i * 128, 128), 128)
+            branch_t[here, across] = branch[p, :, here].astype(F32).T.astype(BF16)
+            return carry
+
+        lax.fori_loop(0, width // 128, turn, 0)
+
+    q_block = 256 if group <= 1024 else 128
+
+    def one_kv_head(j, carry):
+        kv_rows = pl.ds(pl.multiple_of(j * HEAD_SIZE, 32), HEAD_SIZE)
+        key_acc[...] = jnp.zeros_like(key_acc)
+        value_acc[...] = jnp.zeros_like(value_acc)
+        for member in range(members):
+            first = pl.multiple_of((j * members + member) * HEAD_SIZE, 32)
+            head = pl.ds(first, HEAD_SIZE)
+            for start in range(0, group, q_block):
+                stop = start + q_block
+                cols = slice(start, stop)
+                query, grad = query_t[head, cols], grad_t[head, cols]
+                key, value = key_t[kv_rows, :stop], value_t[kv_rows, :stop]
+                scores = lax.dot_general(
+                    query, key, (((0,), (0,)), ((), ())), preferred_element_type=F32
+                )
+                seen = id_col[cols, :] == id_row[:, :stop]
+                at_row = start + lax.broadcasted_iota(jnp.int32, (q_block, stop), 0)
+                at_col = lax.broadcasted_iota(jnp.int32, (q_block, stop), 1)
+                scores = jnp.where(seen & (at_col <= at_row), scores * scale, MASKED)
+                grown = jnp.exp(scores - jnp.max(scores, axis=-1, keepdims=True))
+                probs = grown * (1.0 / jnp.sum(grown, axis=-1, keepdims=True))
+                dprob = lax.dot_general(
+                    grad, value, (((0,), (0,)), ((), ())), preferred_element_type=F32
+                )
+                inner = jnp.sum(probs * dprob, axis=-1, keepdims=True)
+                dscore = (probs * (dprob - inner)).astype(BF16)
+                key_acc[:, :stop] += jnp.dot(query, dscore, preferred_element_type=F32)
+                value_acc[:, :stop] += jnp.dot(
+                    grad, probs.astype(BF16), preferred_element_type=F32
+                )
+                dquery = scale * lax.dot_general(
+                    key, dscore, (((1,), (1,)), ((), ())), preferred_element_type=F32
+                )
+                lead, tail = dquery[:half], dquery[half:]
+                cos, sin = cosine[:, cols], sine[:, cols]
+                grad_t[pl.ds(first, half), cols] = (lead * cos + tail * sin).astype(BF16)
+                grad_t[pl.ds(first + half, half), cols] = (tail * cos - lead * sin).astype(BF16)
+        lead, tail = key_acc[:half] * scale, key_acc[half:] * scale
+        cos, sin = cosine[...], sine[...]
+        first = pl.multiple_of(q_width + j * HEAD_SIZE, 32)
+        grad_t[pl.ds(first, half), :] = (lead * cos + tail * sin).astype(BF16)
+        grad_t[pl.ds(first + half, half), :] = (tail * cos - lead * sin).astype(BF16)
+        first = pl.multiple_of(q_width + kv_width + j * HEAD_SIZE, 32)
+        grad_t[pl.ds(first, HEAD_SIZE), :] = value_acc[...].astype(BF16)
+        return carry
+
+    cut = (kv_heads + 1) // 2
+    lax.fori_loop(0, cut, one_kv_head, 0)
+    mlp.onward(2)
+    lax.fori_loop(cut, kv_heads, one_kv_head, 0)
+    mlp.onward(3)
+
+    def turn_back(i, carry):
+        here = pl.ds(pl.multiple_of(i * 128, 128), 128)
+        piece = grad_t[here, :].astype(F32).T.astype(BF16)
+        for p in range(parts):
+            branch[p, :, here] = piece[p * rows : (p + 1) * rows]
+        return carry
+
+    lax.fori_loop(0, all_width // 128, turn_back, 0)
+    for copy in loads[7:]:
+        copy.wait()
+
+    def incoming(step, here):
+        return lax.dot_general(
+            branch[mp_of(step), :, :all_width], weights[here, :], (((1,), (1,)), ((), ())),
+            preferred_element_type=F32,
+        )
+
+    for step in range(1, parts):
+        for first in range(0, width, 512):
+            give_one[step - 1, :, first : first + 512] = incoming(
+                step, slice(first, first + 512)
+            ).astype(BF16)
+    for copy in to_one:
+        copy.start()
+
+    depth_rows = 4 * attn_out.shape[0]
+    quarter = attn_out.shape[0]
+
+    def weight_block(n):
+        at, k, slot = attn.items[n][:3]
+        lines = pl.ds(pl.multiple_of(at * depth_rows, 32), depth_rows)
+        if n >= SLOTS:
+            attn.items[n - SLOTS][4].wait_send()
+
+        def put(value, first):
+            for i in range(4):
+                attn.ring[0][slot, i // 2, i % 2, :, first : first + value.shape[1]] = value[
+                    i * quarter : (i + 1) * quarter
+                ].astype(BF16)
+
+        step = 512 if all_width % 512 == 0 else all_width
+        for first in range(0, all_width, step):
+            put(
+                lax.dot_general(
+                    normed_t[lines, :], grad_t[first : first + step, :],
+                    (((1,), (1,)), ((), ())), preferred_element_type=F32,
+                ),
+                first,
+            )
+        put(jnp.dot(branch_t[lines, :], attended[...], preferred_element_type=F32), all_width)
+        attn.items[n][4].start()
+
+    done = 4
+    for n in range(depth):
+        weight_block(n)
+        if n >= 1:
+            attn.cross(n - 1)
+        if done < items:
+            mlp.onward(done)
+            done += 1
+    attn.cross(depth - 1)
+
+    for copy in to_out:
+        copy.wait_recv()
+    tile = out_tile.shape[1]
+    for first in range(0, rows, tile):
+        fetch = pltpu.make_async_copy(in_out.at[:, pl.ds(first, tile)], out_tile, stored.at[0])
+        fetch.start()
+        fetch.wait()
+        for line in range(first, first + tile, 16):
+            here = slice(line, line + 16)
+            total = work_out[here, :]
+            for step in range(parts - 1):
+                total = total + out_tile[step, line - first : line - first + 16, :].astype(F32)
+            low[here, :] = (residual[here, :] + total).astype(BF16)
+    put_out = pltpu.make_async_copy(low, block_out, stored.at[1])
+    put_out.start()
+    for first in range(0, width, 512):
+        work_out[:, first : first + 512] = incoming(0, slice(first, first + 512))
+    if done < items:
+        mlp.onward(done)
+        done += 1
+    put_out.wait()
+
+    for copy in to_one:
+        copy.wait_recv()
+
+    def first_norm(here):
+        total = work_out[here, :]
+        for step in range(parts - 1):
+            total = total + in_x[step, here, :].astype(F32)
+        back, terms = norm_back(tokens[here, :].astype(F32), gain_one[...], total)
+        held[0:8] += fold(terms)
+        low[here, :] = (work[here, :] + back).astype(BF16)
+
+    tiles(rows, TILE, first_norm)
+    put_tokens = pltpu.make_async_copy(low, grad_tokens, stored.at[2])
+    put_tokens.start()
+    total_gains.begin()
+    while done < items:
+        mlp.onward(done)
+        done += 1
+        total_gains.advance()
+    while total_gains.number < 3:
+        total_gains.advance()
+    attn.onward(0)
+    mlp.end()
+    for n in range(1, depth):
+        attn.onward(n)
+    total_gains.advance()
+    gains[...] = held[64:80]
+    attn.end()
+    put_tokens.wait()
+    for copy in to_two + to_out + to_one:
+        copy.wait_send()
+    mlp.drain()
+    attn.drain(crossed=max(depth - SLOTS, 0))
+    total_gains.drain()
+
+
+def backward(grads, own_two, give_two, own_out, give_out, residual, cot, tokens, gain_one,
+             gain_two, weights, out_w, normed_t, query_t, key_t, value_t, attended, ids,
+             cosine, sine):
+    depth, parts = lax.axis_size("dp") // 4, lax.axis_size("mp")
+    rows, width = residual.shape
+    group = rows * parts
+    wholes = [grad.reshape(depth, 2, 2, grad.shape[0] // (4 * depth), -1) for grad in grads]
+    heads, kv_heads = query_t.shape[0] // HEAD_SIZE, key_t.shape[0] // HEAD_SIZE
+    attn_block = (width // (4 * depth), weights.shape[1] + out_w.shape[1])
+    stops = depth + parts
+    loaded = (own_two, own_out, residual, cot, tokens, weights, out_w, normed_t, query_t, key_t,
+              value_t, attended)
+    outs = pl.pallas_call(
+        functools.partial(backward_kernel, depth, parts, heads, kv_heads),
+        out_shape=[jax.ShapeDtypeStruct(whole.shape[3:], F32) for whole in wholes]
+        + [
+            jax.ShapeDtypeStruct(attn_block, F32),
+            jax.ShapeDtypeStruct((rows, width), BF16),
+            jax.ShapeDtypeStruct((rows, width), BF16),
+            jax.ShapeDtypeStruct((16, width), F32),
+            jax.ShapeDtypeStruct((parts - 1, rows, width), BF16),
+        ],
+        in_specs=[ANY_SPEC] * 10 + [VMEM_SPEC] * 2 + [ANY_SPEC] * 7 + [VMEM_SPEC] * 4,
+        out_specs=[VMEM_SPEC] * 4 + [ANY_SPEC] * 2 + [VMEM_SPEC, ANY_SPEC],
+        scratch_shapes=[pltpu.VMEM(array.shape, array.dtype) for array in loaded]
+        + [
+            pltpu.VMEM((parts - 1, rows, width), BF16),
+            pltpu.VMEM((parts - 1, 64, width), BF16),
+            pltpu.VMEM((parts, rows, width), BF16),
+            pltpu.VMEM((width, group), BF16),
+            pltpu.VMEM((weights.shape[1], group), BF16),
+            pltpu.VMEM((parts - 1, rows, width), BF16),
+            pltpu.VMEM((HEAD_SIZE, group), F32),
+            pltpu.VMEM((HEAD_SIZE, group), F32),
+            pltpu.VMEM((rows, width), BF16),
+            pltpu.VMEM((80, width), F32),
+            pltpu.VMEM((16 * stops, width), F32),
+            DMA((len(loaded),)),
+            DMA((3,)),
+        ]
+        + [DMA((parts - 1,))] * 8 + [DMA((stops,))] * 2
+        + Sums.scratch(depth, [whole.shape[3:] for whole in wholes], False)
+        + Sums.scratch(depth, [attn_block], True),
+        compiler_params=pltpu.CompilerParams(
+            collective_id=1, has_side_effects=True, vmem_limit_bytes=63 * 2**20
+        ),
+        name="backward",
+    )(*wholes, own_two, give_two, own_out, give_out, residual, cot, tokens, gain_one, gain_two,
+      weights, out_w, normed_t, query_t, key_t, value_t, attended, *ids, cosine, sine)
+    return outs[:7]
+
+
+def own_and_give(whole, parts):
+    me = lax.axis_index("mp")
+    rows = whole.shape[0] // parts
+    own = lax.dynamic_slice_in_dim(whole, me * rows, rows, 0)
+    give = [
+        lax.dynamic_slice_in_dim(whole, lax.rem(me + step, parts) * rows, rows, 0).astype(BF16)
+        for step in range(1, parts)
+    ]
+    return own, jnp.stack(give)
 
 
 def shards(
@@ -114,21 +752,22 @@
     members = heads // kv_heads
     factor = HEAD_SIZE ** (-0.5)
 
-    attn_w = lax.all_gather(
-        jnp.concatenate([w_query, key_weight, value_weight, w_out.T], axis=1),
-        "dp", axis=0, tiled=True,
-    )
-    mlp_w = lax.all_gather(
-        jnp.concatenate([w_gate, w_up, w_down.T], axis=1), "dp", axis=0, tiled=True
-    )
-    cuts = (q_width, q_width + kv_width, q_width + 2 * kv_width)
-    query_w, key_w, value_w, out_wt = jnp.split(attn_w, cuts, axis=1)
-    gate_w, up_w, down_wt = jnp.split(mlp_w, 3, axis=1)
-
+    width = tokens.shape[1]
     inputs = tokens.astype(F32)
     gain_one, gain_two = norm_attn.astype(F32), norm_mlp.astype(F32)
-    normed_one = mp_gather((rms_parts(inputs)[1] * gain_one).astype(BF16), parts)
-    grad_rows = mp_gather(cotangent, parts)
+    mlp_shard = jnp.concatenate([w_gate, w_up, w_down.T], axis=1)
+    attn_w, out_wt, normed_one, grad_rows = gather_attn(
+        (jnp.concatenate([w_query, key_weight, value_weight], axis=1), w_out.T),
+        (rms_parts(inputs)[1] * gain_one).astype(BF16),
+        cotangent,
+    )
+    mlp_shard, attn_w = lax.optimization_barrier((mlp_shard, attn_w))
+    mlp_w = lax.all_gather(mlp_shard, "dp", axis=0, tiled=True)
+    attn_w, out_wt = attn_w.reshape(width, -1), out_wt.reshape(width, -1)
+    normed_one, grad_rows = normed_one.reshape(group, width), grad_rows.reshape(group, width)
+    cuts = (q_width, q_width + kv_width)
+    query_w, key_w, value_w = jnp.split(attn_w, cuts, axis=1)
+    gate_w, up_w, down_wt = jnp.split(mlp_w, 3, axis=1)
 
     segment, position = layout(seq_lengths[0], group)
     cosine, sine = rotation(position)
@@ -168,55 +807,34 @@
         BF16
     )
     grad_up = (grad_hidden * swish).astype(BF16)
-    grad_mlp = jnp.concatenate(
-        [
-            outer_sum(normed_two, grad_gate).astype(BF16),
-            outer_sum(normed_two, grad_up).astype(BF16),
-            outer_sum(grad_rows, hidden).astype(BF16),
-        ],
-        axis=1,
+    grads_mlp = (
+        outer_sum(normed_two, grad_gate).astype(BF16),
+        outer_sum(normed_two, grad_up).astype(BF16),
+        outer_sum(grad_rows, hidden).astype(BF16),
     )
-    grad_mlp = lax.psum_scatter(grad_mlp, "dp", scatter_dimension=0, tiled=True)
-    grad_two = mp_sum_rows(mul_t(grad_gate, gate_w) + mul_t(grad_up, up_w), parts)
-    block_out = (residual + mp_sum_rows(branch, parts)).astype(BF16)
-
-    from_two, gain_two_grad = rms_back(residual, gain_two, grad_two)
-    grad_residual = cotangent.astype(F32) + from_two
-    grad_branch = mp_gather(grad_residual.astype(BF16), parts)
-    grad_attended = (
-        mul(grad_branch, out_wt).astype(BF16).reshape(group, kv_heads, members, HEAD_SIZE)
+    ids = jnp.where(segment >= 0, segment, 3 + places)
+    grad_gate_w, grad_up_w, grad_down_w, grad_attn, block_out, grad_tokens, gains = backward(
+        grads_mlp,
+        *own_and_give(mul_t(grad_gate, gate_w) + mul_t(grad_up, up_w), parts),
+        *own_and_give(branch, parts),
+        residual,
+        cotangent,
+        tokens,
+        gain_one[None, :],
+        gain_two[None, :],
+        attn_w,
+        out_wt,
+        normed_one.T,
+        query.reshape(group, q_width).T,
+        key.reshape(group, kv_width).T,
+        value.reshape(group, kv_width).T,
+        attended,
+        (ids[:, None], ids[None, :]),
+        cosine[:, 0, :].T,
+        sine[:, 0, :].T,
     )
-    dprob = jnp.einsum("qhgd,khd->hgqk", grad_attended, value, preferred_element_type=F32)
-    inner = jnp.sum(probs * dprob, axis=-1, keepdims=True)
-    dscore = (probs * (dprob - inner)).astype(BF16)
-    grad_query = jnp.einsum("hgqk,khd->qhgd", dscore, key, preferred_element_type=F32) * factor
-    grad_key = jnp.einsum("hgqk,qhgd->khd", dscore, query, preferred_element_type=F32) * factor
-    grad_value = jnp.einsum(
-        "hgqk,qhgd->khd", probs_low, grad_attended, preferred_element_type=F32
-    )
-    grad_query = rotate(grad_query.reshape(group, heads, HEAD_SIZE), cosine, -sine)
-    grad_query = grad_query.astype(BF16).reshape(group, q_width)
-    grad_key = rotate(grad_key, cosine, -sine).astype(BF16).reshape(group, kv_width)
-    grad_value = grad_value.astype(BF16).reshape(group, kv_width)
-    grad_attn = jnp.concatenate(
-        [
-            outer_sum(normed_one, grad_query).astype(BF16),
-            outer_sum(normed_one, grad_key).astype(BF16),
-            outer_sum(normed_one, grad_value).astype(BF16),
-            outer_sum(grad_branch, attended).astype(BF16),
-        ],
-        axis=1,
-    )
-    grad_attn = lax.psum_scatter(grad_attn, "dp", scatter_dimension=0, tiled=True)
-    grad_one = mp_sum_rows(
-        mul_t(grad_query, query_w) + mul_t(grad_key, key_w) + mul_t(grad_value, value_w), parts
-    )
-    from_one, gain_one_grad = rms_back(inputs, gain_one, grad_one)
-    grad_tokens = (grad_residual + from_one).astype(BF16)
-    gains = lax.psum(jnp.stack([gain_one_grad, gain_two_grad]), ("dp", "mp"))
-
-    attn_parts = jnp.split(grad_attn.astype(F32), cuts, axis=1)
-    mlp_parts = jnp.split(grad_mlp.astype(F32), 3, axis=1)
+    attn_parts = jnp.split(grad_attn, cuts + (q_width + 2 * kv_width,), axis=1)
+    gains = jnp.sum(gains.reshape(2, 8, width), axis=1)
     return (
         block_out,
         grad_tokens,
@@ -226,9 +844,9 @@
         attn_parts[2],
         attn_parts[3].T,
         gains[1],
-        mlp_parts[0],
-        mlp_parts[1],
-        mlp_parts[2].T,
+        grad_gate_w,
+        grad_up_w,
+        grad_down_w.T,
     )
 
 

time: 614 us -> 449 us (0.73)
  the two profiles are of different devices: /device:TPU:10 before, /device:TPU:24 now
where the time goes in v3:
time: 449 us; the launch traced here: 441 us
  Pallas kernels  254 us (57%)
  matrix products  68.2 us (15%)
  waiting for transfers between devices  48.8 us (11%)
  local copies, waits for them, and re-layouts  32 us (7%)
  other arithmetic  18.5 us (4%)
  between operations  16.9 us (4%)
    pallas_call x1, Pallas kernels, backward(): pl.pallas_call(functools.partial(backward_kernel, depth, parts, heads, kv...  191 us
    pallas_call x1, Pallas kernels, gather_attn(): pl.pallas_call(functools.partial(gather_kernel, depth, parts, count), out...  62.8 us
    dot_general x6, matrix products, mul(): return jnp.dot(left, right, preferred_element_type=F32)  28.4 us
    all_gather x1, waiting for transfers between devices, shards(): mlp_w = lax.all_gather(mlp_shard, 'dp', axis=0, tiled=True)  24.6 us
    ppermute x2, waiting for transfers between devices, mp_shift(): lax.ppermute(block, 'mp', [(i, (i + step) % parts) for i in range(parts)])  24.1 us
    dot_general x3, matrix products, outer_sum(): lax.dot_general(left, right, (((0,), (0,)), ((), ())), preferred_element_...  16.4 us
    dot_general x4, matrix products, mul_t(): lax.dot_general(left, right, (((1,), (1,)), ((), ())), preferred_element_...  13.4 us
  transfers between devices with their start and end apart: 3, of which 3 were waited for; matrix products, arithmetic and copies ran while one was open for 10% of the time, Pallas kernels for 0%

profile of v3, /device:TPU:24, one launch (start us, length us, event | category | flops | bytes accessed | tf_op | source)
XLA Modules:
  0.0 441.4 jit_solution(2827745842726164299)
XLA Ops:
  7.3 1.5 fusion.22
  9.5 2.3 fusion.24.refs_2_
  12.5 1.1 pad_maximum_fusion
  13.6 62.8 %gather_attn.1 = (bf16[16,96,1536]{2,1,0:T(8,128)(2,1)}, bf16[16,96,768]{2,1,0:T(8,128)(2,1)}, bf16[2,256,1536]{2,1,0:T(8,128)(2,1)}, bf16[2,256,1536]{2,1,0:T(8,128)(2,1)}) custom-call(bf16[96,1536]{1,0:T(8,128)(2,1)} %pad_maximum_fusion.9.refs_0_, bf16[96,768]{1,0:T(8,128)(2,1)} %bitcast.118, bf16[256,1536]{1,0:T(8,128)(2,1)} %fusion.24.refs_2_, ...), custom_call_target="tpu_custom_call" | custom-call | tf_op jit(solution)/shard_map/gather_attn/pallas_call | solution.py:199
  76.4 1.4 slice_bitcast_fusion.1
  78.4 1.8 slice_bitcast_fusion
  80.3 2.5 copy.33
  87.3 2.4 fusion.52
  89.9 1.4 fusion.53
  91.6 2.1 convolution_convert_fusion.3
  93.7 5.5 %fusion.47 = (f32[4,2,512]{2,1,0:T(2,128)S(1)}, f32[4,2,512,512]{2,3,1,0:T(8,128)}) fusion(pred[512,512]{0,1:T(8,128)(4,1)S(1)} %fusion.28, bf16[512,4,2,48]{0,3,2,1:T(8,128)(2,1)S(1)} %bitcast.110, bf16[512,4,2,48]{0,3,2,1:T(8,128)(2,1)S(1)} %bitcast.109, bf16[512,4,48]{0,2,1:T(8,128)(2,1)S(1)} %get-tuple-element.49, ...), kind=kOutput, calls=%fused_computation.101 | convolution fusion | flops 413401600 | bytes 9846784 | tf_op jit(solution)/shard_map/sub | solution.py:789
  99.2 4.5 %fusion.25 = bf16[4,96,2,512]{3,1,2,0:T(8,128)(2,1)S(1)} fusion(bf16[512,4,96,1]{0,2,3,1:T(8,128)(2,1)S(1)} %bitcast.115, f32[4,2,512,512]{2,3,1,0:T(8,128)} %get-tuple-element.62, f32[4,2,512]{2,1,0:T(2,128)S(1)} %get-tuple-element.61), kind=kOutput, calls=%fused_computation.42 | convolution fusion | flops 407240704 | bytes 9584640 | tf_op jit(solution)/shard_map/hgqk,khd->qhgd/dot_general | solution.py:793
  103.8 1.4 fusion.54
  105.3 1.7 copy-done.4
  107.0 1.0 dynamic-slice_convert_fusion.2
  107.9 1.5 collective-permute-start
  109.4 18.0 %collective-permute-done = bf16[256,1536]{1,0:T(8,128)(2,1)} collective-permute-done((bf16[256,1536]{1,0:T(8,128)(2,1)}, bf16[256,1536]{1,0:T(8,128)(2,1)}, u32[]{:S(2)}, u32[]{:S(2)}) %collective-permute-start) | collective-permute-done | bytes 786464 | tf_op jit(solution)/shard_map/ppermute | solution.py:64
  127.4 2.2 multiply_reduce_fusion
  129.7 1.3 constant_dynamic-update-slice_fusion.1
  131.0 1.1 copy-done.6
  132.1 1.5 collective-permute-start.1
  134.8 1.7 copy.42
  136.6 2.4 copy.36.refs_18_
  139.0 1.2 compare_select_fusion.1.refs_20_
  140.2 1.4 compare_select_fusion.refs_19_
  142.4 0.9 pad_maximum_fusion.2
  143.4 1.1 multiply_sine_fusion
  144.5 6.1 %collective-permute-done.1 = bf16[256,1536]{1,0:T(8,128)(2,1)} collective-permute-done((bf16[256,1536]{1,0:T(8,128)(2,1)}, bf16[256,1536]{1,0:T(8,128)(2,1)}, u32[]{:S(2)}, u32[]{:S(2)}) %collective-permute-start.1) | collective-permute-done | bytes 786464 | tf_op jit(solution)/shard_map/ppermute | solution.py:64
  150.6 1.2 constant_dynamic-update-slice_fusion
  151.8 24.6 %all-gather.2.cloned.1.call-done = bf16[1536,6144]{1,0:T(8,128)(2,1)} async-done(((bf16[96,6144]{1,0:T(8,128)(2,1)}), bf16[1536,6144]{1,0:T(8,128)(2,1)}) %all-gather.2.cloned.1.call-update) | async-done | bytes 18874384 | tf_op jit(solution)/shard_map/all_gather | solution.py:765
  176.5 9.0 %fusion.12 = f32[512,2048]{1,0:T(8,128)} fusion(bf16[512,1536]{1,0:T(8,128)(2,1)} %bitcast.119, bf16[1536,6144]{1,0:T(8,128)(2,1)} %all-gather.2.cloned.1.call-done), kind=kOutput, calls=%fused_computation.18 | convolution fusion | flops 3221225472 | bytes 12058624 | tf_op jit(solution)/shard_map/dot_general | solution.py:52
  185.4 1.2 copy-done.26
  186.6 5.1 %fusion.4 = f32[512,2048]{1,0:T(8,128)} fusion(bf16[512,1536]{1,0:T(8,128)(2,1)S(1)} %constant_dynamic-update-slice_fusion, bf16[1536,6144]{1,0:T(8,128)(2,1)S(1)} %copy-done.26), kind=kOutput, calls=%fused_computation.10 | convolution fusion | flops 3221225472 | bytes 12058624 | tf_op jit(solution)/shard_map/dot_general | solution.py:52
  191.8 8.4 %multiply_convert_fusion = (bf16[512,2048]{1,0:T(8,128)(2,1)S(1)}, bf16[512,2048]{1,0:T(8,128)(2,1)S(1)}, bf16[512,2048]{1,0:T(8,128)(2,1)}) fusion(f32[512,2048]{1,0:T(8,128)} %fusion.4, f32[512,2048]{1,0:T(8,128)} %fusion.12, bf16[512,1536]{1,0:T(8,128)(2,1)S(1)} %constant_dynamic-update-slice_fusion, bf16[1536,6144]{1,0:T(8,128)(2,1)S(1)} %copy-done.26), kind=kOutput, calls=%fused_computation.20 | convolution fusion | flops 3236954112 | bytes 22544384 | tf_op jit(solution)/shard_map/dot_general | solution.py:52
  200.2 3.5 fusion.10
  203.7 1.0 fusion.33.refs_6_
  204.6 1.2 constant_dynamic-slice_fusion.refs_5_
  205.9 5.6 %convolution_convert_fusion = bf16[1536,2048]{1,0:T(8,128)(2,1)} fusion(bf16[512,1536]{1,0:T(8,128)(2,1)S(1)} %bitcast.120, bf16[512,2048]{1,0:T(8,128)(2,1)S(1)} %get-tuple-element.43), kind=kOutput, calls=%fused_computation.4 | convolution fusion | flops 3224371200 | bytes 9961472 | tf_op jit(solution)/shard_map/dot_general | solution.py:60
  211.5 3.5 fusion.2
  215.0 5.1 %fusion.19 = f32[512,1536]{1,0:T(8,128)S(1)} fusion(f32[512,1536]{1,0:T(8,128)S(1)} %fusion.2, bf16[512,2048]{1,0:T(8,128)(2,1)} %get-tuple-element.45, bf16[1536,6144]{1,0:T(8,128)(2,1)S(1)} %copy-done.26), kind=kOutput, calls=%fused_computation.29 | convolution fusion | flops 3222011904 | bytes 14680064 | tf_op jit(solution)/shard_map/dot_general | solution.py:56
  220.0 1.0 fusion.32.refs_4_
  221.0 1.3 constant_dynamic-slice_fusion.1.refs_3_
  222.3 5.4 %convolution_convert_fusion.1 = bf16[1536,2048]{1,0:T(8,128)(2,1)} fusion(bf16[512,1536]{1,0:T(8,128)(2,1)S(1)} %constant_dynamic-update-slice_fusion, bf16[512,2048]{1,0:T(8,128)(2,1)S(1)} %copy-done.30), kind=kOutput, calls=%fused_computation.5 | convolution fusion | flops 3224371200 | bytes 9961472 | tf_op jit(solution)/shard_map/dot_general | solution.py:60
  227.7 5.4 %convolution_convert_fusion.2 = bf16[1536,2048]{1,0:T(8,128)(2,1)} fusion(bf16[512,1536]{1,0:T(8,128)(2,1)S(1)} %constant_dynamic-update-slice_fusion, bf16[512,2048]{1,0:T(8,128)(2,1)S(1)} %copy-done.29), kind=kOutput, calls=%fused_computation.6 | convolution fusion | flops 3224371200 | bytes 9961472 | tf_op jit(solution)/shard_map/dot_general | solution.py:60
  233.1 191.2 %backward.1 = (f32[96,2048]{1,0:T(8,128)}, f32[96,2048]{1,0:T(8,128)}, f32[96,2048]{1,0:T(8,128)}, f32[96,2304]{1,0:T(8,128)}, bf16[256,1536]{1,0:T(8,128)(2,1)}...) custom-call(bf16[4,2,2,96,2048]{4,3,2,1,0:T(8,128)(2,1)} %bitcast.99, ...), custom_call_target="tpu_custom_call" | custom-call | tf_op jit(solution)/shard_map/backward/pallas_call | solution.py:682
  424.3 1.8 fusion.45
  426.1 2.0 slice_bitcast_fusion.2
  428.1 0.9 bitcast_reduce_fusion
  (85 shorter events, 12.4 us)
Async XLA Ops:
  7.2 4.5 %copy-start.19 = (bf16[96,384]{1,0:T(8,128)(2,1)S(1)}, bf16[96,384]{1,0:T(8,128)(2,1)}, u32[]{:S(2)}) copy-start(bf16[96,384]{1,0:T(8,128)(2,1)} %param.17) | copy-start | bytes 221188
  7.2 4.5 %copy-start.20 = (bf16[96,384]{1,0:T(8,128)(2,1)S(1)}, bf16[96,384]{1,0:T(8,128)(2,1)}, u32[]{:S(2)}) copy-start(bf16[96,384]{1,0:T(8,128)(2,1)} %param.16) | copy-start | bytes 221188
  7.2 4.5 %copy-start.18 = (bf16[96,768]{1,0:T(8,128)(2,1)S(1)}, bf16[96,768]{1,0:T(8,128)(2,1)}, u32[]{:S(2)}) copy-start(bf16[96,768]{1,0:T(8,128)(2,1)} %param.15) | copy-start | bytes 442372
  7.2 5.3 %copy-start.15 = (bf16[2048,96]{0,1:T(8,128)(2,1)S(1)}, bf16[2048,96]{0,1:T(8,128)(2,1)}, u32[]{:S(2)}) copy-start(bf16[2048,96]{0,1:T(8,128)(2,1)} %param.22) | copy-start | bytes 1179652
  7.2 5.3 %copy-start.16 = (bf16[96,2048]{1,0:T(8,128)(2,1)S(1)}, bf16[96,2048]{1,0:T(8,128)(2,1)}, u32[]{:S(2)}) copy-start(bf16[96,2048]{1,0:T(8,128)(2,1)} %param.21) | copy-start | bytes 1179652
  7.2 5.2 %copy-start.17 = (bf16[96,2048]{1,0:T(8,128)(2,1)S(1)}, bf16[96,2048]{1,0:T(8,128)(2,1)}, u32[]{:S(2)}) copy-start(bf16[96,2048]{1,0:T(8,128)(2,1)} %param.20) | copy-start | bytes 1179652
  7.2 169.2 %all-gather.2.cloned.1.call-start = ((), (), s32[]{:S(2)}) async-start(), calls=%async_computation | async-start | bytes 20054016 | tf_op jit(solution)/shard_map/all_gather | solution.py:765
  80.3 2.5 copy-start.23
  85.3 4.4 copy-start.24
  87.3 2.5 copy-start.3
  87.3 2.6 copy-start.5
  93.7 5.5 %copy-start.14 = (bf16[512,384]{0,1:T(8,128)(2,1)}, bf16[512,384]{0,1:T(8,128)(2,1)S(1)}, u32[]{:S(2)}) copy-start(bf16[512,384]{0,1:T(8,128)(2,1)S(1)} %convolution_convert_fusion.3) | copy-start | bytes 1179652
  99.2 4.5 %copy-start.2 = (bf16[16,96,768]{2,1,0:T(8,128)(2,1)S(1)}, bf16[16,96,768]{2,1,0:T(8,128)(2,1)}, u32[]{:S(2)}) copy-start(bf16[16,96,768]{2,1,0:T(8,128)(2,1)} %get-tuple-element.27) | copy-start | bytes 7077892
  103.8 4.1 copy-start.8
  103.8 5.6 %copy-start.22 = (bf16[1536]{0:T(1024)(128)(2,1)S(1)}, bf16[1536]{0:T(1024)(128)(2,1)}, u32[]{:S(2)}) copy-start(bf16[1536]{0:T(1024)(128)(2,1)} %param.19) | copy-start | bytes 9220
  105.2 1.7 copy-start.4
  107.0 20.5 %copy-start.1 = (bf16[256,1536]{1,0:T(8,128)(2,1)S(1)}, bf16[256,1536]{1,0:T(8,128)(2,1)}, u32[]{:S(2)}) copy-start(bf16[256,1536]{1,0:T(8,128)(2,1)} %refs_9_.1) | copy-start | bytes 2359300
  107.9 19.5 %collective-permute-start = (bf16[256,1536]{1,0:T(8,128)(2,1)}, bf16[256,1536]{1,0:T(8,128)(2,1)}, u32[]{:S(2)}, u32[]{:S(2)}) collective-permute-start(bf16[256,1536]{1,0:T(8,128)(2,1)} %dynamic-slice_convert_fusion.2), channel_id=1, source_target_pairs={{0,1},{1,0},{2,3},{3,2},{4,5},{5,4},{6,7},{7,6},{8,9},{9,8},{10,11... | collective-permute-start | bytes 2359304 | tf_op jit(solution)/shard_map/ppermute | solution.py:64
  129.6 1.4 copy-start
  129.6 4.0 copy-start.21
  131.0 1.1 copy-start.6
  132.1 18.5 %collective-permute-start.1 = (bf16[256,1536]{1,0:T(8,128)(2,1)}, bf16[256,1536]{1,0:T(8,128)(2,1)}, u32[]{:S(2)}, u32[]{:S(2)}) collective-permute-start(bf16[256,1536]{1,0:T(8,128)(2,1)} %get-tuple-element.40), channel_id=1, source_target_pairs={{0,1},{1,0},{2,3},{3,2},{4,5},{5,4},{6,7},{7,6},{8,9},{9,8},{10,11... | collective-permute-start | bytes 2359304 | tf_op jit(solution)/shard_map/ppermute | solution.py:64
  136.6 6.8 %copy-start.25 = (f32[48]{0:T(128)S(1)}, f32[48]{0:T(128)}, u32[]{:S(2)}) copy-start(f32[48]{0:T(128)} %copy-done.24) | copy-start | bytes 580
  136.6 14.0 %copy-start.7 = (bf16[512,1536]{1,0:T(8,128)(2,1)S(1)}, bf16[512,1536]{1,0:T(8,128)(2,1)}, u32[]{:S(2)}) copy-start(bf16[512,1536]{1,0:T(8,128)(2,1)} %copy-done.6) | copy-start | bytes 4718596
  176.5 10.2 %copy-start.26 = (bf16[1536,6144]{1,0:T(8,128)(2,1)S(1)}, bf16[1536,6144]{1,0:T(8,128)(2,1)}, u32[]{:S(2)}) copy-start(bf16[1536,6144]{1,0:T(8,128)(2,1)} %all-gather.2.cloned.1.call-done) | copy-start | bytes 56623108
  200.2 11.3 %copy-start.28 = (bf16[512,2048]{1,0:T(8,128)(2,1)}, bf16[512,2048]{1,0:T(8,128)(2,1)S(1)}, u32[]{:S(2)}) copy-start(bf16[512,2048]{1,0:T(8,128)(2,1)S(1)} %get-tuple-element.44) | copy-start | bytes 6291460
  203.7 2.2 copy-start.27
  220.0 2.3 copy-start.30
  222.3 5.4 %copy-start.29 = (bf16[512,2048]{1,0:T(8,128)(2,1)S(1)}, bf16[512,2048]{1,0:T(8,128)(2,1)}, u32[]{:S(2)}) copy-start(bf16[512,2048]{1,0:T(8,128)(2,1)} %copy-done.28) | copy-start | bytes 6291460
  424.3 5.4 %copy-start.13 = (bf16[256,1536]{1,0:T(8,128)(2,1)S(1)}, bf16[256,1536]{1,0:T(8,128)(2,1)}, u32[]{:S(2)}) copy-start(bf16[256,1536]{1,0:T(8,128)(2,1)} %get-tuple-element.76) | copy-start | bytes 2359300
  424.3 6.3 %copy-start.12 = (bf16[256,1536]{1,0:T(8,128)(2,1)S(1)}, bf16[256,1536]{1,0:T(8,128)(2,1)}, u32[]{:S(2)}) copy-start(bf16[256,1536]{1,0:T(8,128)(2,1)} %get-tuple-element.77) | copy-start | bytes 2359300
  426.1 5.3 %copy-start.11 = (f32[96,2048]{1,0:T(8,128)S(1)}, f32[96,2048]{1,0:T(8,128)}, u32[]{:S(2)}) copy-start(f32[96,2048]{1,0:T(8,128)} %get-tuple-element.84) | copy-start | bytes 2359300
  429.7 2.7 copy-start.10
  430.5 2.6 copy-start.9
Sparse Core Ops, SparseCore 0:
  76.5 99.9 all-gather.1

commit v4 on v3

--- a/solution.py
+++ b/solution.py
@@ -128,69 +128,160 @@
     )
 
 
+class Gather:
+    def __init__(self, depth, parts, shards, wholes, sems):
+        self.depth, self.shards, self.wholes = depth, shards, wholes
+        self.where = place(depth, parts)
+        self.kept, self.z_sems, self.y_sems, self.c_sems = (
+            sems[0], sems[1:3], sems[3:5], sems[5:7]
+        )
+        self.slots = 2 * depth - 1
+
+    @staticmethod
+    def semaphores(depth, count):
+        slots = count * (2 * depth - 1)
+        return [DMA((count,))] + [DMA((slots,))] * 4 + [DMA((2 * slots,))] * 2
+
+    def block(self, i, move, at_y):
+        me, part, z, y, core, dp_of, mp_of = self.where
+        return self.wholes[i].at[(z + move) * 4 + at_y * 2 + core]
+
+    def slot(self, move):
+        return -move if move <= 0 else self.depth - 1 + move
+
+    def source(self, i, move):
+        return self.shards[i] if move == 0 else self.block(i, move, self.where[3])
+
+    def along_z(self, i, move, ahead):
+        me, part, z, y, core, dp_of, mp_of = self.where
+        at = i * self.slots + self.slot(move - ahead)
+        device = ((z + ahead) * 4 + y * 2 + core, part)
+        return send(self.source(i, move), self.block(i, move, y), self.z_sems, at, device)
+
+    def arrival(self, i, move):
+        me, part, z, y, core, dp_of, mp_of = self.where
+        at = i * self.slots + self.slot(move)
+        block = self.block(i, move, y)
+        return send(block, block, self.z_sems, at, (me, part))
+
+    def along_y(self, i, move):
+        me, part, z, y, core, dp_of, mp_of = self.where
+        at = i * self.slots + self.slot(move)
+        return send(self.source(i, move), self.block(i, move, y), self.y_sems, at,
+                    (dp_of(0, 1 - y, core), part))
+
+    def across(self, i, move, other):
+        me, part, z, y, core, dp_of, mp_of = self.where
+        at = 2 * (i * self.slots + self.slot(move)) + other
+        at_y = 1 - y if other else y
+        source = self.block(i, move, at_y) if other else self.source(i, move)
+        return send(source, self.block(i, move, at_y), self.c_sems, at,
+                    (dp_of(0, y, 1 - core), part))
+
+    def there(self, move, action):
+        z = self.where[2]
+        if move == 0:
+            action()
+        else:
+            pl.when((z + move >= 0) & (z + move < self.depth))(action)
+
+    def begin(self, i):
+        self.keep(i).start()
+        for ahead in (1, -1):
+            self.there(ahead, lambda ahead=ahead: self.along_z(i, 0, ahead).start())
+        self.along_y(i, 0).start()
+        self.across(i, 0, 0).start()
+
+    def keep(self, i):
+        return pltpu.make_async_copy(self.shards[i], self.wholes[i].at[self.where[0]],
+                                     self.kept.at[i])
+
+    def moves(self, step):
+        return (0,) if step == 0 else (-step, step)
+
+    def from_z(self, i, step):
+        for move in self.moves(step):
+            ahead = 1 if move < 0 else -1
+
+            def pass_on(move=move, ahead=ahead):
+                self.arrival(i, move).wait_recv()
+                self.there(ahead, lambda: self.along_z(i, move, ahead).start())
+                self.along_y(i, move).start()
+                self.across(i, move, 0).start()
+
+            self.there(move, pass_on)
+
+    def from_y(self, i, step):
+        for move in self.moves(step):
+
+            def pass_on(move=move):
+                self.along_y(i, move).wait_recv()
+                self.across(i, move, 1).start()
+
+            self.there(move, pass_on)
+
+    def end(self, i):
+        self.keep(i).wait()
+        for step in range(self.depth):
+            for move in self.moves(step):
+
+                def settle(move=move):
+                    self.across(i, move, 0).wait_recv()
+                    self.across(i, move, 1).wait_recv()
+
+                self.there(move, settle)
+
+    def drain(self, i):
+        for step in range(self.depth):
+            for move in self.moves(step):
+
+                def settle(move=move):
+                    self.across(i, move, 0).wait_send()
+                    self.across(i, move, 1).wait_send()
+                    self.along_y(i, move).wait_send()
+                    for ahead in (1, -1):
+                        if move * ahead <= 0:
+                            self.there(
+                                ahead, lambda ahead=ahead: self.along_z(i, move, ahead).wait_send()
+                            )
+
+                self.there(move, settle)
+
+
 def gather_kernel(depth, parts, count, *refs):
     shards, normed, cot = refs[:count], refs[count], refs[count + 1]
-    weights, normed_all, cot_all = refs[count + 2 : 2 * count + 2], refs[-11], refs[-10]
-    z_sent, z_got, y_sent, y_got, c_sent, c_got, x_sent, x_got, kept = refs[-9:]
+    weights = refs[count + 2 : 2 * count + 2]
+    normed_all, cot_all, x_sent, x_got, kept = refs[2 * count + 2 : 2 * count + 7]
     me, part, z, y, core, dp_of, mp_of = place(depth, parts)
+    work = Gather(depth, parts, shards, weights, refs[2 * count + 7 :])
     own = [
-        pltpu.make_async_copy(shard, whole.at[me], kept.at[i])
-        for i, (shard, whole) in enumerate(zip(shards, weights))
+        pltpu.make_async_copy(normed, normed_all.at[part], kept.at[0]),
+        pltpu.make_async_copy(cot, cot_all.at[part], kept.at[1]),
     ]
-    own.append(pltpu.make_async_copy(normed, normed_all.at[part], kept.at[count]))
-    own.append(pltpu.make_async_copy(cot, cot_all.at[part], kept.at[count + 1]))
-    for copy in own:
-        copy.start()
     greet(depth, parts)
-    other_y, other_core = (dp_of(0, 1 - y, core), part), (dp_of(0, y, 1 - core), part)
-    steps = [(step, i) for step in range(depth) for i in range(count)]
-
-    along_z = [
-        send(shards[i], weights[i].at[me], (z_sent, z_got), n, (dp_of(step, y, core), part))
-        for n, (step, i) in enumerate(steps[count:])
-    ]
     along_x = [
         send(source, target.at[part], (x_sent, x_got), i * (parts - 1) + step - 1,
              (me, mp_of(step)))
         for i, (source, target) in enumerate(((normed, normed_all), (cot, cot_all)))
         for step in range(1, parts)
     ]
-
-    def block(step, i, at_y):
-        return weights[i].at[dp_of(depth - step, at_y, core)]
-
-    along_y, here_across, there_across = [], [], []
-    for n, (step, i) in enumerate(steps):
-        source = shards[i] if step == 0 else block(step, i, y)
-        along_y.append(send(source, block(step, i, y), (y_sent, y_got), n, other_y))
-        here_across.append(
-            send(source, block(step, i, y), (c_sent, c_got), 2 * n, other_core)
-        )
-        there_across.append(
-            send(block(step, i, 1 - y), block(step, i, 1 - y), (c_sent, c_got), 2 * n + 1,
-                 other_core)
-        )
-    for copy in along_z:
+    for i in range(count):
+        work.begin(i)
+    for copy in along_x + own:
         copy.start()
-    for copy in along_y[:count] + here_across[:count]:
-        copy.start()
-    for copy in along_x:
-        copy.start()
-    for n in range(count, len(steps)):
-        along_z[n - count].wait_recv()
-        along_y[n].start()
-        here_across[n].start()
-    for n in range(len(steps)):
-        along_y[n].wait_recv()
-        there_across[n].start()
-    for copy in along_x:
+    for step in range(1, depth):
+        for i in range(count):
+            work.from_z(i, step)
+        for i in range(count):
+            work.from_y(i, step - 1)
+    for i in range(count):
+        work.from_y(i, depth - 1)
+    for copy in along_x + own:
         copy.wait()
-    for copy in along_z + along_y:
-        copy.wait_send()
-    for copy in here_across + there_across:
-        copy.wait()
-    for copy in own:
-        copy.wait()
+    for i in range(count):
+        work.end(i)
+    for i in range(count):
+        work.drain(i)
 
 
 def gather_attn(shards, normed, cot):
@@ -200,10 +291,10 @@
         functools.partial(gather_kernel, depth, parts, count),
         out_shape=[jax.ShapeDtypeStruct((size,) + shard.shape, shard.dtype) for shard in shards]
         + [jax.ShapeDtypeStruct((parts,) + rows.shape, rows.dtype) for rows in (normed, cot)],
-        in_specs=[ANY_SPEC] * (count + 2),
+        in_specs=[VMEM_SPEC] * (count + 2),
         out_specs=[ANY_SPEC] * (count + 2),
-        scratch_shapes=[DMA((count * (depth - 1),))] * 2 + [DMA((count * depth,))] * 2
-        + [DMA((2 * count * depth,))] * 2 + [DMA((2 * (parts - 1),))] * 2 + [DMA((count + 2,))],
+        scratch_shapes=[DMA((2 * (parts - 1),))] * 2 + [DMA((2,))]
+        + Gather.semaphores(depth, count),
         compiler_params=pltpu.CompilerParams(collective_id=0, has_side_effects=True),
         name="gather_attn",
     )(*shards, normed, cot)
@@ -472,6 +563,7 @@
         mlp.cross(n)
     mlp.onward(0)
     mlp.onward(1)
+    mlp.onward(2)
     for copy in to_branch:
         copy.wait()
     for copy in loads[3:7]:
@@ -495,13 +587,13 @@
 
     q_block = 256 if group <= 1024 else 128
 
-    def one_kv_head(j, carry):
-        kv_rows = pl.ds(pl.multiple_of(j * HEAD_SIZE, 32), HEAD_SIZE)
+    def one_kv_head(j):
+        kv_rows = slice(j * HEAD_SIZE, (j + 1) * HEAD_SIZE)
         key_acc[...] = jnp.zeros_like(key_acc)
         value_acc[...] = jnp.zeros_like(value_acc)
         for member in range(members):
-            first = pl.multiple_of((j * members + member) * HEAD_SIZE, 32)
-            head = pl.ds(first, HEAD_SIZE)
+            first = (j * members + member) * HEAD_SIZE
+            head = slice(first, first + HEAD_SIZE)
             for start in range(0, group, q_block):
                 stop = start + q_block
                 cols = slice(start, stop)
@@ -530,22 +622,25 @@
                 )
                 lead, tail = dquery[:half], dquery[half:]
                 cos, sin = cosine[:, cols], sine[:, cols]
-                grad_t[pl.ds(first, half), cols] = (lead * cos + tail * sin).astype(BF16)
-                grad_t[pl.ds(first + half, half), cols] = (tail * cos - lead * sin).astype(BF16)
+                grad_t[first : first + half, cols] = (lead * cos + tail * sin).astype(BF16)
+                grad_t[first + half : first + HEAD_SIZE, cols] = (tail * cos - lead * sin).astype(BF16)
         lead, tail = key_acc[:half] * scale, key_acc[half:] * scale
         cos, sin = cosine[...], sine[...]
-        first = pl.multiple_of(q_width + j * HEAD_SIZE, 32)
-        grad_t[pl.ds(first, half), :] = (lead * cos + tail * sin).astype(BF16)
-        grad_t[pl.ds(first + half, half), :] = (tail * cos - lead * sin).astype(BF16)
-        first = pl.multiple_of(q_width + kv_width + j * HEAD_SIZE, 32)
-        grad_t[pl.ds(first, HEAD_SIZE), :] = value_acc[...].astype(BF16)
-        return carry
-
-    cut = (kv_heads + 1) // 2
-    lax.fori_loop(0, cut, one_kv_head, 0)
-    mlp.onward(2)
-    lax.fori_loop(cut, kv_heads, one_kv_head, 0)
-    mlp.onward(3)
+        first = q_width + j * HEAD_SIZE
+        grad_t[first : first + half, :] = (lead * cos + tail * sin).astype(BF16)
+        grad_t[first + half : first + HEAD_SIZE, :] = (tail * cos - lead * sin).astype(BF16)
+        first = q_width + kv_width + j * HEAD_SIZE
+        grad_t[first : first + HEAD_SIZE, :] = value_acc[...].astype(BF16)
+
+    done = 3
+    if done < items:
+        mlp.onward(done)
+        done += 1
+    for j in range(kv_heads):
+        one_kv_head(j)
+        if done < items:
+            mlp.onward(done)
+            done += 1
 
     def turn_back(i, carry):
         here = pl.ds(pl.multiple_of(i * 128, 128), 128)
@@ -599,7 +694,6 @@
         put(jnp.dot(branch_t[lines, :], attended[...], preferred_element_type=F32), all_width)
         attn.items[n][4].start()
 
-    done = 4
     for n in range(depth):
         weight_block(n)
         if n >= 1:

time: 449 us -> 421 us (0.938)
  Pallas kernels: 254 us -> 226 us
    pallas_call x1, Pallas kernels: 62.8 us -> 45.4 us  [gather_attn(): pl.pallas_call(functools.partial(gather_kernel, depth, parts, count), out...]
    pallas_call x1, Pallas kernels: 191 us -> 181 us  [backward(): pl.pallas_call(functools.partial(backward_kernel, depth, parts, heads, kv...]
  transfers between devices with their start and end apart: 3 -> 3, of which waited for: 3 -> 3; matrix products, arithmetic and copies ran while one was open for 10% -> 11% of each run, Pallas kernels for 0% -> 0%
where the time goes in v4:
time: 421 us; the launch traced here: 412 us
  Pallas kernels  226 us (54%)
  matrix products  68.1 us (16%)
  waiting for transfers between devices  48.8 us (12%)
  local copies, waits for them, and re-layouts  32.4 us (8%)
  other arithmetic  18.4 us (4%)
  between operations  16.9 us (4%)
    pallas_call x1, Pallas kernels, backward(): pl.pallas_call(functools.partial(backward_kernel, depth, parts, heads, kv...  181 us
    pallas_call x1, Pallas kernels, gather_attn(): pl.pallas_call(functools.partial(gather_kernel, depth, parts, count), out...  45.4 us
    dot_general x6, matrix products, mul(): return jnp.dot(left, right, preferred_element_type=F32)  28.4 us
    ppermute x2, waiting for transfers between devices, mp_shift(): lax.ppermute(block, 'mp', [(i, (i + step) % parts) for i in range(parts)])  26.8 us
    all_gather x1, waiting for transfers between devices, shards(): mlp_w = lax.all_gather(mlp_shard, 'dp', axis=0, tiled=True)  21.9 us
    dot_general x3, matrix products, outer_sum(): lax.dot_general(left, right, (((0,), (0,)), ((), ())), preferred_element_...  16.3 us
    dot_general x4, matrix products, mul_t(): lax.dot_general(left, right, (((1,), (1,)), ((), ())), preferred_element_...  13.4 us
    unnamed x67, local copies, waits for them, and re-layouts  8.64 us
  transfers between devices with their start and end apart: 3, of which 3 were waited for; matrix products, arithmetic and copies ran while one was open for 11% of the time, Pallas kernels for 0%

profile of v4, /device:TPU:24, one launch (start us, length us, event | category | flops | bytes accessed | tf_op | source)
XLA Modules:
  0.0 412.4 jit_solution(6437007558923684814)
XLA Ops:
  7.3 1.5 fusion.22
  9.5 2.3 fusion.24.refs_2_
  12.5 1.1 pad_maximum_fusion
  13.6 45.4 %gather_attn.1 = (bf16[16,96,1536]{2,1,0:T(8,128)(2,1)}, bf16[16,96,768]{2,1,0:T(8,128)(2,1)}, bf16[2,256,1536]{2,1,0:T(8,128)(2,1)}, bf16[2,256,1536]{2,1,0:T(8,128)(2,1)}) custom-call(bf16[96,1536]{1,0:T(8,128)(2,1)} %pad_maximum_fusion.9.refs_0_, bf16[96,768]{1,0:T(8,128)(2,1)} %bitcast.118, bf16[256,1536]{1,0:T(8,128)(2,1)} %fusion.24.refs_2_, ...), custom_call_target="tpu_custom_call" | custom-call | tf_op jit(solution)/shard_map/gather_attn/pallas_call | solution.py:290
  59.1 1.4 slice_bitcast_fusion.1
  61.1 1.8 slice_bitcast_fusion
  62.9 2.5 copy.33
  70.0 2.4 fusion.52
  72.6 1.4 fusion.53
  74.3 2.1 convolution_convert_fusion.3
  76.4 5.5 %fusion.47 = (f32[4,2,512]{2,1,0:T(2,128)S(1)}, f32[4,2,512,512]{2,3,1,0:T(8,128)}) fusion(pred[512,512]{0,1:T(8,128)(4,1)S(1)} %fusion.28, bf16[512,4,2,48]{0,3,2,1:T(8,128)(2,1)S(1)} %bitcast.110, bf16[512,4,2,48]{0,3,2,1:T(8,128)(2,1)S(1)} %bitcast.109, bf16[512,4,48]{0,2,1:T(8,128)(2,1)S(1)} %get-tuple-element.49, ...), kind=kOutput, calls=%fused_computation.101 | convolution fusion | flops 413401600 | bytes 9846784 | tf_op jit(solution)/shard_map/sub | solution.py:883
  81.9 4.5 %fusion.25 = bf16[4,96,2,512]{3,1,2,0:T(8,128)(2,1)S(1)} fusion(bf16[512,4,96,1]{0,2,3,1:T(8,128)(2,1)S(1)} %bitcast.115, f32[4,2,512,512]{2,3,1,0:T(8,128)} %get-tuple-element.62, f32[4,2,512]{2,1,0:T(2,128)S(1)} %get-tuple-element.61), kind=kOutput, calls=%fused_computation.42 | convolution fusion | flops 407240704 | bytes 9584640 | tf_op jit(solution)/shard_map/hgqk,khd->qhgd/dot_general | solution.py:887
  86.5 1.4 fusion.54
  87.9 1.7 copy-done.4
  89.6 1.0 dynamic-slice_convert_fusion.2
  91.4 19.5 %collective-permute-done = bf16[256,1536]{1,0:T(8,128)(2,1)} collective-permute-done((bf16[256,1536]{1,0:T(8,128)(2,1)}, bf16[256,1536]{1,0:T(8,128)(2,1)}, u32[]{:S(2)}, u32[]{:S(2)}) %collective-permute-start) | collective-permute-done | bytes 786464 | tf_op jit(solution)/shard_map/ppermute | solution.py:64
  110.9 2.0 multiply_reduce_fusion
  113.1 1.3 constant_dynamic-update-slice_fusion.1
  114.4 1.1 copy-done.6
  115.5 1.0 collective-permute-start.1
  117.8 2.0 copy.42
  119.8 2.4 copy.36.refs_18_
  122.2 1.2 compare_select_fusion.1.refs_20_
  123.5 1.4 compare_select_fusion.refs_19_
  125.7 0.9 pad_maximum_fusion.2
  126.7 1.1 multiply_sine_fusion
  127.8 7.3 %collective-permute-done.1 = bf16[256,1536]{1,0:T(8,128)(2,1)} collective-permute-done((bf16[256,1536]{1,0:T(8,128)(2,1)}, bf16[256,1536]{1,0:T(8,128)(2,1)}, u32[]{:S(2)}, u32[]{:S(2)}) %collective-permute-start.1) | collective-permute-done | bytes 786464 | tf_op jit(solution)/shard_map/ppermute | solution.py:64
  135.1 1.2 constant_dynamic-update-slice_fusion
  136.3 21.9 %all-gather.2.cloned.1.call-done = bf16[1536,6144]{1,0:T(8,128)(2,1)} async-done(((bf16[96,6144]{1,0:T(8,128)(2,1)}), bf16[1536,6144]{1,0:T(8,128)(2,1)}) %all-gather.2.cloned.1.call-update) | async-done | bytes 18874384 | tf_op jit(solution)/shard_map/all_gather | solution.py:859
  158.2 9.0 %fusion.12 = f32[512,2048]{1,0:T(8,128)} fusion(bf16[512,1536]{1,0:T(8,128)(2,1)} %bitcast.119, bf16[1536,6144]{1,0:T(8,128)(2,1)} %all-gather.2.cloned.1.call-done), kind=kOutput, calls=%fused_computation.18 | convolution fusion | flops 3221225472 | bytes 12058624 | tf_op jit(solution)/shard_map/dot_general | solution.py:52
  167.2 1.2 copy-done.26
  168.4 5.1 %fusion.4 = f32[512,2048]{1,0:T(8,128)} fusion(bf16[512,1536]{1,0:T(8,128)(2,1)S(1)} %constant_dynamic-update-slice_fusion, bf16[1536,6144]{1,0:T(8,128)(2,1)S(1)} %copy-done.26), kind=kOutput, calls=%fused_computation.10 | convolution fusion | flops 3221225472 | bytes 12058624 | tf_op jit(solution)/shard_map/dot_general | solution.py:52
  173.5 8.5 %multiply_convert_fusion = (bf16[512,2048]{1,0:T(8,128)(2,1)S(1)}, bf16[512,2048]{1,0:T(8,128)(2,1)S(1)}, bf16[512,2048]{1,0:T(8,128)(2,1)}) fusion(f32[512,2048]{1,0:T(8,128)} %fusion.4, f32[512,2048]{1,0:T(8,128)} %fusion.12, bf16[512,1536]{1,0:T(8,128)(2,1)S(1)} %constant_dynamic-update-slice_fusion, bf16[1536,6144]{1,0:T(8,128)(2,1)S(1)} %copy-done.26), kind=kOutput, calls=%fused_computation.20 | convolution fusion | flops 3236954112 | bytes 22544384 | tf_op jit(solution)/shard_map/dot_general | solution.py:52
  181.9 3.5 fusion.10
  185.4 1.0 fusion.33.refs_6_
  186.4 1.2 constant_dynamic-slice_fusion.refs_5_
  187.6 5.6 %convolution_convert_fusion = bf16[1536,2048]{1,0:T(8,128)(2,1)} fusion(bf16[512,1536]{1,0:T(8,128)(2,1)S(1)} %bitcast.120, bf16[512,2048]{1,0:T(8,128)(2,1)S(1)} %get-tuple-element.43), kind=kOutput, calls=%fused_computation.4 | convolution fusion | flops 3224371200 | bytes 9961472 | tf_op jit(solution)/shard_map/dot_general | solution.py:60
  193.2 3.5 fusion.2
  196.7 5.1 %fusion.19 = f32[512,1536]{1,0:T(8,128)S(1)} fusion(f32[512,1536]{1,0:T(8,128)S(1)} %fusion.2, bf16[512,2048]{1,0:T(8,128)(2,1)} %get-tuple-element.45, bf16[1536,6144]{1,0:T(8,128)(2,1)S(1)} %copy-done.26), kind=kOutput, calls=%fused_computation.29 | convolution fusion | flops 3222011904 | bytes 14680064 | tf_op jit(solution)/shard_map/dot_general | solution.py:56
  201.8 1.0 fusion.32.refs_4_
  202.7 1.3 constant_dynamic-slice_fusion.1.refs_3_
  204.0 5.4 %convolution_convert_fusion.1 = bf16[1536,2048]{1,0:T(8,128)(2,1)} fusion(bf16[512,1536]{1,0:T(8,128)(2,1)S(1)} %constant_dynamic-update-slice_fusion, bf16[512,2048]{1,0:T(8,128)(2,1)S(1)} %copy-done.30), kind=kOutput, calls=%fused_computation.5 | convolution fusion | flops 3224371200 | bytes 9961472 | tf_op jit(solution)/shard_map/dot_general | solution.py:60
  209.4 5.4 %convolution_convert_fusion.2 = bf16[1536,2048]{1,0:T(8,128)(2,1)} fusion(bf16[512,1536]{1,0:T(8,128)(2,1)S(1)} %constant_dynamic-update-slice_fusion, bf16[512,2048]{1,0:T(8,128)(2,1)S(1)} %copy-done.29), kind=kOutput, calls=%fused_computation.6 | convolution fusion | flops 3224371200 | bytes 9961472 | tf_op jit(solution)/shard_map/dot_general | solution.py:60
  214.8 180.6 %backward.1 = (f32[96,2048]{1,0:T(8,128)}, f32[96,2048]{1,0:T(8,128)}, f32[96,2048]{1,0:T(8,128)}, f32[96,2304]{1,0:T(8,128)}, bf16[256,1536]{1,0:T(8,128)(2,1)}...) custom-call(bf16[4,2,2,96,2048]{4,3,2,1,0:T(8,128)(2,1)} %bitcast.99, ...), custom_call_target="tpu_custom_call" | custom-call | tf_op jit(solution)/shard_map/backward/pallas_call | solution.py:776
  395.3 1.8 fusion.45
  397.2 2.0 slice_bitcast_fusion.2
  399.1 0.9 bitcast_reduce_fusion
  402.5 0.9 copy.52
  (85 shorter events, 12.4 us)
Async XLA Ops:
  7.2 4.5 %copy-start.19 = (bf16[96,384]{1,0:T(8,128)(2,1)S(1)}, bf16[96,384]{1,0:T(8,128)(2,1)}, u32[]{:S(2)}) copy-start(bf16[96,384]{1,0:T(8,128)(2,1)} %param.17) | copy-start | bytes 221188
  7.2 4.5 %copy-start.20 = (bf16[96,384]{1,0:T(8,128)(2,1)S(1)}, bf16[96,384]{1,0:T(8,128)(2,1)}, u32[]{:S(2)}) copy-start(bf16[96,384]{1,0:T(8,128)(2,1)} %param.16) | copy-start | bytes 221188
  7.2 4.5 %copy-start.18 = (bf16[96,768]{1,0:T(8,128)(2,1)S(1)}, bf16[96,768]{1,0:T(8,128)(2,1)}, u32[]{:S(2)}) copy-start(bf16[96,768]{1,0:T(8,128)(2,1)} %param.15) | copy-start | bytes 442372
  7.2 5.3 %copy-start.15 = (bf16[2048,96]{0,1:T(8,128)(2,1)S(1)}, bf16[2048,96]{0,1:T(8,128)(2,1)}, u32[]{:S(2)}) copy-start(bf16[2048,96]{0,1:T(8,128)(2,1)} %param.22) | copy-start | bytes 1179652
  7.2 5.3 %copy-start.16 = (bf16[96,2048]{1,0:T(8,128)(2,1)S(1)}, bf16[96,2048]{1,0:T(8,128)(2,1)}, u32[]{:S(2)}) copy-start(bf16[96,2048]{1,0:T(8,128)(2,1)} %param.21) | copy-start | bytes 1179652
  7.2 5.2 %copy-start.17 = (bf16[96,2048]{1,0:T(8,128)(2,1)S(1)}, bf16[96,2048]{1,0:T(8,128)(2,1)}, u32[]{:S(2)}) copy-start(bf16[96,2048]{1,0:T(8,128)(2,1)} %param.20) | copy-start | bytes 1179652
  7.2 151.0 %all-gather.2.cloned.1.call-start = ((), (), s32[]{:S(2)}) async-start(), calls=%async_computation | async-start | bytes 20054016 | tf_op jit(solution)/shard_map/all_gather | solution.py:859
  62.9 2.5 copy-start.23
  68.0 4.4 %copy-start.24 = (f32[48]{0:T(128)}, f32[48]{0:T(128)S(1)}, u32[]{:S(2)}) copy-start(f32[48]{0:T(128)S(1)} %multiply_power_fusion) | copy-start | bytes 580
  70.0 2.5 copy-start.3
  70.0 2.6 copy-start.5
  76.4 5.5 %copy-start.14 = (bf16[512,384]{0,1:T(8,128)(2,1)}, bf16[512,384]{0,1:T(8,128)(2,1)S(1)}, u32[]{:S(2)}) copy-start(bf16[512,384]{0,1:T(8,128)(2,1)S(1)} %convolution_convert_fusion.3) | copy-start | bytes 1179652
  81.9 4.5 %copy-start.2 = (bf16[16,96,768]{2,1,0:T(8,128)(2,1)S(1)}, bf16[16,96,768]{2,1,0:T(8,128)(2,1)}, u32[]{:S(2)}) copy-start(bf16[16,96,768]{2,1,0:T(8,128)(2,1)} %get-tuple-element.27) | copy-start | bytes 7077892
  86.4 4.1 %copy-start.8 = (bf16[4,96,2,512]{3,1,2,0:T(8,128)(2,1)}, bf16[4,96,2,512]{3,1,2,0:T(8,128)(2,1)S(1)}, u32[]{:S(2)}) copy-start(bf16[4,96,2,512]{3,1,2,0:T(8,128)(2,1)S(1)} %fusion.25) | copy-start | bytes 2359300
  86.5 5.0 %copy-start.22 = (bf16[1536]{0:T(1024)(128)(2,1)S(1)}, bf16[1536]{0:T(1024)(128)(2,1)}, u32[]{:S(2)}) copy-start(bf16[1536]{0:T(1024)(128)(2,1)} %param.19) | copy-start | bytes 9220
  87.9 1.7 copy-start.4
  89.6 21.3 %copy-start.1 = (bf16[256,1536]{1,0:T(8,128)(2,1)S(1)}, bf16[256,1536]{1,0:T(8,128)(2,1)}, u32[]{:S(2)}) copy-start(bf16[256,1536]{1,0:T(8,128)(2,1)} %refs_9_.1) | copy-start | bytes 2359300
  90.6 20.3 %collective-permute-start = (bf16[256,1536]{1,0:T(8,128)(2,1)}, bf16[256,1536]{1,0:T(8,128)(2,1)}, u32[]{:S(2)}, u32[]{:S(2)}) collective-permute-start(bf16[256,1536]{1,0:T(8,128)(2,1)} %dynamic-slice_convert_fusion.2), channel_id=1, source_target_pairs={{0,1},{1,0},{2,3},{3,2},{4,5},{5,4},{6,7},{7,6},{8,9},{9,8},{10,11... | collective-permute-start | bytes 2359304 | tf_op jit(solution)/shard_map/ppermute | solution.py:64
  113.0 1.4 copy-start
  113.0 3.6 copy-start.21
  114.4 1.1 copy-start.6
  115.5 19.6 %collective-permute-start.1 = (bf16[256,1536]{1,0:T(8,128)(2,1)}, bf16[256,1536]{1,0:T(8,128)(2,1)}, u32[]{:S(2)}, u32[]{:S(2)}) collective-permute-start(bf16[256,1536]{1,0:T(8,128)(2,1)} %get-tuple-element.40), channel_id=1, source_target_pairs={{0,1},{1,0},{2,3},{3,2},{4,5},{5,4},{6,7},{7,6},{8,9},{9,8},{10,11... | collective-permute-start | bytes 2359304 | tf_op jit(solution)/shard_map/ppermute | solution.py:64
  119.8 6.9 %copy-start.25 = (f32[48]{0:T(128)S(1)}, f32[48]{0:T(128)}, u32[]{:S(2)}) copy-start(f32[48]{0:T(128)} %copy-done.24) | copy-start | bytes 580
  119.8 15.3 %copy-start.7 = (bf16[512,1536]{1,0:T(8,128)(2,1)S(1)}, bf16[512,1536]{1,0:T(8,128)(2,1)}, u32[]{:S(2)}) copy-start(bf16[512,1536]{1,0:T(8,128)(2,1)} %copy-done.6) | copy-start | bytes 4718596
  158.2 10.2 %copy-start.26 = (bf16[1536,6144]{1,0:T(8,128)(2,1)S(1)}, bf16[1536,6144]{1,0:T(8,128)(2,1)}, u32[]{:S(2)}) copy-start(bf16[1536,6144]{1,0:T(8,128)(2,1)} %all-gather.2.cloned.1.call-done) | copy-start | bytes 56623108
  181.9 11.3 %copy-start.28 = (bf16[512,2048]{1,0:T(8,128)(2,1)}, bf16[512,2048]{1,0:T(8,128)(2,1)S(1)}, u32[]{:S(2)}) copy-start(bf16[512,2048]{1,0:T(8,128)(2,1)S(1)} %get-tuple-element.44) | copy-start | bytes 6291460
  185.4 2.2 copy-start.27
  201.7 2.3 copy-start.30
  204.0 5.4 %copy-start.29 = (bf16[512,2048]{1,0:T(8,128)(2,1)S(1)}, bf16[512,2048]{1,0:T(8,128)(2,1)}, u32[]{:S(2)}) copy-start(bf16[512,2048]{1,0:T(8,128)(2,1)} %copy-done.28) | copy-start | bytes 6291460
  395.3 5.4 %copy-start.13 = (bf16[256,1536]{1,0:T(8,128)(2,1)S(1)}, bf16[256,1536]{1,0:T(8,128)(2,1)}, u32[]{:S(2)}) copy-start(bf16[256,1536]{1,0:T(8,128)(2,1)} %get-tuple-element.76) | copy-start | bytes 2359300
  395.3 6.3 %copy-start.12 = (bf16[256,1536]{1,0:T(8,128)(2,1)S(1)}, bf16[256,1536]{1,0:T(8,128)(2,1)}, u32[]{:S(2)}) copy-start(bf16[256,1536]{1,0:T(8,128)(2,1)} %get-tuple-element.77) | copy-start | bytes 2359300
  397.2 5.3 %copy-start.11 = (f32[96,2048]{1,0:T(8,128)S(1)}, f32[96,2048]{1,0:T(8,128)}, u32[]{:S(2)}) copy-start(f32[96,2048]{1,0:T(8,128)} %get-tuple-element.84) | copy-start | bytes 2359300
  400.7 2.7 copy-start.10
  401.6 2.6 copy-start.9
Sparse Core Ops, SparseCore 0:
  59.2 98.9 all-gather.1

commit v5 on v4

--- a/solution.py
+++ b/solution.py
@@ -103,6 +103,22 @@
         return lax.rem(part + step, parts)
 
     return me, part, z, y, core, dp_of, mp_of
+
+
+def flipped(value, mask):
+    result = value
+    for bit in (1 << i for i in range(mask.bit_length())):
+        if mask & bit:
+            result = result + bit * (1 - 2 * lax.rem(value // bit, 2))
+    return result
+
+
+def lowest(mask):
+    return mask & -mask
+
+
+def masks(depth):
+    return sorted(range(1, depth), key=lambda m: (lowest(m), -m)) + [0]
 
 
 def greet(depth, parts):
@@ -312,106 +328,190 @@
     lax.fori_loop(0, target.shape[0] // 16, body, 0)
 
 
-SLOTS = 2
+class Ring:
+    def __init__(self, buffer):
+        self.buffer, self.users, self.next = buffer, [None] * buffer.shape[0], 0
+
+    def take(self, copy):
+        slot = self.next
+        if self.users[slot] is not None:
+            self.users[slot].wait_send()
+        self.users[slot] = copy
+        self.next = (slot + 1) % len(self.users)
+
+    def peek(self, ahead):
+        return (self.next + ahead) % len(self.users)
+
+    def drain(self):
+        for copy in self.users:
+            if copy is not None:
+                copy.wait_send()
 
 
 class Sums:
-    def __init__(self, depth, parts, wholes, outs, scratch):
-        self.depth, self.wholes, self.outs = depth, wholes, outs
-        count = len(outs)
-        self.held, self.ring, self.y_in, self.z_in = (
-            scratch[i * count : (i + 1) * count] for i in range(4)
-        )
-        self.sems = scratch[4 * count :]
-        self.order = [(step, k) for step in range(1, depth + 1) for k in range(count)]
+    def __init__(self, depth, parts, order, widths, rows, refs, wholes, ring, start, outs):
+        self.depth, self.wholes, self.outs, self.order = depth, wholes, outs, order
+        self.rows, self.widths, self.ring = rows, widths, ring
+        count = len(widths)
+        self.held = refs[:count]
+        self.y_in, self.z_in = refs[count : 2 * count], refs[2 * count : 3 * count]
+        self.y_tile, self.z_tile, self.stage = refs[3 * count : 3 * count + 3]
+        self.sems = refs[3 * count + 3 :]
         self.where = place(depth, parts)
-        self.items = [self.item(n) for n in range(len(self.order))]
+        slots = len(ring.users)
+        self.slots = [(start + n) % slots for n in range(len(order))]
+        self.items = [self.item(n) for n in range(len(order))]
+        self.crossed = self.passed = 0
+        self.pending = self.putting = None
 
     @staticmethod
-    def scratch(depth, blocks, computed):
-        count = len(blocks)
-        lead = (SLOTS, 2, 2) if computed else (SLOTS, 2)
-        buffers = [pltpu.VMEM((depth, 2) + block, BF16) for block in blocks]
-        buffers += [pltpu.VMEM(lead + block, BF16) for block in blocks]
-        buffers += [pltpu.VMEM((depth,) + block, BF16) for block in blocks]
-        buffers += [pltpu.VMEM((depth - 1,) + block, BF16) for block in blocks]
-        return buffers + [DMA((depth * count,))] * 7
+    def held_shapes(depth, widths, rows):
+        return [pltpu.VMEM((depth, 2, rows, width), BF16) for width in widths]
+
+    @staticmethod
+    def landing_shapes(depth, widths, rows):
+        return [jax.ShapeDtypeStruct((depth, rows, width), BF16) for width in widths] + [
+            jax.ShapeDtypeStruct((depth - 1, rows, width), BF16) for width in widths
+        ]
+
+    @staticmethod
+    def tiles(depth, widths, rows):
+        wide = max(widths)
+        return [
+            pltpu.VMEM((rows, wide), BF16),
+            pltpu.VMEM((depth - 1, rows, wide), BF16),
+            pltpu.VMEM((rows, wide), F32),
+        ] + [DMA((depth * len(widths),))] * 7 + [DMA((depth + 2,))]
 
     def item(self, n):
-        step, k = self.order[n]
+        k, mask = self.order[n]
         me, part, z, y, core, dp_of, mp_of = self.where
-        at = lax.rem(z + step, self.depth)
-        kept, c_sent, c_got, y_sent, y_got, z_sent, z_got = self.sems
-        held, slot = self.held[k], (n // len(self.outs)) % SLOTS
+        at = flipped(z, mask)
+        kept, c_sent, c_got, y_sent, y_got, z_sent, z_got, moved = self.sems
+        held, width = self.held[k], self.widths[k]
+        every, slot = pl.ds(0, width), self.slots[n]
         own = None
         if self.wholes is None:
-            mine = self.ring[k].at[slot, :, core]
-            give = self.ring[k].at[slot, :, 1 - core]
+            give = self.ring.buffer.at[slot, :, 1 - core, :, every]
         else:
-            mine = self.ring[k].at[slot]
             give = self.wholes[k].at[at, :, 1 - core]
-            own = pltpu.make_async_copy(self.wholes[k].at[at, :, core], mine, kept.at[n])
+            own = pltpu.make_async_copy(
+                self.wholes[k].at[at, :, core], self.ring.buffer.at[slot], kept.at[n]
+            )
         across = send(give, held.at[at], (c_sent, c_got), n, (dp_of(0, y, 1 - core), part))
         along_y = send(
             held.at[at, 1 - y], self.y_in[k].at[at], (y_sent, y_got), n,
             (dp_of(0, 1 - y, core), part),
         )
         along_z = None
-        if step < self.depth:
+        if mask > 0:
             along_z = send(
-                held.at[at, y], self.z_in[k].at[step - 1], (z_sent, z_got), n,
-                (dp_of(step, y, core), part),
+                held.at[at, y], self.z_in[k].at[mask - 1], (z_sent, z_got), n,
+                (flipped(z, lowest(mask)) * 4 + y * 2 + core, part),
             )
-        return at, k, slot, own, across, along_y, along_z
+        return at, k, own, across, along_y, along_z
 
     def load(self, n):
-        self.items[n][3].start()
-        self.items[n][4].start()
+        at, k, own, across, along_y, along_z = self.items[n]
+        self.ring.take(across)
+        own.start()
+        across.start()
 
     def begin(self):
-        self.ahead = SLOTS * len(self.outs)
-        for n in range(min(self.ahead, len(self.items))):
+        self.ahead = min(len(self.ring.users), len(self.items))
+        for n in range(self.ahead):
             self.load(n)
 
-    def cross(self, n):
+    def slot_for(self, n):
+        self.ring.take(self.items[n][3])
+        return self.ring.buffer.at[self.slots[n]]
+
+    def cross(self):
         core = self.where[4]
-        at, k, slot, own, across, along_y, along_z = self.items[n]
+        n = self.crossed
+        self.crossed += 1
+        at, k, own, across, along_y, along_z = self.items[n]
         if own is not None:
             own.wait()
         across.wait_recv()
         for at_y in range(2):
             if own is not None:
-                mine = self.ring[k].at[slot, at_y]
+                mine = self.ring.buffer.at[self.slots[n], at_y]
             else:
-                mine = self.ring[k].at[slot, at_y, core]
-            add_rows(self.held[k].at[at, at_y], (mine, self.held[k].at[at, at_y]))
+                mine = self.ring.buffer.at[self.slots[n], at_y, core, :, pl.ds(0, self.widths[k])]
+            held = self.held[k].at[at, at_y]
+            add_rows(held, (mine, held))
         along_y.start()
         if own is not None and n + self.ahead < len(self.items):
             self.load(n + self.ahead)
 
-    def onward(self, n):
-        y = self.where[3]
-        at, k, slot, own, across, along_y, along_z = self.items[n]
+    def onward(self):
+        self.settle()
+        n = self.passed
+        if n >= self.crossed:
+            return
+        self.passed += 1
+        moved = self.sems[7]
+        at, k, own, across, along_y, along_z = self.items[n]
+        mask, every = self.order[n][1], pl.ds(0, self.widths[k])
         along_y.wait_recv()
-        held = self.held[k].at[at, y]
-        add_rows(held, (held, self.y_in[k].at[at]))
+        tile = self.y_tile.at[:, every]
+        fetches = [pltpu.make_async_copy(self.y_in[k].at[at], tile, moved.at[0])]
+        fetches[0].start()
+        tiles_in = [tile]
+        if mask > 0:
+            more, from_z = self.from_z(k, mask)
+            fetches += more
+            tiles_in += from_z
+        self.pending = n, fetches, tiles_in
+
+    def settle(self):
+        if self.pending is None:
+            return
+        n, fetches, landed = self.pending
+        self.pending = None
+        at, k, own, across, along_y, along_z = self.items[n]
+        for fetch in fetches:
+            fetch.wait()
+        held = self.held[k].at[at, self.where[3]]
+        add_rows(held, [held] + landed)
         if along_z is not None:
             along_z.start()
 
-    def end(self):
+    def from_z(self, k, mask):
+        moved, every = self.sems[7], pl.ds(0, self.widths[k])
+        fetches, landed = [], []
+        bit = 1
+        while bit < (lowest(mask) if mask else self.depth):
+            sender = mask ^ bit
+            self.items[self.order.index((k, sender))][5].wait_recv()
+            tile = self.z_tile.at[len(landed), :, every]
+            fetch = pltpu.make_async_copy(
+                self.z_in[k].at[sender - 1], tile, moved.at[1 + len(landed)]
+            )
+            fetch.start()
+            fetches.append(fetch)
+            landed.append(tile)
+            bit *= 2
+        return fetches, landed
+
+    def finish(self, k):
+        self.settle()
         z, y = self.where[2:4]
-        for k, out in enumerate(self.outs):
-            for item in self.items:
-                if item[1] == k and item[6] is not None:
-                    item[6].wait_recv()
-            add_rows(
-                out, [self.held[k].at[z, y]] + [self.z_in[k].at[i] for i in range(self.depth - 1)]
-            )
-
-    def drain(self, crossed=0):
-        for n, (at, k, slot, own, across, along_y, along_z) in enumerate(self.items):
-            if n >= crossed:
-                across.wait_send()
+        moved, every = self.sems[7], pl.ds(0, self.widths[k])
+        fetches, landed = self.from_z(k, 0)
+        for fetch in fetches:
+            fetch.wait()
+        stage = self.stage.at[:, every]
+        if self.putting is not None:
+            self.putting.wait()
+        add_rows(stage, [self.held[k].at[z, y]] + landed)
+        self.putting = pltpu.make_async_copy(stage, self.outs[k], moved.at[self.depth + 1])
+        self.putting.start()
+
+    def drain(self):
+        self.putting.wait()
+        for at, k, own, across, along_y, along_z in self.items:
             along_y.wait_send()
             if along_z is not None:
                 along_z.wait_send()
@@ -484,63 +584,253 @@
         body(pl.ds(pl.multiple_of(i * tile, tile), tile))
         return carry
 
-    lax.fori_loop(0, rows // tile, run, 0)
-
-
-def backward_kernel(depth, parts, heads, kv_heads, *refs):
-    (gate, up, down, own_two_in, give_two, own_out_in, give_out, residual_in, cot_in, tokens_in,
-     gain_one, gain_two, weights_in, out_w_in, normed_t_in, query_t_in, key_t_in, value_t_in,
-     attended_in, id_col, id_row, cosine, sine) = refs[:23]
-    (gate_out, up_out, down_out, attn_out, block_out, grad_tokens, gains, in_out) = refs[23:31]
-    (work, work_out, residual, cot, tokens, weights, out_w, normed_t, query_t, key_t, value_t,
-     attended, in_x, out_tile, branch, branch_t, grad_t, give_one, key_acc, value_acc, low,
-     held, around, loaded, stored, two_sent, two_got, out_sent, out_got, b_sent, b_got,
-     one_sent, one_got, g_sent, g_got) = refs[31:66]
-    rest = refs[66:]
+    lax.fori_loop(0, rows // tile, run, 0, unroll=4)
+
+
+def dot_nt(left, right):
+    return lax.dot_general(
+        left, right, (((1,), (1,)), ((), ())), preferred_element_type=F32
+    )
+
+
+class Named(dict):
+    __getattr__ = dict.get
+
+
+def backward_kernel(depth, parts, heads, kv_heads, chunks, names, *refs):
+    r = Named(zip(names, refs))
+    rest = refs[len(names) :]
     me, part, z, y, core, dp_of, mp_of = place(depth, parts)
-    rows, width = residual.shape
+    work, work_out, residual = r.work, r.work_out, r.residual
+    branch, branch_t, grad_t = r.branch, r.branch_t, r.grad_t
+    in_x, give_x, low, held = r.in_x, r.give_x, r.low, r.held
+    weights, out_w, normed_t, attended = (
+        r.weights, r.out_w, r.normed_t, r.attended
+    )
+    rows, width = work.shape
     group = rows * parts
     members = heads // kv_heads
     q_width, kv_width = heads * HEAD_SIZE, kv_heads * HEAD_SIZE
     all_width = q_width + 2 * kv_width
     half = HEAD_SIZE // 2
     scale = HEAD_SIZE ** (-0.5)
-    mlp_refs = 4 * 3 + 7
-    mlp = Sums(depth, parts, (gate, up, down), (gate_out, up_out, down_out), rest[:mlp_refs])
-    attn = Sums(depth, parts, None, (attn_out,), rest[mlp_refs:])
-    total_gains = Gains(depth, parts, held, around, (g_sent, g_got))
-
-    pairs = [
-        (own_two_in, work), (residual_in, residual), (cot_in, cot), (out_w_in, out_w),
-        (query_t_in, query_t), (key_t_in, key_t), (value_t_in, value_t), (own_out_in, work_out),
-        (weights_in, weights), (normed_t_in, normed_t), (attended_in, attended),
-        (tokens_in, tokens),
-    ]
-    loads = [pltpu.make_async_copy(a, b, loaded.at[i]) for i, (a, b) in enumerate(pairs)]
-
-    def along_x(source, target, sems):
+    quarter = width // (4 * depth)
+    inside = chunks > 0
+    if inside:
+        weights, out_w = r.wide.at[0], r.wide.at[1, :, pl.ds(0, q_width)]
+        residual = r.others_two.at[0]
+
+    mlp_widths, attn_widths = mlp_and_attn_widths(
+        r, inside, chunks, r.attended_in.shape[1], all_width
+    )
+    count = len(mlp_widths)
+    if inside:
+        mlp_order = [(k, mask) for k in range(count) for mask in masks(depth)]
+        ring = attn_ring = Ring(r.ring)
+        attn_start = len(mlp_order) % len(ring.users)
+        wholes = None
+    else:
+        mlp_order = [(k, mask) for mask in masks(depth) for k in range(count)]
+        ring, attn_ring, attn_start = Ring(r.ring), Ring(r.attn_ring), 0
+        wholes = [r["grad%d" % k] for k in range(count)]
+    attn_order = [(k, mask) for mask in masks(depth) for k in range(2)]
+    mlp_refs = (
+        [r["mlp_held%d" % k] for k in range(count)]
+        + [r["mlp_y%d" % k] for k in range(count)]
+        + [r["mlp_z%d" % k] for k in range(count)]
+        + list(rest[:11])
+    )
+    attn_refs = (
+        [r["attn_held%d" % k] for k in range(2)]
+        + [r["attn_y%d" % k] for k in range(2)]
+        + [r["attn_z%d" % k] for k in range(2)]
+        + list(rest[11:22])
+    )
+    mlp = Sums(depth, parts, mlp_order, mlp_widths, quarter, mlp_refs, wholes, ring, 0,
+               [r["mlp_out%d" % k] for k in range(count)])
+    attn = Sums(depth, parts, attn_order, attn_widths, quarter, attn_refs, None, attn_ring,
+                attn_start, [r["attn_out%d" % k] for k in range(2)])
+    total_gains = Gains(depth, parts, held, r.around, (r.g_sent, r.g_got))
+
+    loading = [0]
+
+    def load(source, target):
+        copy = pltpu.make_async_copy(source, target, r.loaded.at[loading[0]])
+        loading[0] += 1
+        copy.start()
+        return copy
+
+    def wait(copies):
+        for copy in copies:
+            copy.wait()
+
+    def along_x(source, target, name):
+        sems = (r[name + "_sent"], r[name + "_got"])
         return [
             send(source(step), target(step), sems, step - 1, (me, mp_of(step)))
             for step in range(1, parts)
         ]
 
-    to_two = along_x(lambda s: give_two.at[s - 1], lambda s: in_x.at[s - 1], (two_sent, two_got))
-    to_out = along_x(lambda s: give_out.at[s - 1], lambda s: in_out.at[s - 1], (out_sent, out_got))
-    to_branch = along_x(lambda s: branch.at[part], lambda s: branch.at[part], (b_sent, b_got))
-    to_one = along_x(lambda s: give_one.at[s - 1], lambda s: in_x.at[s - 1], (one_sent, one_got))
-
-    greet(depth, parts)
-    for copy in to_two:
-        copy.start()
-    mlp.begin()
-    for copy in loads:
-        copy.start()
-    items = len(mlp.items)
-    early = min(8, items)
-    for n in range(early):
-        mlp.cross(n)
-    for copy in loads[:3]:
-        copy.wait()
+    give_two = give_x if inside else r.give_two
+    give_out = r.give_out_low if inside else r.give_out
+    to_two = along_x(lambda s: give_two.at[s - 1], lambda s: in_x.at[s - 1], "two")
+    to_out = along_x(lambda s: give_out.at[s - 1], lambda s: r.in_out.at[s - 1], "out")
+    to_branch = along_x(lambda s: branch.at[part], lambda s: branch.at[part], "branch")
+    to_one = along_x(lambda s: give_x.at[s - 1], lambda s: in_x.at[s - 1], "one")
+
+    if inside:
+        hidden_width = mlp_widths[0] // 3
+        gate_cols, up_cols, down_cols = (
+            slice(i * hidden_width, (i + 1) * hidden_width) for i in range(3)
+        )
+
+        def load_chunk(k):
+            lanes = pl.ds(k * 3 * hidden_width, 3 * hidden_width)
+            return load(r.mlp_w_in.at[:, lanes], r.wide.at[k % 2])
+
+        def load_part(i):
+            lanes = pl.ds(i * hidden_width, hidden_width)
+            return load(r.mlp_w_in.at[:, lanes], r.wide.at[0, :, lanes])
+
+        first_loads = [load(r.normed_two_in, branch), load_part(0), load_part(1)]
+        next_loads = [load(r.cot_in, r.cot), load_part(2)]
+        block_loads = [load(r.normed_two_t_in, branch_t), load(r.cot_t_in, normed_t)]
+        chunk_loads = [None]
+        if chunks > 1:
+            chunk_loads.append(load_chunk(1))
+        greet(depth, parts)
+        late_loads = [
+            load(r.query_t_in, r.query_t), load(r.key_t_in, r.key_t),
+            load(r.value_t_in, r.value_t), load(r.attended_in, attended),
+            load(r.tokens_in, r.tokens),
+        ]
+        wait(first_loads)
+
+        def add_to(own, others, k, product):
+            for step in range(parts):
+                target = own if step == 0 else others.at[step - 1]
+                value = product(step)
+                if k == 0:
+                    target[...] = value
+                else:
+                    target[...] += value
+
+        hidden, grad_gate, grad_up = r.hidden, r.grad_gate, r.grad_up
+
+        def feed_forward(k):
+            if k > 0:
+                chunk_loads[k].wait()
+            wide = r.wide.at[k % 2]
+            here = slice(k * hidden_width, (k + 1) * hidden_width)
+            for p in range(parts):
+                lines = slice(p * rows, (p + 1) * rows)
+                gate = jnp.dot(branch[p], wide[:, gate_cols], preferred_element_type=F32)
+                up = jnp.dot(branch[p], wide[:, up_cols], preferred_element_type=F32)
+                if k == 0 and p == 0:
+                    wait(next_loads)
+                back = jnp.dot(r.cot[p], wide[:, down_cols], preferred_element_type=F32)
+                sigmoid = 1.0 / (1.0 + jnp.exp(-gate))
+                swish = gate * sigmoid
+                hidden[lines, here] = (swish * up).astype(BF16)
+                grad_gate[lines, here] = (
+                    back * up * sigmoid * (1.0 + gate * (1.0 - sigmoid))
+                ).astype(BF16)
+                grad_up[lines, here] = (back * swish).astype(BF16)
+
+            def lines_of(step):
+                return pl.ds(pl.multiple_of(mp_of(step) * rows, rows), rows)
+
+            add_to(
+                work, r.others_two, k,
+                lambda step: dot_nt(grad_gate[lines_of(step), here], wide[:, gate_cols])
+                + dot_nt(grad_up[lines_of(step), here], wide[:, up_cols]),
+            )
+            add_to(
+                work_out, r.others_out, k,
+                lambda step: dot_nt(hidden[lines_of(step), here], wide[:, down_cols]),
+            )
+            if k + 2 < chunks:
+                chunk_loads.append(load_chunk(k + 2))
+
+        def mlp_block(n):
+            k = mlp_order[n][0]
+            here = slice(k * hidden_width, (k + 1) * hidden_width)
+            at = mlp.items[n][0]
+            lines = pl.ds(pl.multiple_of(at * 4 * quarter, 32), 4 * quarter)
+            slot = mlp.slot_for(n)
+            for value, cols in (
+                (jnp.dot(branch_t[lines, :], grad_gate[:, here], preferred_element_type=F32),
+                 gate_cols),
+                (jnp.dot(branch_t[lines, :], grad_up[:, here], preferred_element_type=F32),
+                 up_cols),
+                (jnp.dot(normed_t[lines, :], hidden[:, here], preferred_element_type=F32),
+                 down_cols),
+            ):
+                for i in range(4):
+                    slot[i // 2, i % 2, :, cols] = value[
+                        i * quarter : (i + 1) * quarter
+                    ].astype(BF16)
+            mlp.items[n][3].start()
+
+        made = [0]
+
+        def make_blocks(stop):
+            while made[0] < stop:
+                mlp_block(made[0])
+                made[0] += 1
+                if made[0] >= 2:
+                    mlp.cross()
+
+        for k in range(chunks):
+            feed_forward(k)
+            if k == 0:
+                wait(block_loads)
+                make_blocks(depth)
+                mlp.cross()
+            else:
+                mlp.onward()
+        for step in range(1, parts):
+            give_x[step - 1] = r.others_two[step - 1].astype(BF16)
+            give_out[step - 1] = r.others_out[step - 1].astype(BF16)
+        for copy in to_two:
+            copy.start()
+        residual_load = load(r.residual_in, residual)
+        attn_loads = [load(r.weights_in, weights), load(r.out_w_in, out_w)]
+        total_blocks = len(mlp_order)
+
+        def more_blocks(stop):
+            while made[0] < min(stop, total_blocks):
+                mlp_block(made[0])
+                made[0] += 1
+                if made[0] - mlp.crossed == 2 or made[0] == total_blocks:
+                    mlp.cross()
+                if made[0] % 3 == 0:
+                    mlp.onward()
+
+        more_blocks(3 * depth)
+        wait([residual_load])
+        own_cot = r.cot.at[part]
+    else:
+        greet(depth, parts)
+        for copy in to_two:
+            copy.start()
+        mlp.begin()
+        first_loads = [
+            load(r.own_two_in, work), load(r.residual_in, residual),
+            load(r.cot_in, r.cot),
+        ]
+        late_loads = [
+            load(r[name + "_in"], r[name])
+            for name in ("out_w", "query_t", "key_t", "value_t", "weights", "normed_t",
+                         "attended", "tokens")
+        ] + [load(r.own_out_in, work_out)]
+        attn_loads = []
+        for n in range(min(8, len(mlp_order))):
+            mlp.cross()
+        wait(first_loads)
+        own_cot = r.cot
+    items = len(mlp_order)
+    mlp.settle()
     for copy in to_two:
         copy.wait_recv()
 
@@ -550,28 +840,25 @@
         total = work[here, :]
         for step in range(parts - 1):
             total = total + in_x[step, here, :].astype(F32)
-        back, terms = norm_back(residual[here, :], gain_two[...], total)
+        back, terms = norm_back(residual[here, :], r.gain_two[...], total)
         held[8:16] += fold(terms)
-        result = cot[here, :].astype(F32) + back
+        result = own_cot[here, :].astype(F32) + back
         work[here, :] = result
         branch[part, here, :] = result.astype(BF16)
 
     tiles(rows, TILE, second)
     for copy in to_branch + to_out:
         copy.start()
-    for n in range(early, items):
-        mlp.cross(n)
-    mlp.onward(0)
-    mlp.onward(1)
-    mlp.onward(2)
-    for copy in to_branch:
-        copy.wait()
-    for copy in loads[3:7]:
-        copy.wait()
-
+    if inside:
+        more_blocks(total_blocks)
+        attn_loads.append(load(r.normed_t_in, normed_t))
+    while mlp.crossed < items:
+        mlp.cross()
     block = 256 if q_width % 256 == 0 else q_width
-    for p in range(parts):
-        across = slice(p * rows, (p + 1) * rows)
+
+    def take_rows(step):
+        p = mp_of(step)
+        across = pl.ds(pl.multiple_of(p * rows, rows), rows)
         for first in range(0, q_width, block):
             piece = jnp.dot(
                 branch[p], out_w[:, first : first + block], preferred_element_type=F32
@@ -585,7 +872,21 @@
 
         lax.fori_loop(0, width // 128, turn, 0)
 
+    wait(late_loads + attn_loads)
+    mlp.onward()
+    take_rows(0)
+    mlp.onward()
+    mlp.settle()
+    for copy in to_branch:
+        copy.wait()
+    for step in range(1, parts):
+        take_rows(step)
+
     q_block = 256 if group <= 1024 else 128
+    key_acc, value_acc = r.key_acc, r.value_acc
+    query_t, key_t, value_t, cosine, sine = (
+        r.query_t, r.key_t, r.value_t, r.cosine, r.sine
+    )
 
     def one_kv_head(j):
         kv_rows = slice(j * HEAD_SIZE, (j + 1) * HEAD_SIZE)
@@ -602,7 +903,7 @@
                 scores = lax.dot_general(
                     query, key, (((0,), (0,)), ((), ())), preferred_element_type=F32
                 )
-                seen = id_col[cols, :] == id_row[:, :stop]
+                seen = r.id_col[cols, :] == r.id_row[:, :stop]
                 at_row = start + lax.broadcasted_iota(jnp.int32, (q_block, stop), 0)
                 at_col = lax.broadcasted_iota(jnp.int32, (q_block, stop), 1)
                 scores = jnp.where(seen & (at_col <= at_row), scores * scale, MASKED)
@@ -617,13 +918,13 @@
                 value_acc[:, :stop] += jnp.dot(
                     grad, probs.astype(BF16), preferred_element_type=F32
                 )
-                dquery = scale * lax.dot_general(
-                    key, dscore, (((1,), (1,)), ((), ())), preferred_element_type=F32
-                )
+                dquery = scale * dot_nt(key, dscore)
                 lead, tail = dquery[:half], dquery[half:]
                 cos, sin = cosine[:, cols], sine[:, cols]
                 grad_t[first : first + half, cols] = (lead * cos + tail * sin).astype(BF16)
-                grad_t[first + half : first + HEAD_SIZE, cols] = (tail * cos - lead * sin).astype(BF16)
+                grad_t[first + half : first + HEAD_SIZE, cols] = (
+                    tail * cos - lead * sin
+                ).astype(BF16)
         lead, tail = key_acc[:half] * scale, key_acc[half:] * scale
         cos, sin = cosine[...], sine[...]
         first = q_width + j * HEAD_SIZE
@@ -632,15 +933,12 @@
         first = q_width + kv_width + j * HEAD_SIZE
         grad_t[first : first + HEAD_SIZE, :] = value_acc[...].astype(BF16)
 
-    done = 3
-    if done < items:
-        mlp.onward(done)
-        done += 1
+    if not inside:
+        mlp.onward()
     for j in range(kv_heads):
         one_kv_head(j)
-        if done < items:
-            mlp.onward(done)
-            done += 1
+        if not inside or j % 4 != 2:
+            mlp.onward()
 
     def turn_back(i, carry):
         here = pl.ds(pl.multiple_of(i * 128, 128), 128)
@@ -650,64 +948,57 @@
         return carry
 
     lax.fori_loop(0, all_width // 128, turn_back, 0)
-    for copy in loads[7:]:
-        copy.wait()
+    for copy in to_two:
+        copy.wait_send()
 
     def incoming(step, here):
-        return lax.dot_general(
-            branch[mp_of(step), :, :all_width], weights[here, :], (((1,), (1,)), ((), ())),
-            preferred_element_type=F32,
-        )
+        return dot_nt(branch[mp_of(step), :, :all_width], weights[here, :])
 
     for step in range(1, parts):
         for first in range(0, width, 512):
-            give_one[step - 1, :, first : first + 512] = incoming(
+            give_x[step - 1, :, first : first + 512] = incoming(
                 step, slice(first, first + 512)
             ).astype(BF16)
     for copy in to_one:
         copy.start()
-
-    depth_rows = 4 * attn_out.shape[0]
-    quarter = attn_out.shape[0]
-
-    def weight_block(n):
-        at, k, slot = attn.items[n][:3]
-        lines = pl.ds(pl.multiple_of(at * depth_rows, 32), depth_rows)
-        if n >= SLOTS:
-            attn.items[n - SLOTS][4].wait_send()
+    mlp.onward()
+
+    def attn_block(n):
+        k = attn_order[n][0]
+        lines = pl.ds(pl.multiple_of(attn.items[n][0] * 4 * quarter, 32), 4 * quarter)
+        slot = attn.slot_for(n)
 
         def put(value, first):
             for i in range(4):
-                attn.ring[0][slot, i // 2, i % 2, :, first : first + value.shape[1]] = value[
+                slot[i // 2, i % 2, :, first : first + value.shape[1]] = value[
                     i * quarter : (i + 1) * quarter
                 ].astype(BF16)
 
-        step = 512 if all_width % 512 == 0 else all_width
-        for first in range(0, all_width, step):
-            put(
-                lax.dot_general(
-                    normed_t[lines, :], grad_t[first : first + step, :],
-                    (((1,), (1,)), ((), ())), preferred_element_type=F32,
-                ),
-                first,
-            )
-        put(jnp.dot(branch_t[lines, :], attended[...], preferred_element_type=F32), all_width)
-        attn.items[n][4].start()
-
-    for n in range(depth):
-        weight_block(n)
+        if k == 0:
+            wide = 512 if all_width % 512 == 0 else all_width
+            for first in range(0, all_width, wide):
+                put(dot_nt(normed_t[lines, :], grad_t[first : first + wide, :]), first)
+        else:
+            put(jnp.dot(branch_t[lines, :], attended[...], preferred_element_type=F32), 0)
+        attn.items[n][3].start()
+
+    for n in range(len(attn_order)):
+        attn_block(n)
         if n >= 1:
-            attn.cross(n - 1)
-        if done < items:
-            mlp.onward(done)
-            done += 1
-    attn.cross(depth - 1)
+            attn.cross()
+        if n % 2 == 1 and not (inside and n < 2):
+            mlp.onward()
+    attn.cross()
 
     for copy in to_out:
         copy.wait_recv()
+    if inside:
+        for copy in to_out:
+            copy.wait_send()
+    out_tile, stored = r.out_tile, r.stored
     tile = out_tile.shape[1]
     for first in range(0, rows, tile):
-        fetch = pltpu.make_async_copy(in_out.at[:, pl.ds(first, tile)], out_tile, stored.at[0])
+        fetch = pltpu.make_async_copy(r.in_out.at[:, pl.ds(first, tile)], out_tile, stored.at[0])
         fetch.start()
         fetch.wait()
         for line in range(first, first + tile, 16):
@@ -716,13 +1007,12 @@
             for step in range(parts - 1):
                 total = total + out_tile[step, line - first : line - first + 16, :].astype(F32)
             low[here, :] = (residual[here, :] + total).astype(BF16)
-    put_out = pltpu.make_async_copy(low, block_out, stored.at[1])
+    put_out = pltpu.make_async_copy(low, r.block_out, stored.at[1])
     put_out.start()
     for first in range(0, width, 512):
         work_out[:, first : first + 512] = incoming(0, slice(first, first + 512))
-    if done < items:
-        mlp.onward(done)
-        done += 1
+    mlp.onward()
+    mlp.settle()
     put_out.wait()
 
     for copy in to_one:
@@ -732,85 +1022,144 @@
         total = work_out[here, :]
         for step in range(parts - 1):
             total = total + in_x[step, here, :].astype(F32)
-        back, terms = norm_back(tokens[here, :].astype(F32), gain_one[...], total)
+        back, terms = norm_back(r.tokens[here, :].astype(F32), r.gain_one[...], total)
         held[0:8] += fold(terms)
         low[here, :] = (work[here, :] + back).astype(BF16)
 
     tiles(rows, TILE, first_norm)
-    put_tokens = pltpu.make_async_copy(low, grad_tokens, stored.at[2])
+    put_tokens = pltpu.make_async_copy(low, r.grad_tokens, stored.at[2])
     put_tokens.start()
     total_gains.begin()
-    while done < items:
-        mlp.onward(done)
-        done += 1
+    while mlp.passed < items:
+        mlp.onward()
         total_gains.advance()
+    mlp.settle()
     while total_gains.number < 3:
         total_gains.advance()
-    attn.onward(0)
-    mlp.end()
-    for n in range(1, depth):
-        attn.onward(n)
+    attn.onward()
+    for k in range(count):
+        mlp.finish(k)
+        attn.onward()
+    while attn.passed < len(attn_order):
+        attn.onward()
     total_gains.advance()
-    gains[...] = held[64:80]
-    attn.end()
+    r.gains[...] = held[64:80]
+    for k in range(2):
+        attn.finish(k)
     put_tokens.wait()
-    for copy in to_two + to_out + to_one:
+    for copy in to_one + ([] if inside else to_out):
         copy.wait_send()
     mlp.drain()
-    attn.drain(crossed=max(depth - SLOTS, 0))
+    attn.drain()
+    ring.drain()
+    if attn_ring is not ring:
+        attn_ring.drain()
     total_gains.drain()
 
 
-def backward(grads, own_two, give_two, own_out, give_out, residual, cot, tokens, gain_one,
-             gain_two, weights, out_w, normed_t, query_t, key_t, value_t, attended, ids,
-             cosine, sine):
+def mlp_and_attn_widths(r, inside, chunks, out_width, all_width):
+    if inside:
+        widths = [r.mlp_w_in.shape[1] // chunks] * chunks
+    else:
+        widths = [r["grad%d" % k].shape[4] for k in range(3)]
+    return widths, [all_width, out_width]
+
+
+def backward(mlp_args, chunks, residual, cot, tokens, gain_one, gain_two, weights, out_w, normed_t,
+             query_t, key_t, value_t, attended, ids, cosine, sine):
     depth, parts = lax.axis_size("dp") // 4, lax.axis_size("mp")
     rows, width = residual.shape
     group = rows * parts
-    wholes = [grad.reshape(depth, 2, 2, grad.shape[0] // (4 * depth), -1) for grad in grads]
+    quarter = width // (4 * depth)
     heads, kv_heads = query_t.shape[0] // HEAD_SIZE, key_t.shape[0] // HEAD_SIZE
-    attn_block = (width // (4 * depth), weights.shape[1] + out_w.shape[1])
+    inside = chunks > 0
+    small = dict(
+        gain_one=gain_one, gain_two=gain_two, id_col=ids[0], id_row=ids[1],
+        cosine=cosine, sine=sine,
+    )
+    large = dict(
+        residual_in=residual, cot_in=cot, tokens_in=tokens, weights_in=weights,
+        out_w_in=out_w, normed_t_in=normed_t, query_t_in=query_t, key_t_in=key_t,
+        value_t_in=value_t, attended_in=attended,
+    )
+    large.update(mlp_args)
+    shapes = Named(large)
+    mlp_widths, attn_widths = mlp_and_attn_widths(
+        shapes, inside, chunks, attended.shape[1], weights.shape[1]
+    )
+    count = len(mlp_widths)
+    struct = jax.ShapeDtypeStruct
+    outs = {"mlp_out%d" % k: struct((quarter, w), F32) for k, w in enumerate(mlp_widths)}
+    outs.update({"attn_out%d" % k: struct((quarter, w), F32) for k, w in enumerate(attn_widths)})
+    rows_out = struct((rows, width), BF16)
+    outs.update(
+        block_out=rows_out, grad_tokens=rows_out, in_out=struct((parts - 1, rows, width), BF16)
+    )
+    for kind, widths in (("mlp", mlp_widths), ("attn", attn_widths)):
+        landing = Sums.landing_shapes(depth, widths, quarter)
+        for k in range(len(widths)):
+            outs["%s_y%d" % (kind, k)] = landing[k]
+            outs["%s_z%d" % (kind, k)] = landing[len(widths) + k]
+    gains_out = dict(gains=struct((16, width), F32))
+
+    def like(array):
+        return pltpu.VMEM(array.shape, array.dtype)
+
+    rows_f32, rows_low = pltpu.VMEM((rows, width), F32), pltpu.VMEM((rows, width), BF16)
+    x_low = pltpu.VMEM((parts - 1, rows, width), BF16)
     stops = depth + parts
-    loaded = (own_two, own_out, residual, cot, tokens, weights, out_w, normed_t, query_t, key_t,
-              value_t, attended)
-    outs = pl.pallas_call(
-        functools.partial(backward_kernel, depth, parts, heads, kv_heads),
-        out_shape=[jax.ShapeDtypeStruct(whole.shape[3:], F32) for whole in wholes]
-        + [
-            jax.ShapeDtypeStruct(attn_block, F32),
-            jax.ShapeDtypeStruct((rows, width), BF16),
-            jax.ShapeDtypeStruct((rows, width), BF16),
-            jax.ShapeDtypeStruct((16, width), F32),
-            jax.ShapeDtypeStruct((parts - 1, rows, width), BF16),
-        ],
-        in_specs=[ANY_SPEC] * 10 + [VMEM_SPEC] * 2 + [ANY_SPEC] * 7 + [VMEM_SPEC] * 4,
-        out_specs=[VMEM_SPEC] * 4 + [ANY_SPEC] * 2 + [VMEM_SPEC, ANY_SPEC],
-        scratch_shapes=[pltpu.VMEM(array.shape, array.dtype) for array in loaded]
-        + [
-            pltpu.VMEM((parts - 1, rows, width), BF16),
-            pltpu.VMEM((parts - 1, 64, width), BF16),
-            pltpu.VMEM((parts, rows, width), BF16),
-            pltpu.VMEM((width, group), BF16),
-            pltpu.VMEM((weights.shape[1], group), BF16),
-            pltpu.VMEM((parts - 1, rows, width), BF16),
-            pltpu.VMEM((HEAD_SIZE, group), F32),
-            pltpu.VMEM((HEAD_SIZE, group), F32),
-            pltpu.VMEM((rows, width), BF16),
-            pltpu.VMEM((80, width), F32),
-            pltpu.VMEM((16 * stops, width), F32),
-            DMA((len(loaded),)),
-            DMA((3,)),
-        ]
-        + [DMA((parts - 1,))] * 8 + [DMA((stops,))] * 2
-        + Sums.scratch(depth, [whole.shape[3:] for whole in wholes], False)
-        + Sums.scratch(depth, [attn_block], True),
+    scratch = dict(
+        work=rows_f32, work_out=rows_f32, cot=like(cot), tokens=rows_low,
+        normed_t=like(normed_t), query_t=like(query_t), key_t=like(key_t),
+        value_t=like(value_t), attended=like(attended), in_x=x_low, give_x=x_low,
+        out_tile=pltpu.VMEM((parts - 1, 64, width), BF16),
+        branch=pltpu.VMEM((parts, rows, width), BF16),
+        branch_t=pltpu.VMEM((width, group), BF16),
+        grad_t=pltpu.VMEM((weights.shape[1], group), BF16),
+        key_acc=pltpu.VMEM((HEAD_SIZE, group), F32),
+        value_acc=pltpu.VMEM((HEAD_SIZE, group), F32),
+        held=pltpu.VMEM((80, width), F32), around=pltpu.VMEM((16 * stops, width), F32),
+        loaded=DMA((20 + chunks,)), stored=DMA((3,)), g_sent=DMA((stops,)), g_got=DMA((stops,)),
+    )
+    for name in ("two", "out", "branch", "one"):
+        scratch[name + "_sent"] = scratch[name + "_got"] = DMA((parts - 1,))
+    if inside:
+        hidden = pltpu.VMEM((group, chunks * mlp_widths[0] // 3), BF16)
+        others = pltpu.VMEM((parts - 1, rows, width), F32)
+        scratch.update(
+            wide=pltpu.VMEM((2, width, mlp_widths[0]), BF16),
+            hidden=hidden, grad_gate=hidden, grad_up=hidden,
+            others_two=others, others_out=others, give_out_low=x_low,
+            ring=pltpu.VMEM((3, 2, 2, quarter, mlp_widths[0]), BF16),
+        )
+    else:
+        scratch.update(
+            residual=rows_f32, weights=like(weights), out_w=like(out_w),
+            ring=pltpu.VMEM((6, 2, quarter, mlp_widths[0]), BF16),
+            attn_ring=pltpu.VMEM((3, 2, 2, quarter, max(attn_widths)), BF16),
+        )
+    scratch.update(low=rows_low)
+    for kind, widths in (("mlp", mlp_widths), ("attn", attn_widths)):
+        for k, shape in enumerate(Sums.held_shapes(depth, widths, quarter)):
+            scratch["%s_held%d" % (kind, k)] = shape
+    names = list(large) + list(small) + list(outs) + list(gains_out) + list(scratch)
+    kernel = functools.partial(
+        backward_kernel, depth, parts, heads, kv_heads, chunks, names
+    )
+    results = pl.pallas_call(
+        kernel,
+        out_shape=list(outs.values()) + list(gains_out.values()),
+        in_specs=[ANY_SPEC] * len(large) + [VMEM_SPEC] * len(small),
+        out_specs=[ANY_SPEC] * len(outs) + [VMEM_SPEC],
+        scratch_shapes=list(scratch.values())
+        + Sums.tiles(depth, mlp_widths, quarter)
+        + Sums.tiles(depth, attn_widths, quarter),
         compiler_params=pltpu.CompilerParams(
             collective_id=1, has_side_effects=True, vmem_limit_bytes=63 * 2**20
         ),
         name="backward",
-    )(*wholes, own_two, give_two, own_out, give_out, residual, cot, tokens, gain_one, gain_two,
-      weights, out_w, normed_t, query_t, key_t, value_t, attended, *ids, cosine, sine)
-    return outs[:7]
+    )(*large.values(), *small.values())
+    return Named(zip(list(outs) + list(gains_out), results))
 
 
 def own_and_give(whole, parts):
@@ -849,7 +1198,17 @@
     width = tokens.shape[1]
     inputs = tokens.astype(F32)
     gain_one, gain_two = norm_attn.astype(F32), norm_mlp.astype(F32)
-    mlp_shard = jnp.concatenate([w_gate, w_up, w_down.T], axis=1)
+    chunks = hidden_width // 512 if group <= 512 and hidden_width % 512 == 0 else 0
+    turned = w_down.T
+    unit = hidden_width // max(chunks, 1)
+    mlp_shard = jnp.concatenate(
+        [
+            part[:, k * unit : (k + 1) * unit]
+            for k in range(max(chunks, 1))
+            for part in (w_gate, w_up, turned)
+        ],
+        axis=1,
+    )
     attn_w, out_wt, normed_one, grad_rows = gather_attn(
         (jnp.concatenate([w_query, key_weight, value_weight], axis=1), w_out.T),
         (rms_parts(inputs)[1] * gain_one).astype(BF16),
@@ -861,7 +1220,6 @@
     normed_one, grad_rows = normed_one.reshape(group, width), grad_rows.reshape(group, width)
     cuts = (q_width, q_width + kv_width)
     query_w, key_w, value_w = jnp.split(attn_w, cuts, axis=1)
-    gate_w, up_w, down_wt = jnp.split(mlp_w, 3, axis=1)
 
     segment, position = layout(seq_lengths[0], group)
     cosine, sine = rotation(position)
@@ -891,28 +1249,47 @@
     residual = inputs + mp_sum_rows(mul_t(attended, out_wt), parts)
     normed_two = mp_gather((rms_parts(residual)[1] * gain_two).astype(BF16), parts)
 
-    gate_act, up_act = mul(normed_two, gate_w), mul(normed_two, up_w)
-    sigmoid_g = jax.nn.sigmoid(gate_act)
-    swish = gate_act * sigmoid_g
-    hidden = (swish * up_act).astype(BF16)
-    branch = mul_t(hidden, down_wt)
-    grad_hidden = mul(grad_rows, down_wt)
-    grad_gate = (grad_hidden * up_act * sigmoid_g * (1.0 + gate_act * (1.0 - sigmoid_g))).astype(
-        BF16
-    )
-    grad_up = (grad_hidden * swish).astype(BF16)
-    grads_mlp = (
-        outer_sum(normed_two, grad_gate).astype(BF16),
-        outer_sum(normed_two, grad_up).astype(BF16),
-        outer_sum(grad_rows, hidden).astype(BF16),
-    )
+    if chunks:
+        mlp_args = dict(
+            mlp_w_in=mlp_w,
+            normed_two_in=normed_two.reshape(parts, rows, width),
+            normed_two_t_in=normed_two.T,
+            cot_t_in=grad_rows.T,
+        )
+    else:
+        gate_w, up_w, down_wt = jnp.split(mlp_w, 3, axis=1)
+        gate_act, up_act = mul(normed_two, gate_w), mul(normed_two, up_w)
+        sigmoid_g = jax.nn.sigmoid(gate_act)
+        swish = gate_act * sigmoid_g
+        hidden = (swish * up_act).astype(BF16)
+        grad_hidden = mul(grad_rows, down_wt)
+        grad_gate = (
+            grad_hidden * up_act * sigmoid_g * (1.0 + gate_act * (1.0 - sigmoid_g))
+        ).astype(BF16)
+        grad_up = (grad_hidden * swish).astype(BF16)
+        grads = (
+            outer_sum(normed_two, grad_gate).astype(BF16),
+            outer_sum(normed_two, grad_up).astype(BF16),
+            outer_sum(grad_rows, hidden).astype(BF16),
+        )
+        depth = lax.axis_size("dp") // 4
+        mlp_args = {
+            "grad%d" % k: grad.reshape(depth, 2, 2, width // (4 * depth), -1)
+            for k, grad in enumerate(grads)
+        }
+        own_two, give_two = own_and_give(
+            mul_t(grad_gate, gate_w) + mul_t(grad_up, up_w), parts
+        )
+        own_out, give_out = own_and_give(mul_t(hidden, down_wt), parts)
+        mlp_args.update(
+            own_two_in=own_two, give_two=give_two, own_out_in=own_out, give_out=give_out
+        )
     ids = jnp.where(segment >= 0, segment, 3 + places)
-    grad_gate_w, grad_up_w, grad_down_w, grad_attn, block_out, grad_tokens, gains = backward(
-        grads_mlp,
-        *own_and_give(mul_t(grad_gate, gate_w) + mul_t(grad_up, up_w), parts),
-        *own_and_give(branch, parts),
+    done = backward(
+        mlp_args,
+        chunks,
         residual,
-        cotangent,
+        grad_rows.reshape(parts, rows, width) if chunks else cotangent,
         tokens,
         gain_one[None, :],
         gain_two[None, :],
@@ -922,13 +1299,21 @@
         query.reshape(group, q_width).T,
         key.reshape(group, kv_width).T,
         value.reshape(group, kv_width).T,
-        attended,
+        jnp.pad(attended, ((0, 0), (0, -q_width % 128))),
         (ids[:, None], ids[None, :]),
         cosine[:, 0, :].T,
         sine[:, 0, :].T,
     )
-    attn_parts = jnp.split(grad_attn, cuts + (q_width + 2 * kv_width,), axis=1)
-    gains = jnp.sum(gains.reshape(2, 8, width), axis=1)
+    block_out, grad_tokens = done.block_out, done.grad_tokens
+    mlp_parts = [done["mlp_out%d" % k] for k in range(chunks or 3)]
+    if chunks:
+        mlp_parts = [
+            jnp.concatenate(part, axis=1)
+            for part in zip(*(jnp.split(piece, 3, axis=1) for piece in mlp_parts))
+        ]
+    grad_gate_w, grad_up_w, grad_down_w = mlp_parts
+    attn_parts = jnp.split(done.attn_out0, cuts, axis=1) + [done.attn_out1[:, :q_width]]
+    gains = jnp.sum(done.gains.reshape(2, 8, width), axis=1)
     return (
         block_out,
         grad_tokens,

time: 421 us -> 357 us (0.85)
  the two profiles are of different devices: /device:TPU:24 before, /device:TPU:10 now
where the time goes in v5:
time: 357 us; the launch traced here: 350 us
  Pallas kernels  220 us (62%)
  waiting for transfers between devices  39.6 us (11%)
  local copies, waits for them, and re-layouts  34.3 us (10%)
  matrix products  19.2 us (5%)
  other arithmetic  18.6 us (5%)
  between operations  16.8 us (5%)
    pallas_call x1, Pallas kernels, backward(): pl.pallas_call(kernel, out_shape=list(outs.values()) + list(gains_out.val...  174 us
    pallas_call x1, Pallas kernels, gather_attn(): pl.pallas_call(functools.partial(gather_kernel, depth, parts, count), out...  46.5 us
    ppermute x2, waiting for transfers between devices, mp_shift(): lax.ppermute(block, 'mp', [(i, (i + step) % parts) for i in range(parts)])  20.4 us
    all_gather x1, waiting for transfers between devices, shards(): mlp_w = lax.all_gather(mlp_shard, 'dp', axis=0, tiled=True)  19.2 us
    dot_general x4, local copies, waits for them, and re-layouts, mul(): return jnp.dot(left, right, preferred_element_type=F32)  7.36 us
  transfers between devices with their start and end apart: 3, of which 3 were waited for; matrix products, arithmetic and copies ran while one was open for 16% of the time, Pallas kernels for 0%

profile of v5, /device:TPU:10, one launch (start us, length us, event | category | flops | bytes accessed | tf_op | source)
XLA Modules:
  0.0 349.8 jit_solution(15757074848387228383)
XLA Ops:
  7.2 0.7 convert_element_type.58
  7.9 1.4 copy.37
  9.9 1.2 copy.38.refs_2_
  11.3 0.7 copy-done.20
  12.0 0.7 pad_maximum_fusion.10.refs_0_
  12.8 46.5 %gather_attn.1 = (bf16[16,96,1536]{2,1,0:T(8,128)(2,1)}, bf16[16,96,768]{2,1,0:T(8,128)(2,1)}, bf16[2,256,1536]{2,1,0:T(8,128)(2,1)}, bf16[2,256,1536]{2,1,0:T(8,128)(2,1)}) custom-call(bf16[96,1536]{1,0:T(8,128)(2,1)} %pad_maximum_fusion.10.refs_0_, bf16[96,768]{1,0:T(8,128)(2,1)} %bitcast.106, bf16[256,1536]{1,0:T(8,128)(2,1)} %copy.38.refs_2_, ...), custom_call_target="tpu_custom_call" | custom-call | tf_op jit(solution)/shard_map/gather_attn/pallas_call | solution.py:306
  59.3 1.4 slice_bitcast_fusion.1
  60.7 1.6 copy.40
  62.4 1.8 slice_bitcast_fusion
  64.2 2.5 copy.42
  69.3 0.7 broadcast_compare_fusion
  69.9 0.7 select_convert_fusion
  71.3 2.7 fusion.38
  74.3 1.4 fusion.39
  76.0 2.2 convolution_convert_fusion
  78.3 5.4 %fusion.33 = (f32[4,2,512]{2,1,0:T(2,128)S(1)}, f32[4,2,512,512]{2,3,1,0:T(8,128)}) fusion(pred[512,512]{0,1:T(8,128)(4,1)S(1)} %fusion.12, bf16[512,4,2,48]{0,3,2,1:T(8,128)(2,1)S(1)} %bitcast.95, bf16[512,4,2,48]{0,3,2,1:T(8,128)(2,1)S(1)} %bitcast.94, bf16[512,4,48]{0,2,1:T(8,128)(2,1)S(1)} %get-tuple-element.50, ...), kind=kOutput, calls=%fused_computation.91 | convolution fusion | flops 413401600 | bytes 9846784 | tf_op jit(solution)/shard_map/sub | solution.py:1241
  83.7 4.4 %fusion.9 = bf16[4,96,2,512]{3,1,2,0:T(8,128)(2,1)S(1)} fusion(bf16[512,4,96,1]{0,2,3,1:T(8,128)(2,1)S(1)} %bitcast.99, f32[4,2,512,512]{2,3,1,0:T(8,128)} %get-tuple-element.73, f32[4,2,512]{2,1,0:T(2,128)S(1)} %get-tuple-element.72), kind=kOutput, calls=%fused_computation.19 | convolution fusion | flops 407240704 | bytes 9584640 | tf_op jit(solution)/shard_map/hgqk,khd->qhgd/dot_general | solution.py:1245
  88.1 3.0 fusion.40
  91.2 1.5 dynamic-slice_convert_fusion
  92.7 0.6 collective-permute-start
  93.3 19.3 %collective-permute-done = bf16[256,1536]{0,1:T(8,128)(2,1)S(1)} collective-permute-done((bf16[256,1536]{0,1:T(8,128)(2,1)S(1)}, bf16[256,1536]{0,1:T(8,128)(2,1)S(1)}, u32[]{:S(2)}, u32[]{:S(2)}) %collective-permute-start) | collective-permute-done | bytes 786464 | tf_op jit(solution)/shard_map/ppermute | solution.py:64
  112.6 1.8 multiply_reduce_fusion
  114.6 1.2 constant_dynamic-update-slice_fusion.1
  117.5 2.6 copy.57
  120.1 2.3 copy.49.refs_9_
  122.4 2.6 copy.59
  125.0 1.3 compare_select_fusion.1.refs_17_
  126.2 1.4 compare_select_fusion.refs_16_
  127.7 1.8 maximum_convert_fusion
  129.5 1.9 pad_maximum_fusion.1
  131.4 1.1 multiply_sine_fusion
  132.5 1.6 copy.48.refs_0_
  134.2 1.1 collective-permute-done.1
  135.2 1.2 constant_dynamic-update-slice_fusion
  136.5 1.9 copy.58
  138.3 19.2 %all-gather.2.cloned.1.call-done.refs_10_ = bf16[1536,6144]{1,0:T(8,128)(2,1)} async-done(((bf16[96,6144]{1,0:T(8,128)(2,1)}), bf16[1536,6144]{1,0:T(8,128)(2,1)}) %all-gather.2.cloned.1.call-update) | async-done | bytes 18874384 | tf_op jit(solution)/shard_map/all_gather | solution.py:1218
  157.5 173.6 %backward.1 = (f32[96,1536]{1,0:T(8,128)}, f32[96,1536]{1,0:T(8,128)}, f32[96,1536]{1,0:T(8,128)}, f32[96,1536]{1,0:T(8,128)}, f32[96,1536]{1,0:T(8,128)}, /*ind...) custom-call(f32[256,1536]{1,0:T(8,128)} %copy.48.refs_0_, ...), custom_call_target="tpu_custom_call" | custom-call | tf_op jit(solution)/shard_map/backward/pallas_call | solution.py:1149
  331.2 1.8 split.57
  332.9 1.8 fusion.31
  334.7 0.9 bitcast_reduce_fusion
  335.7 0.6 slice_reduce_fusion
  336.5 0.9 copy-done.11
  337.4 0.9 maximum_bitcast_fusion
  338.3 0.9 pad_maximum_fusion.3
  339.3 0.9 pad_maximum_fusion.2
  340.2 0.9 copy.76
  341.1 0.9 copy.77
  342.0 0.7 copy.78
  (87 shorter events, 4.6 us)
Async XLA Ops:
  7.2 150.4 %all-gather.2.cloned.1.call-start = ((), (), s32[]{:S(2)}) async-start(), calls=%async_computation | async-start | bytes 20054016 | tf_op jit(solution)/shard_map/all_gather | solution.py:1218
  9.6 1.5 copy-start.16
  9.6 1.5 copy-start.17
  9.6 1.5 copy-start.18
  11.0 0.9 copy-start.20
  11.0 1.0 copy-start.21
  11.0 1.0 copy-start.22
  11.3 48.0 %copy-start.5 = (bf16[96,6144]{1,0:T(8,128)(2,1)}, bf16[96,6144]{1,0:T(8,128)(2,1)S(1)}, u32[]{:S(2)}) copy-start(bf16[96,6144]{1,0:T(8,128)(2,1)S(1)} %slice_dynamic-update-slice_fusion) | copy-start | bytes 3538948
  64.2 2.5 copy-start.25
  69.3 4.8 %copy-start.26 = (f32[48]{0:T(128)}, f32[48]{0:T(128)S(1)}, u32[]{:S(2)}) copy-start(f32[48]{0:T(128)S(1)} %multiply_power_fusion) | copy-start | bytes 580
  71.3 2.9 copy-start.2
  71.3 3.0 copy-start.3
  74.2 4.1 %copy-start.9 = (bf16[512,4,48]{0,2,1:T(8,128)(2,1)}, bf16[512,4,48]{0,2,1:T(8,128)(2,1)S(1)}, u32[]{:S(2)}) copy-start(bf16[512,4,48]{0,2,1:T(8,128)(2,1)S(1)} %get-tuple-element.49) | copy-start | bytes 589828
  74.2 4.1 %copy-start.10 = (bf16[512,4,48]{0,2,1:T(8,128)(2,1)}, bf16[512,4,48]{0,2,1:T(8,128)(2,1)S(1)}, u32[]{:S(2)}) copy-start(bf16[512,4,48]{0,2,1:T(8,128)(2,1)S(1)} %get-tuple-element.50) | copy-start | bytes 589828
  76.0 2.3 copy-start.4
  78.2 5.4 %copy-start.15 = (bf16[512,384]{0,1:T(8,128)(2,1)}, bf16[512,384]{0,1:T(8,128)(2,1)S(1)}, u32[]{:S(2)}) copy-start(bf16[512,384]{0,1:T(8,128)(2,1)S(1)} %convolution_convert_fusion) | copy-start | bytes 1179652
  83.7 4.4 %copy-start.1 = (bf16[16,96,768]{2,1,0:T(8,128)(2,1)S(1)}, bf16[16,96,768]{2,1,0:T(8,128)(2,1)}, u32[]{:S(2)}) copy-start(bf16[16,96,768]{2,1,0:T(8,128)(2,1)} %get-tuple-element.29) | copy-start | bytes 7077892
  88.1 3.0 copy-start.8
  91.2 2.1 copy-start.24
  92.7 19.9 %collective-permute-start = (bf16[256,1536]{0,1:T(8,128)(2,1)S(1)}, bf16[256,1536]{0,1:T(8,128)(2,1)S(1)}, u32[]{:S(2)}, u32[]{:S(2)}) collective-permute-start(bf16[256,1536]{0,1:T(8,128)(2,1)S(1)} %dynamic-slice_convert_fusion), channel_id=1, source_target_pairs={{0,1},{1,0},{2,3},{3,2},{4,5},{5,4},{6,7},{7,6},{8,9},{9,8},{10,11... | collective-permute-start | bytes 2359304 | tf_op jit(solution)/shard_map/ppermute | solution.py:64
  114.6 1.7 copy-start.23
  115.7 19.5 %collective-permute-start.1 = (bf16[256,1536]{0,1:T(8,128)(2,1)}, bf16[256,1536]{0,1:T(8,128)(2,1)}, u32[]{:S(2)}, u32[]{:S(2)}) collective-permute-start(bf16[256,1536]{0,1:T(8,128)(2,1)} %get-tuple-element.44), channel_id=1, source_target_pairs={{0,1},{1,0},{2,3},{3,2},{4,5},{5,4},{6,7},{7,6},{8,9},{9,8},{10,11... | collective-permute-start | bytes 2359304 | tf_op jit(solution)/shard_map/ppermute | solution.py:64
  125.0 6.4 %copy-start.27 = (f32[48]{0:T(128)S(1)}, f32[48]{0:T(128)}, u32[]{:S(2)}) copy-start(f32[48]{0:T(128)} %copy-done.26) | copy-start | bytes 580
  136.4 1.9 copy-start
  331.1 5.1 %copy-start.14 = (f32[96,1536]{1,0:T(8,128)S(1)}, f32[96,1536]{1,0:T(8,128)}, u32[]{:S(2)}) copy-start(f32[96,1536]{1,0:T(8,128)} %get-tuple-element.37) | copy-start | bytes 1769476
  331.1 5.2 %copy-start.13 = (f32[96,1536]{1,0:T(8,128)S(1)}, f32[96,1536]{1,0:T(8,128)}, u32[]{:S(2)}) copy-start(f32[96,1536]{1,0:T(8,128)} %get-tuple-element.38) | copy-start | bytes 1769476
  332.9 3.4 copy-start.12
  336.3 1.1 copy-start.11
  338.3 1.9 copy-start.7
  339.3 1.8 copy-start.6
  340.2 1.8 copy-start.19
Sparse Core Ops, SparseCore 0:
  59.4 98.0 all-gather.1

commit v6 on v5

--- a/solution.py
+++ b/solution.py
@@ -737,6 +737,11 @@
                 ).astype(BF16)
                 grad_up[lines, here] = (back * swish).astype(BF16)
 
+            if k == 0:
+                wait(block_loads)
+                make_blocks(depth)
+                mlp.cross()
+
             def lines_of(step):
                 return pl.ds(pl.multiple_of(mp_of(step) * rows, rows), rows)
 
@@ -783,11 +788,7 @@
 
         for k in range(chunks):
             feed_forward(k)
-            if k == 0:
-                wait(block_loads)
-                make_blocks(depth)
-                mlp.cross()
-            else:
+            if k > 0:
                 mlp.onward()
         for step in range(1, parts):
             give_x[step - 1] = r.others_two[step - 1].astype(BF16)
@@ -873,10 +874,13 @@
         lax.fori_loop(0, width // 128, turn, 0)
 
     wait(late_loads + attn_loads)
-    mlp.onward()
     take_rows(0)
     mlp.onward()
     mlp.settle()
+    finished = 0
+    if inside and mlp.passed > depth:
+        mlp.finish(0)
+        finished = 1
     for copy in to_branch:
         copy.wait()
     for step in range(1, parts):
@@ -1030,22 +1034,23 @@
     put_tokens = pltpu.make_async_copy(low, r.grad_tokens, stored.at[2])
     put_tokens.start()
     total_gains.begin()
+    total_gains.advance()
+    total_gains.advance()
     while mlp.passed < items:
         mlp.onward()
-        total_gains.advance()
     mlp.settle()
-    while total_gains.number < 3:
-        total_gains.advance()
+    for n in range(len(attn_order) - 1):
+        attn.onward()
+        if finished < count:
+            mlp.finish(finished)
+            finished += 1
+        if n == len(attn_order) - 4:
+            total_gains.advance()
+    attn.finish(0)
     attn.onward()
-    for k in range(count):
-        mlp.finish(k)
-        attn.onward()
-    while attn.passed < len(attn_order):
-        attn.onward()
     total_gains.advance()
     r.gains[...] = held[64:80]
-    for k in range(2):
-        attn.finish(k)
+    attn.finish(1)
     put_tokens.wait()
     for copy in to_one + ([] if inside else to_out):
         copy.wait_send()

time: 357 us -> 350 us (0.980)
  Pallas kernels: 220 us -> 216 us
    pallas_call x1, Pallas kernels: 174 us -> 170 us  [backward(): pl.pallas_call(kernel, out_shape=list(outs.values()) + list(gains_out.val...]
where the time goes in v6:
time: 350 us; the launch traced here: 346 us
  Pallas kernels  216 us (62%)
  waiting for transfers between devices  39.5 us (11%)
  local copies, waits for them, and re-layouts  34.5 us (10%)
  matrix products  19.2 us (5%)
  other arithmetic  18.6 us (5%)
  between operations  16.8 us (5%)
    pallas_call x1, Pallas kernels, backward(): pl.pallas_call(kernel, out_shape=list(outs.values()) + list(gains_out.val...  170 us
    pallas_call x1, Pallas kernels, gather_attn(): pl.pallas_call(functools.partial(gather_kernel, depth, parts, count), out...  46.5 us
    ppermute x2, waiting for transfers between devices, mp_shift(): lax.ppermute(block, 'mp', [(i, (i + step) % parts) for i in range(parts)])  20.4 us
    all_gather x1, waiting for transfers between devices, shards(): mlp_w = lax.all_gather(mlp_shard, 'dp', axis=0, tiled=True)  19 us
    dot_general x4, local copies, waits for them, and re-layouts, mul(): return jnp.dot(left, right, preferred_element_type=F32)  7.37 us
  transfers between devices with their start and end apart: 3, of which 3 were waited for; matrix products, arithmetic and copies ran while one was open for 16% of the time, Pallas kernels for 0%

profile of v6, /device:TPU:10, one launch (start us, length us, event | category | flops | bytes accessed | tf_op | source)
XLA Modules:
  0.0 346.0 jit_solution(17656040587943011287)
XLA Ops:
  7.2 0.7 convert_element_type.58
  7.9 1.4 copy.37
  9.9 1.2 copy.38.refs_2_
  11.3 0.7 copy-done.20
  12.0 0.7 pad_maximum_fusion.10.refs_0_
  12.8 46.5 %gather_attn.1 = (bf16[16,96,1536]{2,1,0:T(8,128)(2,1)}, bf16[16,96,768]{2,1,0:T(8,128)(2,1)}, bf16[2,256,1536]{2,1,0:T(8,128)(2,1)}, bf16[2,256,1536]{2,1,0:T(8,128)(2,1)}) custom-call(bf16[96,1536]{1,0:T(8,128)(2,1)} %pad_maximum_fusion.10.refs_0_, bf16[96,768]{1,0:T(8,128)(2,1)} %bitcast.106, bf16[256,1536]{1,0:T(8,128)(2,1)} %copy.38.refs_2_, ...), custom_call_target="tpu_custom_call" | custom-call | tf_op jit(solution)/shard_map/gather_attn/pallas_call | solution.py:306
  59.3 1.4 slice_bitcast_fusion.1
  60.7 1.6 copy.40
  62.4 1.8 slice_bitcast_fusion
  64.2 2.5 copy.42
  69.3 0.7 broadcast_compare_fusion
  69.9 0.7 select_convert_fusion
  71.3 2.8 fusion.38
  74.3 1.4 fusion.39
  76.0 2.2 convolution_convert_fusion
  78.3 5.4 %fusion.33 = (f32[4,2,512]{2,1,0:T(2,128)S(1)}, f32[4,2,512,512]{2,3,1,0:T(8,128)}) fusion(pred[512,512]{0,1:T(8,128)(4,1)S(1)} %fusion.12, bf16[512,4,2,48]{0,3,2,1:T(8,128)(2,1)S(1)} %bitcast.95, bf16[512,4,2,48]{0,3,2,1:T(8,128)(2,1)S(1)} %bitcast.94, bf16[512,4,48]{0,2,1:T(8,128)(2,1)S(1)} %get-tuple-element.50, ...), kind=kOutput, calls=%fused_computation.91 | convolution fusion | flops 413401600 | bytes 9846784 | tf_op jit(solution)/shard_map/sub | solution.py:1246
  83.7 4.4 %fusion.9 = bf16[4,96,2,512]{3,1,2,0:T(8,128)(2,1)S(1)} fusion(bf16[512,4,96,1]{0,2,3,1:T(8,128)(2,1)S(1)} %bitcast.99, f32[4,2,512,512]{2,3,1,0:T(8,128)} %get-tuple-element.73, f32[4,2,512]{2,1,0:T(2,128)S(1)} %get-tuple-element.72), kind=kOutput, calls=%fused_computation.19 | convolution fusion | flops 407240704 | bytes 9584640 | tf_op jit(solution)/shard_map/hgqk,khd->qhgd/dot_general | solution.py:1250
  88.1 3.0 fusion.40
  91.2 1.5 dynamic-slice_convert_fusion
  93.3 19.3 %collective-permute-done = bf16[256,1536]{0,1:T(8,128)(2,1)S(1)} collective-permute-done((bf16[256,1536]{0,1:T(8,128)(2,1)S(1)}, bf16[256,1536]{0,1:T(8,128)(2,1)S(1)}, u32[]{:S(2)}, u32[]{:S(2)}) %collective-permute-start) | collective-permute-done | bytes 786464 | tf_op jit(solution)/shard_map/ppermute | solution.py:64
  112.6 1.8 multiply_reduce_fusion
  114.6 1.2 constant_dynamic-update-slice_fusion.1
  116.3 0.6 broadcast_in_dim.87.refs_14_
  117.5 2.6 copy.57
  120.1 2.3 copy.49.refs_9_
  122.4 2.6 copy.59
  125.0 1.3 compare_select_fusion.1.refs_17_
  126.2 1.4 compare_select_fusion.refs_16_
  127.7 1.8 maximum_convert_fusion
  129.5 1.9 pad_maximum_fusion.1
  131.4 1.1 multiply_sine_fusion
  132.5 1.6 copy.48.refs_0_
  134.2 1.1 collective-permute-done.1
  135.2 1.2 constant_dynamic-update-slice_fusion
  136.5 2.0 copy.58
  138.5 19.0 %all-gather.2.cloned.1.call-done.refs_10_ = bf16[1536,6144]{1,0:T(8,128)(2,1)} async-done(((bf16[96,6144]{1,0:T(8,128)(2,1)}), bf16[1536,6144]{1,0:T(8,128)(2,1)}) %all-gather.2.cloned.1.call-update) | async-done | bytes 18874384 | tf_op jit(solution)/shard_map/all_gather | solution.py:1223
  157.5 169.8 %backward.1 = (f32[96,1536]{1,0:T(8,128)}, f32[96,1536]{1,0:T(8,128)}, f32[96,1536]{1,0:T(8,128)}, f32[96,1536]{1,0:T(8,128)}, f32[96,1536]{1,0:T(8,128)}, /*ind...) custom-call(f32[256,1536]{1,0:T(8,128)} %copy.48.refs_0_, ...), custom_call_target="tpu_custom_call" | custom-call | tf_op jit(solution)/shard_map/backward/pallas_call | solution.py:1154
  327.4 1.8 split.57
  329.2 1.8 fusion.31
  330.9 0.9 bitcast_reduce_fusion
  331.9 0.6 slice_reduce_fusion
  332.7 0.9 copy-done.11
  333.6 0.9 maximum_bitcast_fusion
  334.5 0.9 pad_maximum_fusion.3
  335.5 0.9 pad_maximum_fusion.2
  336.4 0.9 copy.76
  337.3 0.9 copy.77
  338.2 0.7 copy.78
  (87 shorter events, 4.6 us)
Async XLA Ops:
  7.2 150.4 %all-gather.2.cloned.1.call-start = ((), (), s32[]{:S(2)}) async-start(), calls=%async_computation | async-start | bytes 20054016 | tf_op jit(solution)/shard_map/all_gather | solution.py:1223
  9.6 1.5 copy-start.16
  9.6 1.5 copy-start.17
  9.6 1.5 copy-start.18
  11.0 0.9 copy-start.20
  11.0 1.0 copy-start.21
  11.0 1.0 copy-start.22
  11.3 48.0 %copy-start.5 = (bf16[96,6144]{1,0:T(8,128)(2,1)}, bf16[96,6144]{1,0:T(8,128)(2,1)S(1)}, u32[]{:S(2)}) copy-start(bf16[96,6144]{1,0:T(8,128)(2,1)S(1)} %slice_dynamic-update-slice_fusion) | copy-start | bytes 3538948
  64.2 2.5 copy-start.25
  69.3 4.8 %copy-start.26 = (f32[48]{0:T(128)}, f32[48]{0:T(128)S(1)}, u32[]{:S(2)}) copy-start(f32[48]{0:T(128)S(1)} %multiply_power_fusion) | copy-start | bytes 580
  71.3 2.9 copy-start.2
  71.3 3.0 copy-start.3
  74.2 4.1 %copy-start.9 = (bf16[512,4,48]{0,2,1:T(8,128)(2,1)}, bf16[512,4,48]{0,2,1:T(8,128)(2,1)S(1)}, u32[]{:S(2)}) copy-start(bf16[512,4,48]{0,2,1:T(8,128)(2,1)S(1)} %get-tuple-element.49) | copy-start | bytes 589828
  74.2 4.1 %copy-start.10 = (bf16[512,4,48]{0,2,1:T(8,128)(2,1)}, bf16[512,4,48]{0,2,1:T(8,128)(2,1)S(1)}, u32[]{:S(2)}) copy-start(bf16[512,4,48]{0,2,1:T(8,128)(2,1)S(1)} %get-tuple-element.50) | copy-start | bytes 589828
  76.0 2.3 copy-start.4
  78.3 5.4 %copy-start.15 = (bf16[512,384]{0,1:T(8,128)(2,1)}, bf16[512,384]{0,1:T(8,128)(2,1)S(1)}, u32[]{:S(2)}) copy-start(bf16[512,384]{0,1:T(8,128)(2,1)S(1)} %convolution_convert_fusion) | copy-start | bytes 1179652
  83.7 4.4 %copy-start.1 = (bf16[16,96,768]{2,1,0:T(8,128)(2,1)S(1)}, bf16[16,96,768]{2,1,0:T(8,128)(2,1)}, u32[]{:S(2)}) copy-start(bf16[16,96,768]{2,1,0:T(8,128)(2,1)} %get-tuple-element.29) | copy-start | bytes 7077892
  88.1 3.0 copy-start.8
  91.2 2.1 copy-start.24
  92.7 19.9 %collective-permute-start = (bf16[256,1536]{0,1:T(8,128)(2,1)S(1)}, bf16[256,1536]{0,1:T(8,128)(2,1)S(1)}, u32[]{:S(2)}, u32[]{:S(2)}) collective-permute-start(bf16[256,1536]{0,1:T(8,128)(2,1)S(1)} %dynamic-slice_convert_fusion), channel_id=1, source_target_pairs={{0,1},{1,0},{2,3},{3,2},{4,5},{5,4},{6,7},{7,6},{8,9},{9,8},{10,11... | collective-permute-start | bytes 2359304 | tf_op jit(solution)/shard_map/ppermute | solution.py:64
  114.6 1.7 copy-start.23
  115.7 19.5 %collective-permute-start.1 = (bf16[256,1536]{0,1:T(8,128)(2,1)}, bf16[256,1536]{0,1:T(8,128)(2,1)}, u32[]{:S(2)}, u32[]{:S(2)}) collective-permute-start(bf16[256,1536]{0,1:T(8,128)(2,1)} %get-tuple-element.44), channel_id=1, source_target_pairs={{0,1},{1,0},{2,3},{3,2},{4,5},{5,4},{6,7},{7,6},{8,9},{9,8},{10,11... | collective-permute-start | bytes 2359304 | tf_op jit(solution)/shard_map/ppermute | solution.py:64
  125.0 6.4 %copy-start.27 = (f32[48]{0:T(128)S(1)}, f32[48]{0:T(128)}, u32[]{:S(2)}) copy-start(f32[48]{0:T(128)} %copy-done.26) | copy-start | bytes 580
  136.5 2.1 copy-start
  327.3 5.1 %copy-start.14 = (f32[96,1536]{1,0:T(8,128)S(1)}, f32[96,1536]{1,0:T(8,128)}, u32[]{:S(2)}) copy-start(f32[96,1536]{1,0:T(8,128)} %get-tuple-element.37) | copy-start | bytes 1769476
  327.4 5.2 %copy-start.13 = (f32[96,1536]{1,0:T(8,128)S(1)}, f32[96,1536]{1,0:T(8,128)}, u32[]{:S(2)}) copy-start(f32[96,1536]{1,0:T(8,128)} %get-tuple-element.38) | copy-start | bytes 1769476
  329.2 3.4 copy-start.12
  332.5 1.1 copy-start.11
  334.5 1.9 copy-start.7
  335.5 1.8 copy-start.6
  336.4 1.8 copy-start.19
Sparse Core Ops, SparseCore 0:
  59.4 98.0 all-gather.1

commit v7 on v6

--- a/solution.py
+++ b/solution.py
@@ -871,7 +871,7 @@
             branch_t[here, across] = branch[p, :, here].astype(F32).T.astype(BF16)
             return carry
 
-        lax.fori_loop(0, width // 128, turn, 0)
+        lax.fori_loop(0, width // 128, turn, 0, unroll=3)
 
     wait(late_loads + attn_loads)
     take_rows(0)
@@ -951,7 +951,7 @@
             branch[p, :, here] = piece[p * rows : (p + 1) * rows]
         return carry
 
-    lax.fori_loop(0, all_width // 128, turn_back, 0)
+    lax.fori_loop(0, all_width // 128, turn_back, 0, unroll=3)
     for copy in to_two:
         copy.wait_send()
 

time: 350 us -> 351 us (level)
  no operation moved by 1% of the time
where the time goes in v7:
time: 351 us; the launch traced here: 345 us
  Pallas kernels  215 us (61%)
  waiting for transfers between devices  39.5 us (11%)
  local copies, waits for them, and re-layouts  34.5 us (10%)
  matrix products  19.2 us (5%)
  other arithmetic  18.6 us (5%)
  between operations  16.8 us (5%)
    pallas_call x1, Pallas kernels, backward(): pl.pallas_call(kernel, out_shape=list(outs.values()) + list(gains_out.val...  169 us
    pallas_call x1, Pallas kernels, gather_attn(): pl.pallas_call(functools.partial(gather_kernel, depth, parts, count), out...  46.5 us
    ppermute x2, waiting for transfers between devices, mp_shift(): lax.ppermute(block, 'mp', [(i, (i + step) % parts) for i in range(parts)])  20.4 us
    all_gather x1, waiting for transfers between devices, shards(): mlp_w = lax.all_gather(mlp_shard, 'dp', axis=0, tiled=True)  19 us
    dot_general x4, local copies, waits for them, and re-layouts, mul(): return jnp.dot(left, right, preferred_element_type=F32)  7.37 us
  transfers between devices with their start and end apart: 3, of which 3 were waited for; matrix products, arithmetic and copies ran while one was open for 16% of the time, Pallas kernels for 0%

profile of v7, /device:TPU:10, one launch (start us, length us, event | category | flops | bytes accessed | tf_op | source)
XLA Modules:
  0.0 344.8 jit_solution(12239854604308437199)
XLA Ops:
  7.2 0.7 convert_element_type.58
  7.9 1.4 copy.37
  9.9 1.2 copy.38.refs_2_
  11.3 0.7 copy-done.20
  12.0 0.7 pad_maximum_fusion.10.refs_0_
  12.8 46.5 %gather_attn.1 = (bf16[16,96,1536]{2,1,0:T(8,128)(2,1)}, bf16[16,96,768]{2,1,0:T(8,128)(2,1)}, bf16[2,256,1536]{2,1,0:T(8,128)(2,1)}, bf16[2,256,1536]{2,1,0:T(8,128)(2,1)}) custom-call(bf16[96,1536]{1,0:T(8,128)(2,1)} %pad_maximum_fusion.10.refs_0_, bf16[96,768]{1,0:T(8,128)(2,1)} %bitcast.106, bf16[256,1536]{1,0:T(8,128)(2,1)} %copy.38.refs_2_, ...), custom_call_target="tpu_custom_call" | custom-call | tf_op jit(solution)/shard_map/gather_attn/pallas_call | solution.py:306
  59.3 1.4 slice_bitcast_fusion.1
  60.7 1.6 copy.40
  62.4 1.8 slice_bitcast_fusion
  64.2 2.5 copy.42
  69.3 0.7 broadcast_compare_fusion
  69.9 0.7 select_convert_fusion
  71.3 2.8 fusion.38
  74.3 1.4 fusion.39
  76.0 2.2 convolution_convert_fusion
  78.3 5.4 %fusion.33 = (f32[4,2,512]{2,1,0:T(2,128)S(1)}, f32[4,2,512,512]{2,3,1,0:T(8,128)}) fusion(pred[512,512]{0,1:T(8,128)(4,1)S(1)} %fusion.12, bf16[512,4,2,48]{0,3,2,1:T(8,128)(2,1)S(1)} %bitcast.95, bf16[512,4,2,48]{0,3,2,1:T(8,128)(2,1)S(1)} %bitcast.94, bf16[512,4,48]{0,2,1:T(8,128)(2,1)S(1)} %get-tuple-element.50, ...), kind=kOutput, calls=%fused_computation.91 | convolution fusion | flops 413401600 | bytes 9846784 | tf_op jit(solution)/shard_map/sub | solution.py:1246
  83.7 4.4 %fusion.9 = bf16[4,96,2,512]{3,1,2,0:T(8,128)(2,1)S(1)} fusion(bf16[512,4,96,1]{0,2,3,1:T(8,128)(2,1)S(1)} %bitcast.99, f32[4,2,512,512]{2,3,1,0:T(8,128)} %get-tuple-element.73, f32[4,2,512]{2,1,0:T(2,128)S(1)} %get-tuple-element.72), kind=kOutput, calls=%fused_computation.19 | convolution fusion | flops 407240704 | bytes 9584640 | tf_op jit(solution)/shard_map/hgqk,khd->qhgd/dot_general | solution.py:1250
  88.1 3.0 fusion.40
  91.2 1.5 dynamic-slice_convert_fusion
  93.3 19.3 %collective-permute-done = bf16[256,1536]{0,1:T(8,128)(2,1)S(1)} collective-permute-done((bf16[256,1536]{0,1:T(8,128)(2,1)S(1)}, bf16[256,1536]{0,1:T(8,128)(2,1)S(1)}, u32[]{:S(2)}, u32[]{:S(2)}) %collective-permute-start) | collective-permute-done | bytes 786464 | tf_op jit(solution)/shard_map/ppermute | solution.py:64
  112.6 1.8 multiply_reduce_fusion
  114.6 1.2 constant_dynamic-update-slice_fusion.1
  116.3 0.6 broadcast_in_dim.87.refs_14_
  117.5 2.6 copy.57
  120.1 2.3 copy.49.refs_9_
  122.4 2.6 copy.59
  125.0 1.3 compare_select_fusion.1.refs_17_
  126.2 1.4 compare_select_fusion.refs_16_
  127.7 1.8 maximum_convert_fusion
  129.5 1.9 pad_maximum_fusion.1
  131.4 1.1 multiply_sine_fusion
  132.5 1.6 copy.48.refs_0_
  134.2 1.1 collective-permute-done.1
  135.2 1.2 constant_dynamic-update-slice_fusion
  136.5 2.0 copy.58
  138.5 19.0 %all-gather.2.cloned.1.call-done.refs_10_ = bf16[1536,6144]{1,0:T(8,128)(2,1)} async-done(((bf16[96,6144]{1,0:T(8,128)(2,1)}), bf16[1536,6144]{1,0:T(8,128)(2,1)}) %all-gather.2.cloned.1.call-update) | async-done | bytes 18874384 | tf_op jit(solution)/shard_map/all_gather | solution.py:1223
  157.5 168.6 %backward.1 = (f32[96,1536]{1,0:T(8,128)}, f32[96,1536]{1,0:T(8,128)}, f32[96,1536]{1,0:T(8,128)}, f32[96,1536]{1,0:T(8,128)}, f32[96,1536]{1,0:T(8,128)}, /*ind...) custom-call(f32[256,1536]{1,0:T(8,128)} %copy.48.refs_0_, ...), custom_call_target="tpu_custom_call" | custom-call | tf_op jit(solution)/shard_map/backward/pallas_call | solution.py:1154
  326.1 1.8 split.57
  327.9 1.8 fusion.31
  329.7 0.9 bitcast_reduce_fusion
  330.6 0.6 slice_reduce_fusion
  331.4 0.9 copy-done.11
  332.4 0.9 maximum_bitcast_fusion
  333.3 0.9 pad_maximum_fusion.3
  334.2 0.9 pad_maximum_fusion.2
  335.2 0.9 copy.76
  336.1 0.9 copy.77
  336.9 0.7 copy.78
  (87 shorter events, 4.6 us)
Async XLA Ops:
  7.2 150.4 %all-gather.2.cloned.1.call-start = ((), (), s32[]{:S(2)}) async-start(), calls=%async_computation | async-start | bytes 20054016 | tf_op jit(solution)/shard_map/all_gather | solution.py:1223
  9.6 1.5 copy-start.16
  9.6 1.5 copy-start.17
  9.6 1.5 copy-start.18
  11.0 0.9 copy-start.20
  11.0 1.0 copy-start.21
  11.0 1.0 copy-start.22
  11.3 48.0 %copy-start.5 = (bf16[96,6144]{1,0:T(8,128)(2,1)}, bf16[96,6144]{1,0:T(8,128)(2,1)S(1)}, u32[]{:S(2)}) copy-start(bf16[96,6144]{1,0:T(8,128)(2,1)S(1)} %slice_dynamic-update-slice_fusion) | copy-start | bytes 3538948
  64.2 2.5 copy-start.25
  69.3 4.8 %copy-start.26 = (f32[48]{0:T(128)}, f32[48]{0:T(128)S(1)}, u32[]{:S(2)}) copy-start(f32[48]{0:T(128)S(1)} %multiply_power_fusion) | copy-start | bytes 580
  71.3 2.9 copy-start.2
  71.3 3.0 copy-start.3
  74.2 4.1 %copy-start.9 = (bf16[512,4,48]{0,2,1:T(8,128)(2,1)}, bf16[512,4,48]{0,2,1:T(8,128)(2,1)S(1)}, u32[]{:S(2)}) copy-start(bf16[512,4,48]{0,2,1:T(8,128)(2,1)S(1)} %get-tuple-element.49) | copy-start | bytes 589828
  74.2 4.1 %copy-start.10 = (bf16[512,4,48]{0,2,1:T(8,128)(2,1)}, bf16[512,4,48]{0,2,1:T(8,128)(2,1)S(1)}, u32[]{:S(2)}) copy-start(bf16[512,4,48]{0,2,1:T(8,128)(2,1)S(1)} %get-tuple-element.50) | copy-start | bytes 589828
  76.0 2.3 copy-start.4
  78.3 5.4 %copy-start.15 = (bf16[512,384]{0,1:T(8,128)(2,1)}, bf16[512,384]{0,1:T(8,128)(2,1)S(1)}, u32[]{:S(2)}) copy-start(bf16[512,384]{0,1:T(8,128)(2,1)S(1)} %convolution_convert_fusion) | copy-start | bytes 1179652
  83.7 4.4 %copy-start.1 = (bf16[16,96,768]{2,1,0:T(8,128)(2,1)S(1)}, bf16[16,96,768]{2,1,0:T(8,128)(2,1)}, u32[]{:S(2)}) copy-start(bf16[16,96,768]{2,1,0:T(8,128)(2,1)} %get-tuple-element.29) | copy-start | bytes 7077892
  88.1 3.0 copy-start.8
  91.2 2.1 copy-start.24
  92.7 19.9 %collective-permute-start = (bf16[256,1536]{0,1:T(8,128)(2,1)S(1)}, bf16[256,1536]{0,1:T(8,128)(2,1)S(1)}, u32[]{:S(2)}, u32[]{:S(2)}) collective-permute-start(bf16[256,1536]{0,1:T(8,128)(2,1)S(1)} %dynamic-slice_convert_fusion), channel_id=1, source_target_pairs={{0,1},{1,0},{2,3},{3,2},{4,5},{5,4},{6,7},{7,6},{8,9},{9,8},{10,11... | collective-permute-start | bytes 2359304 | tf_op jit(solution)/shard_map/ppermute | solution.py:64
  114.6 1.7 copy-start.23
  115.7 19.5 %collective-permute-start.1 = (bf16[256,1536]{0,1:T(8,128)(2,1)}, bf16[256,1536]{0,1:T(8,128)(2,1)}, u32[]{:S(2)}, u32[]{:S(2)}) collective-permute-start(bf16[256,1536]{0,1:T(8,128)(2,1)} %get-tuple-element.44), channel_id=1, source_target_pairs={{0,1},{1,0},{2,3},{3,2},{4,5},{5,4},{6,7},{7,6},{8,9},{9,8},{10,11... | collective-permute-start | bytes 2359304 | tf_op jit(solution)/shard_map/ppermute | solution.py:64
  125.0 6.4 %copy-start.27 = (f32[48]{0:T(128)S(1)}, f32[48]{0:T(128)}, u32[]{:S(2)}) copy-start(f32[48]{0:T(128)} %copy-done.26) | copy-start | bytes 580
  136.5 2.1 copy-start
  326.1 5.1 %copy-start.14 = (f32[96,1536]{1,0:T(8,128)S(1)}, f32[96,1536]{1,0:T(8,128)}, u32[]{:S(2)}) copy-start(f32[96,1536]{1,0:T(8,128)} %get-tuple-element.37) | copy-start | bytes 1769476
  326.1 5.2 %copy-start.13 = (f32[96,1536]{1,0:T(8,128)S(1)}, f32[96,1536]{1,0:T(8,128)}, u32[]{:S(2)}) copy-start(f32[96,1536]{1,0:T(8,128)} %get-tuple-element.38) | copy-start | bytes 1769476
  327.9 3.4 copy-start.12
  331.3 1.1 copy-start.11
  333.3 1.9 copy-start.7
  334.2 1.8 copy-start.6
  335.2 1.8 copy-start.19
Sparse Core Ops, SparseCore 0:
  59.4 98.0 all-gather.1
